TPU v7x, 32 devices: a whole 2x2x4 slice. The times are simulated.
32 devices in a mesh: dp: 8 (over y, x, core), mp: 4 (over z).
Axes of the slice: x: 2, y: 2, z: 4, core: 2. Of those that a mesh axis runs over, the one named last changes fastest.
Arguments:
- weight: bfloat16 [128, 128, 128], P(('dp', 'mp')), may hold values from -6 to 6
- moment_one: float32 [128, 128, 128], P(('dp', 'mp')), may hold values from -1.8 to 1.8
- moment_two: float32 [128, 128, 128], P(('dp', 'mp')), may hold values from 0.01 to 1
- block_row: int32 [128], P(('dp', 'mp')), may hold values from 0 to 63, as said below
- block_col: int32 [128], P(('dp', 'mp')), may hold values from 0 to 55
- dest_slot: int32 [128], P(('dp', 'mp')), may hold values from -1 to 31, as said below
- tokens: bfloat16 [1024, 8192], P('dp', 'mp'), may hold values from -6 to 6
- upstream: bfloat16 [1024, 28672], P('dp', 'mp'), may hold values from -6 to 6
Outputs:
- new_weight: bfloat16 [128, 128, 128], P(('dp', 'mp'))
- new_first: float32 [128, 128, 128], P(('dp', 'mp'))
- new_second: float32 [128, 128, 128], P(('dp', 'mp'))
- hidden_out: bfloat16 [1024, 28672], P('dp', 'mp')
- input_grad: bfloat16 [1024, 8192], P('dp', 'mp')
Inputs may be any that keep to these rules, and one draw needn't show every extreme that they name: Within one tensor slice the pairs (block_row, block_col) are distinct. `dest_slot`: within one tensor slice the non-negative values are distinct; slots d * 4 to (d + 1) * 4 - 1 belong to dp index d, and a block held by dp index d goes to d - 1, d or d + 1; at most 2 blocks of one device go to each neighbour, and in every slice some pair of neighbours exchanges exactly 2 blocks each way.
All inputs are finite; a program needn't handle non-finite values.
Results may differ from a plain program's by a relative error of at most 0.0055.
Values may be sent and summed in bfloat16 or wider, within the bound.
No kernel may reach another device: no remote copies, remote signals or barrier semaphores. Data moves between devices by JAX's collectives and lax.ppermute only.
A program may use at most 128 MiB of HBM per device.

v0:
```python
import math

import jax
import jax.numpy as jnp
from jax import lax
from jax.sharding import PartitionSpec as P

D = 8192


learn_rate = 0.02
beta_first = 0.9
beta_second = 0.95
epsilon = 1e-08
highest = lax.Precision.HIGHEST


def with_halo(shard, sides, width):
    for axis, dim in sides:
        size, length = (lax.axis_size(axis), shard.shape[dim])
        up = [(i, (i + 1) % size) for i in range(size - 1)]
        down = [(j, i) for i, j in up]
        last = lax.slice_in_dim(shard, length - width, length, axis=dim)
        initial = lax.slice_in_dim(shard, 0, width, axis=dim)
        before = lax.ppermute(last, axis, up)
        after = lax.ppermute(initial, axis, down)
        shard = jnp.concatenate([before, shard, after], axis=dim)
    return shard


def adam_update(gradient, weights, first_moment, second_moment):
    first_new = beta_first * first_moment + (1.0 - beta_first) * gradient
    second_new = beta_second * second_moment + (1.0 - beta_second) * gradient * gradient
    stepped = weights - learn_rate * first_new / (jnp.sqrt(second_new) + epsilon)
    return (stepped, first_new, second_new)


def moving_plan(dest_part, goal, kept_dev, half_slots):
    chosen = (dest_part >= 0) & (dest_part // kept_dev == goal)
    order_rank = jnp.cumsum(chosen.astype(jnp.int32)) - 1
    select = (
        (order_rank[None, :] == jnp.arange(half_slots, dtype=jnp.int32)[:, None]) & chosen[None, :]
    ).astype(jnp.float32)
    offsets = (
        jnp.dot(select, (dest_part % kept_dev + 1).astype(jnp.float32), precision=highest) - 1.0
    )
    return (select, offsets)


def relocate(stacked, all_dest):
    kept_dev = stacked.shape[0]
    half_slots = kept_dev // 2
    own_index = lax.axis_index("dp")
    last_index = lax.axis_size("dp") - 1
    own_dest = lax.dynamic_slice_in_dim(all_dest, own_index * kept_dev, kept_dev)
    left_dest = lax.dynamic_slice_in_dim(
        all_dest, jnp.maximum(own_index - 1, 0) * kept_dev, kept_dev
    )
    right_dest = lax.dynamic_slice_in_dim(
        all_dest, jnp.minimum(own_index + 1, last_index) * kept_dev, kept_dev
    )
    send_left, unused_left = moving_plan(own_dest, own_index - 1, kept_dev, half_slots)
    send_right, unused_right = moving_plan(own_dest, own_index + 1, kept_dev, half_slots)
    outgoing = jnp.dot(jnp.concatenate([send_left, send_right], axis=0), stacked, precision=highest)
    padded = with_halo(outgoing.astype(jnp.bfloat16), (("dp", 0),), half_slots).astype(
        outgoing.dtype
    )
    from_left = padded[:half_slots]
    from_right = padded[3 * half_slots :]
    unused_one, left_offsets = moving_plan(left_dest, own_index, kept_dev, half_slots)
    unused_two, right_offsets = moving_plan(right_dest, own_index, kept_dev, half_slots)
    left_offsets = jnp.where(own_index > 0, left_offsets, -1.0)
    right_offsets = jnp.where(own_index < last_index, right_offsets, -1.0)
    staying = (own_dest >= 0) & (own_dest // kept_dev == own_index)
    stay_offsets = jnp.where(staying, own_dest % kept_dev, -1).astype(jnp.float32)
    places = jnp.concatenate([stay_offsets, left_offsets, right_offsets])
    slot_hot = (jnp.arange(kept_dev, dtype=jnp.float32)[:, None] == places[None, :]).astype(
        jnp.float32
    )
    return jnp.dot(
        slot_hot, jnp.concatenate([stacked, from_left, from_right], axis=0), precision=highest
    )


def body(weight, moment_one, moment_two, block_row, block_col, dest_slot, tokens, upstream):
    kept_dev = weight.shape[0]
    block_side = weight.shape[1]
    flat_size = block_side * block_side
    grad_scale = 1.0 / math.sqrt(D)
    features = lax.all_gather(tokens, "mp", axis=1, tiled=True)
    all_weight, all_rows, all_cols, all_dest = (
        lax.all_gather(weight, "dp", axis=0, tiled=True),
        lax.all_gather(block_row, "dp", axis=0, tiled=True),
        lax.all_gather(block_col, "dp", axis=0, tiled=True),
        lax.all_gather(dest_slot, "dp", axis=0, tiled=True),
    )
    token_rows = features.shape[0]
    block_rows = features.shape[1] // block_side
    block_cols = upstream.shape[1] // block_side
    x_blocks = jnp.take(features.reshape(token_rows, block_rows, block_side), all_rows, axis=1)
    d_blocks = jnp.take(upstream.reshape(token_rows, block_cols, block_side), all_cols, axis=1)
    forward = jnp.einsum("tbk,bkj->btj", x_blocks, all_weight, preferred_element_type=jnp.float32)
    col_sums = jax.ops.segment_sum(forward, all_cols, num_segments=block_cols)
    hidden_out = (
        (jnp.swapaxes(col_sums, 0, 1) * grad_scale)
        .reshape(token_rows, block_cols * block_side)
        .astype(jnp.bfloat16)
    )
    backward = jnp.einsum("tbj,bkj->btk", d_blocks, all_weight, preferred_element_type=jnp.float32)
    row_sums = jax.ops.segment_sum(backward, all_rows, num_segments=block_rows)
    partial_in = (jnp.swapaxes(row_sums, 0, 1) * grad_scale).reshape(
        token_rows, block_rows * block_side
    )
    input_grad = lax.psum_scatter(partial_in, "mp", scatter_dimension=1, tiled=True).astype(
        jnp.bfloat16
    )
    old_weight = weight.reshape(kept_dev, flat_size).astype(jnp.float32)
    old_first = moment_one.reshape(kept_dev, flat_size)
    old_second = moment_two.reshape(kept_dev, flat_size)
    gradient = (
        lax.psum_scatter(
            (
                jnp.einsum("tbk,tbj->bkj", x_blocks, d_blocks, preferred_element_type=jnp.float32)
                * grad_scale
            ).astype(jnp.bfloat16),
            "dp",
            scatter_dimension=0,
            tiled=True,
        )
        .astype(jnp.float32)
        .reshape(kept_dev, flat_size)
    )
    held_weight, held_first, held_second = adam_update(gradient, old_weight, old_first, old_second)
    moved = relocate(jnp.concatenate([held_weight, held_first, held_second], axis=1), all_dest)
    stepped = moved[:, :flat_size]
    first_new = moved[:, flat_size : 2 * flat_size]
    second_new = moved[:, 2 * flat_size :]
    new_weight = stepped.astype(jnp.bfloat16).reshape(kept_dev, block_side, block_side)
    new_first = first_new.reshape(kept_dev, block_side, block_side)
    new_second = second_new.reshape(kept_dev, block_side, block_side)
    return (new_weight, new_first, new_second, hidden_out, input_grad)


def solution(mesh):
    return jax.shard_map(
        body,
        mesh=mesh,
        in_specs=(
            P(("dp", "mp"), None, None),
            P(("dp", "mp"), None, None),
            P(("dp", "mp"), None, None),
            P(("dp", "mp")),
            P(("dp", "mp")),
            P(("dp", "mp")),
            P("dp", "mp"),
            P("dp", "mp"),
        ),
        out_specs=(
            P(("dp", "mp"), None, None),
            P(("dp", "mp"), None, None),
            P(("dp", "mp"), None, None),
            P("dp", "mp"),
            P("dp", "mp"),
        ),
        check_vma=False,
    )
```

profile of v0, /device:TPU:0, one launch (start us, length us, event | category | flops | bytes accessed | tf_op | source)
XLA Modules:
  0.0 210.0 jit_solution(1334297399728107847)
XLA Ops:
  7.2 0.0 all-gather.3.cloned.1.call-start
  7.2 2.0 copy.24
  9.3 0.0 all-gather.3.cloned.1.call-update
  9.3 0.0 all-gather.5.cloned.1.call-start
  9.3 0.7 all-gather.5.cloned.1.call-update
  10.0 0.0 reduce-scatter.3.cloned.1.call-start
  10.1 1.2 dynamic-slice
  12.0 0.9 dynamic-update-slice.2
  12.9 0.8 dynamic-update-slice.1
  13.7 0.8 dynamic-update-slice
  14.5 9.5 %all-reduce.3 = (s32[32]{0:T(128)S(1)}, s32[32]{0:T(128)S(1)}, s32[32]{0:T(128)S(1)}) all-reduce(s32[32]{0:T(128)S(1)} %dynamic-update-slice.1, s32[32]{0:T(128)S(1)} %dynamic-update-slice.2, s32[32]{0:T(128)S(1)} %dynamic-update-slice), channel_id=1, replica_groups=mesh['dp'=8,'mp'=4] {'dp'}, use_global_device_ids=true, to_apply=%add.1 | all-reduce | flops 96 | bytes 768
  24.0 3.3 %copy.26 = bf16[128,7168]{0,1:T(8,128)(2,1)S(1)} copy(bf16[128,7168]{1,0:T(8,128)(2,1)} %param.15) | data formatting | bytes 3670016 | tf_op args[7]
  27.3 2.9 %copy.27 = bf16[128,56,128]{2,0,1:T(8,128)(2,1)} copy(bf16[128,56,128]{0,2,1:T(8,128)(2,1)S(1)} %bitcast.95) | data formatting | bytes 3670016 | tf_op jit(solution)/shard_map/reshape | solution.py:101
  30.2 0.1 fusion.48
  30.3 0.2 reduce-window.35
  30.5 0.2 reduce-window.34
  30.7 0.1 convert_bitcast_fusion.5
  30.8 0.2 reduce-window.33
  30.9 0.2 reduce-window.32
  31.1 2.3 %gather_fusion.1 = bf16[32,128,128]{2,1,0:T(8,128)(2,1)S(1)} fusion(bf16[128,56,128]{2,0,1:T(8,128)(2,1)} %copy.27, s32[1024]{0:T(1024)S(1)} %pad_clamp_fusion), kind=kCustom, calls=%fused_computation.1 | custom fusion | bytes 2097280 | tf_op jit(solution)/shard_map/jit(_take)/gather | solution.py:101
  33.4 0.2 fusion.14
  33.6 0.2 fusion.12
  33.9 24.9 %all-gather.3.cloned.1.call-done = bf16[128,8192]{0,1:T(8,128)(2,1)} async-done(((bf16[128,2048]{0,1:T(8,128)(2,1)}), bf16[128,8192]{0,1:T(8,128)(2,1)}) %all-gather.3.cloned.1.call-update) | async-done | bytes 2097168 | tf_op jit(solution)/shard_map/all_gather | solution.py:90
  58.8 3.2 %copy.25 = bf16[128,64,128]{2,0,1:T(8,128)(2,1)S(1)} copy(bf16[128,64,128]{0,2,1:T(8,128)(2,1)} %bitcast.96) | data formatting | bytes 4194304 | tf_op jit(solution)/shard_map/reshape | solution.py:100
  62.0 1.7 gather_fusion
  63.7 2.9 %multiply_convert_fusion.1 = bf16[32,128,128]{2,1,0:T(8,128)(2,1)} fusion(bf16[32,128,128]{2,1,0:T(8,128)(2,1)} %gather_fusion, pred[32]{0:T(512)(128)(4,1)S(1)} %get-tuple-element.43, bf16[32,128,128]{2,1,0:T(8,128)(2,1)S(1)} %gather_fusion.1, pred[32]{0:T(512)(128)(4,1)S(1)} %get-tuple-element.42), kind=kOutput, calls=%fused_computation.7 | convolution fusion | flops 136314880 | bytes 3145792 | tf_op jit(solution)/shard_map/tbk,tbj->bkj/dot_general | solution.py:123
  66.6 0.0 reduce-scatter.3.cloned.1.call-update
  66.6 0.0 reduce-scatter.5.cloned.1.call-start
  66.6 0.1 pad_maximum_fusion.2
  66.8 0.8 multiply_bitcast_fusion.1
  67.6 15.3 %all-gather.5.cloned.1.call-done = bf16[32,128,128]{2,1,0:T(8,128)(2,1)} async-done(((bf16[4,128,128]{2,1,0:T(8,128)(2,1)}), bf16[32,128,128]{2,1,0:T(8,128)(2,1)}) %all-gather.5.cloned.1.call-update) | async-done | bytes 1048592 | tf_op jit(solution)/shard_map/all_gather | solution.py:92
  82.9 2.1 %fusion.15 = f32[32,128,128]{2,1,0:T(8,128)S(1)} fusion(bf16[32,128,128]{2,1,0:T(8,128)(2,1)} %all-gather.5.cloned.1.call-done, bf16[32,128,128]{2,1,0:T(8,128)(2,1)S(1)} %gather_fusion.1, pred[32]{0:T(512)(128)(4,1)S(1)} %get-tuple-element.42), kind=kOutput, calls=%fused_computation.25 | convolution fusion | flops 134742016 | bytes 4194336 | tf_op jit(solution)/shard_map/tbj,bkj->btk/dot_general | solution.py:109
  85.1 2.5 %broadcast_in_dim.60 = f32[64,128,128]{2,1,0:T(8,128)} broadcast(f32[]{:T(128)} %constant.134.clone.1), dimensions={} | broadcast | bytes 4194308 | tf_op jit(solution)/shard_map/broadcast_in_dim | solution.py:110
  87.6 6.2 %scatter_fusion.1 = f32[64,128,128]{2,1,0:T(8,128)} fusion(f32[64,128,128]{2,1,0:T(8,128)} %broadcast_in_dim.60, s32[32]{0:T(128)S(1)} %get-tuple-element.15, f32[32,128,128]{2,1,0:T(8,128)S(1)} %fusion.15), kind=kCustom, calls=%fused_computation.3 | custom fusion | flops 524288 | bytes 6291584 | tf_op jit(solution)/shard_map/scatter-add | solution.py:110
  93.8 5.1 %multiply_bitcast_fusion = f32[128,64,128]{2,0,1:T(8,128)} fusion(f32[64,128,128]{2,1,0:T(8,128)} %scatter_fusion.1), kind=kLoop, calls=%fused_computation.5 | loop fusion | flops 1048576 | bytes 8388608 | tf_op jit(solution)/shard_map/mul | solution.py:111
  98.9 5.6 %copy.30 = f32[128,64,128]{0,2,1:T(8,128)} copy(f32[128,64,128]{2,0,1:T(8,128)} %multiply_bitcast_fusion) | data formatting | bytes 8388608 | tf_op jit(solution)/shard_map/mul | solution.py:111
  104.6 0.0 reduce-scatter.5.cloned.1.call-update
  104.6 1.2 copy-done.1
  105.8 1.8 fusion.18
  107.6 2.3 %broadcast_in_dim.58 = f32[56,128,128]{2,1,0:T(8,128)} broadcast(f32[]{:T(128)} %constant.134.clone.1), dimensions={} | broadcast | bytes 3670020 | tf_op jit(solution)/shard_map/broadcast_in_dim | solution.py:103
  109.9 6.2 %scatter_fusion = f32[56,128,128]{2,1,0:T(8,128)} fusion(f32[56,128,128]{2,1,0:T(8,128)} %broadcast_in_dim.58, s32[32]{0:T(128)S(1)} %get-tuple-element.16, f32[32,128,128]{2,1,0:T(8,128)S(1)} %fusion.18), kind=kCustom, calls=%fused_computation.2 | custom fusion | flops 524288 | bytes 6291584 | tf_op jit(solution)/shard_map/scatter-add | solution.py:103
  116.1 6.1 %reduce-scatter.3.cloned.1.call-done = bf16[4,128,128]{2,1,0:T(8,128)(2,1)} async-done(((bf16[32,128,128]{2,1,0:T(8,128)(2,1)}), bf16[4,128,128]{2,1,0:T(8,128)(2,1)}) %reduce-scatter.3.cloned.1.call-update) | async-done | bytes 131088 | tf_op jit(solution)/shard_map/reduce_scatter | solution.py:121
  122.2 0.9 convert_bitcast_fusion
  123.2 0.8 bitcast_subtract_fusion
  124.0 0.0 copy-start.5
  124.0 0.7 copy-done.5
  124.7 0.9 convolution_convert_fusion
  125.6 1.0 fusion.69
  126.6 1.6 collective-permute-start
  128.2 1.5 collective-permute-start.1
  129.7 1.8 fusion
  131.5 3.3 %copy.29 = bf16[128,56,128]{0,2,1:T(8,128)(2,1)S(1)} copy(bf16[128,56,128]{2,0,1:T(8,128)(2,1)} %fusion) | data formatting | bytes 3670016 | tf_op jit(solution)/shard_map/convert_element_type | solution.py:107
  134.8 0.0 copy-start.6
  134.8 2.9 %copy.31 = bf16[128,7168]{1,0:T(8,128)(2,1)} copy(bf16[128,7168]{0,1:T(8,128)(2,1)S(1)} %bitcast.94) | data formatting | bytes 3670016
  137.7 0.0 collective-permute-done
  137.7 0.0 collective-permute-done.1
  137.7 1.0 maximum_convert_fusion
  138.7 1.3 fusion.1
  140.0 0.7 copy.53
  140.8 0.7 copy.55
  141.5 0.7 copy.54
  142.2 58.9 %reduce-scatter.5.cloned.1.call-done = f32[128,2048]{0,1:T(8,128)} async-done(((f32[128,8192]{0,1:T(8,128)}), f32[128,2048]{0,1:T(8,128)}) %reduce-scatter.5.cloned.1.call-update) | async-done | bytes 1048592 | tf_op jit(solution)/shard_map/reduce_scatter | solution.py:114
  201.1 1.3 convert_element_type.58
  202.4 1.0 copy.32
  (31 shorter events, 0.2 us)
Async XLA Ops:
  7.2 51.6 %all-gather.3.cloned.1.call-start = ((), (), s32[]{:S(2)}) async-start(), calls=%async_computation.2 | async-start | bytes 2621440 | tf_op jit(solution)/shard_map/all_gather | solution.py:90
  9.3 73.7 %all-gather.5.cloned.1.call-start = ((), (), s32[]{:S(2)}) async-start(), calls=%async_computation.4 | async-start | bytes 1179648 | tf_op jit(solution)/shard_map/all_gather | solution.py:92
  10.0 112.2 %reduce-scatter.3.cloned.1.call-start = ((), (), s32[]{:S(2)}) async-start(), calls=%async_computation.3 | async-start | bytes 1179648 | tf_op jit(solution)/shard_map/reduce_scatter | solution.py:121
  63.7 3.0 %copy-start.4 = (bf16[4,128,128]{2,1,0:T(8,128)(2,1)S(1)}, bf16[4,128,128]{2,1,0:T(8,128)(2,1)}, u32[]{:S(2)}) copy-start(bf16[4,128,128]{2,1,0:T(8,128)(2,1)} %param.8) | copy-start | bytes 393220
  63.7 3.1 %copy-start.7 = (f32[4,128,128]{2,1,0:T(8,128)S(1)}, f32[4,128,128]{2,1,0:T(8,128)}, u32[]{:S(2)}) copy-start(f32[4,128,128]{2,1,0:T(8,128)} %param.10) | copy-start | bytes 786436
  63.7 3.1 %copy-start.8 = (f32[4,128,128]{2,1,0:T(8,128)S(1)}, f32[4,128,128]{2,1,0:T(8,128)}, u32[]{:S(2)}) copy-start(f32[4,128,128]{2,1,0:T(8,128)} %param.9) | copy-start | bytes 786436
  66.6 134.5 %reduce-scatter.5.cloned.1.call-start = ((), (), s32[]{:S(2)}) async-start(), calls=%async_computation.5 | async-start | bytes 5242880 | tf_op jit(solution)/shard_map/reduce_scatter | solution.py:114
  104.6 1.2 copy-start.1
  109.9 13.2 %copy-start.2 = (f32[1,4,128,128]{3,2,1,0:T(8,128)S(1)}, f32[1,4,128,128]{3,2,1,0:T(8,128)}, u32[]{:S(2)}) copy-start(f32[1,4,128,128]{3,2,1,0:T(8,128)} %get-tuple-element.44) | copy-start | bytes 786436
  109.9 13.2 %copy-start.3 = (f32[1,4,128,128]{3,2,1,0:T(8,128)S(1)}, f32[1,4,128,128]{3,2,1,0:T(8,128)}, u32[]{:S(2)}) copy-start(f32[1,4,128,128]{3,2,1,0:T(8,128)} %get-tuple-element.45) | copy-start | bytes 786436
  123.2 6.6 %copy-start = (f32[56,128,128]{2,1,0:T(8,128)S(1)}, f32[56,128,128]{2,1,0:T(8,128)}, u32[]{:S(2)}) copy-start(f32[56,128,128]{2,1,0:T(8,128)} %scatter_fusion) | copy-start | bytes 11010052
  124.0 0.7 copy-start.5
  126.6 11.1 %collective-permute-start = (bf16[2,49152]{1,0:T(2,128)(2,1)}, bf16[2,49152]{1,0:T(2,128)(2,1)S(1)}, u32[]{:S(2)}, u32[]{:S(2)}) collective-permute-start(bf16[2,49152]{1,0:T(2,128)(2,1)} %get-tuple-element.36), channel_id=1, source_target_pairs={{0,4},{4,8},{8,12},{12,16},{16,20},{20,24},{24,28},{1,5},{5,9},{9,... | collective-permute-start | bytes 589832 | tf_op jit(solution)/shard_map/ppermute | solution.py:25
  128.2 9.4 %collective-permute-start.1 = (bf16[2,49152]{1,0:T(2,128)(2,1)}, bf16[2,49152]{1,0:T(2,128)(2,1)S(1)}, u32[]{:S(2)}, u32[]{:S(2)}) collective-permute-start(bf16[2,49152]{1,0:T(2,128)(2,1)} %get-tuple-element.37), channel_id=1, source_target_pairs={{4,0},{8,4},{12,8},{16,12},{20,16},{24,20},{28,24},{5,1},{9,5},{13... | collective-permute-start | bytes 589832 | tf_op jit(solution)/shard_map/ppermute | solution.py:26
  134.8 3.9 %copy-start.6 = (f32[4,16384]{1,0:T(4,128)S(1)}, f32[4,16384]{1,0:T(4,128)}, u32[]{:S(2)}) copy-start(f32[4,16384]{1,0:T(4,128)} %copy-done.5) | copy-start | bytes 786436
Sparse Core Ops, SparseCore 0:
  10.1 48.6 all-gather.2
  60.7 22.1 all-gather.4
  86.1 36.0 reduce-scatter.2
  124.4 76.7 reduce-scatter.4
where the time goes:
time: 211 us; the launch traced here: 210 us
  waiting for transfers between devices  106 us (50%)
  local copies, waits for them, and re-layouts  42 us (20%)
  other arithmetic  25.1 us (12%)
  between operations  14.7 us (7%)
  blocking collectives  9.46 us (4%)
  matrix products  9.35 us (4%)
  starting transfers between devices  3.24 us (2%)
    reduce_scatter x1, waiting for transfers between devices, body(): lax.psum_scatter(partial_in, 'mp', scatter_dimension=1, tiled=True)  58.9 us
    all_gather x1, waiting for transfers between devices, body(): features = lax.all_gather(tokens, 'mp', axis=1, tiled=True)  24.9 us
    unnamed x34, local copies, waits for them, and re-layouts  17.1 us
    all_gather x1, waiting for transfers between devices, body(): lax.all_gather(weight, 'dp', axis=0, tiled=True)  15.3 us
    unnamed x1, blocking collectives  9.46 us
    scatter-add x1, other arithmetic, body(): row_sums = jax.ops.segment_sum(backward, all_rows, num_segments=block_rows)  6.22 us
    scatter-add x1, other arithmetic, body(): col_sums = jax.ops.segment_sum(forward, all_cols, num_segments=block_cols)  6.17 us
    reduce_scatter x1, waiting for transfers between devices, body(): lax.psum_scatter((jnp.einsum('tbk,tbj->bkj', x_blocks, d_blocks, preferre...  6.12 us
  transfers between devices with their start and end apart: 6, of which 4 were waited for; matrix products, arithmetic and copies ran while one was open for 33% of the time, Pallas kernels for 0%

commit v1 on v0

v1 whole, which is shorter than its diff:
```python
import functools
import math

import jax
import jax.numpy as jnp
from jax import lax
from jax.experimental import pallas as pl
from jax.experimental.pallas import tpu as pltpu
from jax.sharding import PartitionSpec as P

D = 8192
TILE = 16
VMEM_LIMIT = 48 * 1024 * 1024

learn_rate = 0.02
beta_first = 0.9
beta_second = 0.95
epsilon = 1e-08
grad_scale = 1.0 / math.sqrt(D)

f32 = jnp.float32
bf16 = jnp.bfloat16
VMEM = pl.BlockSpec(memory_space=pltpu.VMEM)
SMEM = pl.BlockSpec(memory_space=pltpu.SMEM)


def params():
    return pltpu.CompilerParams(vmem_limit_bytes=VMEM_LIMIT)


def lanes(ref, index, width):
    return ref[:, pl.ds(pl.multiple_of(index * width, width), width)]


def pack_kernel(row_s, col_s, dest_s, w_ref, one_ref, two_ref, pack_ref, left_ref, right_ref):
    kept, side = w_ref.shape[0], w_ref.shape[1]
    half = kept // 2
    me = lax.axis_index("dp")
    lane = lax.broadcasted_iota(jnp.int32, (TILE, side), 1)
    pitch = side + TILE
    travel = 3 * side
    left_ref[...] = jnp.zeros_like(left_ref)
    right_ref[...] = jnp.zeros_like(right_ref)
    to_left = jnp.int32(0)
    to_right = jnp.int32(0)
    for s in range(kept):
        dest = dest_s[s]
        tile = jnp.where(lane == 0, row_s[s], jnp.where(lane == 1, col_s[s], dest))
        pack_ref[s * pitch : s * pitch + side, :] = w_ref[s]
        pack_ref[s * pitch + side : (s + 1) * pitch, :] = tile.astype(f32).astype(bf16)
        goal = jnp.where(dest >= 0, dest // kept, me)
        for ref, count, going in (
            (left_ref, to_left, goal < me),
            (right_ref, to_right, goal > me),
        ):

            @pl.when(going)
            def _(ref=ref, count=count, s=s):
                base = pl.multiple_of(jnp.minimum(count, half - 1) * travel, TILE)
                ref[pl.ds(base, side), :] = w_ref[s]
                ref[pl.ds(base + side, side), :] = one_ref[s].astype(bf16)
                ref[pl.ds(base + 2 * side, side), :] = two_ref[s].astype(bf16)

        to_left = to_left + (goal < me).astype(jnp.int32)
        to_right = to_right + (goal > me).astype(jnp.int32)


def pack(rows, cols, dests, weight, one, two):
    kept, side, _ = weight.shape
    travel = jax.ShapeDtypeStruct((kept // 2 * 3 * side, side), bf16)
    return pl.pallas_call(
        pack_kernel,
        out_shape=(jax.ShapeDtypeStruct((kept * (side + TILE), side), bf16), travel, travel),
        in_specs=[SMEM, SMEM, SMEM, VMEM, VMEM, VMEM],
        out_specs=(VMEM, VMEM, VMEM),
        compiler_params=params(),
        name="pack_blocks",
    )(rows, cols, dests, weight, one, two)


def backward_kernel(kept, ids, slices, *refs):
    count = len(ids)
    packs = refs[:count]
    up_ref = refs[count]
    shares = refs[count + 1 : count + 1 + slices]
    meta_ref = refs[count + 1 + slices]
    acc, meta_s, sem = refs[count + 2 + slices :]
    side = packs[0].shape[1]
    pitch = side + TILE
    width = shares[0].shape[1]
    for at, ident in enumerate(ids):
        for s in range(kept):
            tile = packs[at][s * pitch + side : (s + 1) * pitch, :].astype(f32)
            row = ident * kept + s
            meta_ref[row : row + 1, :] = tile[0:1, :].astype(jnp.int32)
    copy = pltpu.make_async_copy(meta_ref, meta_s, sem)
    copy.start()
    acc[...] = jnp.zeros_like(acc)
    copy.wait()
    for at, ident in enumerate(ids):
        for s in range(kept):
            row = meta_s[ident * kept + s, 0]
            col = meta_s[ident * kept + s, 1]
            part = lax.dot_general(
                lanes(up_ref, col, side),
                packs[at][s * pitch : s * pitch + side, :],
                (((1,), (1,)), ((), ())),
                preferred_element_type=f32,
            )
            place = pl.ds(pl.multiple_of(row * side, side), side)
            acc[:, place] = acc[:, place] + part
    me = lax.axis_index("mp")
    for k in range(slices):
        share = lanes(acc, lax.rem(me + k, slices), width) * grad_scale
        shares[k][...] = share.astype(shares[k].dtype)


def backward(packs, ids, upstream, kept, slices, features):
    tokens = upstream.shape[0]
    side = packs[0].shape[1]
    blocks = len(ids) * kept
    shares = [
        jax.ShapeDtypeStruct((tokens, features), f32 if k == 0 else bf16) for k in range(slices)
    ]
    outs = pl.pallas_call(
        functools.partial(backward_kernel, kept, ids, slices),
        out_shape=(*shares, jax.ShapeDtypeStruct((blocks, side), jnp.int32)),
        in_specs=[VMEM] * (len(ids) + 1),
        out_specs=(VMEM,) * (slices + 1),
        scratch_shapes=[
            pltpu.VMEM((tokens, slices * features), f32),
            pltpu.SMEM((blocks, side), jnp.int32),
            pltpu.SemaphoreType.DMA,
        ],
        compiler_params=params(),
        cost_estimate=pl.CostEstimate(
            flops=2 * blocks * tokens * side * side,
            bytes_accessed=24 * 1024 * 1024,
            transcendentals=0,
        ),
        name="input_gradient",
    )(*packs, upstream)
    return outs[:slices], outs[slices]


def line_reduce(shares, axis):
    n = len(shares)
    right = left = None
    for step in range(1, n):
        to_right, to_left = shares[n - step], shares[step]
        if right is not None:
            to_right = (to_right.astype(f32) + right.astype(f32)).astype(bf16)
            to_left = (to_left.astype(f32) + left.astype(f32)).astype(bf16)
        right = lax.ppermute(to_right, axis, [(i, i + 1) for i in range(step)])
        left = lax.ppermute(to_left, axis, [(n - 1 - i, n - 2 - i) for i in range(step)])
    if right is None:
        return shares[0].astype(bf16)
    return (shares[0] + right.astype(f32) + left.astype(f32)).astype(bf16)


def gradient_kernel(kept, dp, meta_s, x_ref, up_ref, keep_ref, send_ref, store):
    side = keep_ref.shape[1]
    per = x_ref.shape[2] // side
    blocks = dp * kept
    bits = dp.bit_length() - 1
    me = lax.axis_index("dp")
    store[0:blocks] = jnp.zeros((blocks, side, side), f32)
    for b in range(blocks):
        row, col, dest = meta_s[b, 0], meta_s[b, 1], meta_s[b, 2]
        x = x_ref[row // per, :, pl.ds(pl.multiple_of((row % per) * side, side), side)]
        grad = lax.dot_general(
            x, lanes(up_ref, col, side), (((0,), (0,)), ((), ())), preferred_element_type=f32
        )
        gap = jnp.bitwise_xor(jnp.maximum(dest, 0) // kept, me)
        place = jnp.int32(0)
        for bit in range(bits):
            place = place * 2 + (lax.shift_right_logical(gap, bit) & 1)
        slot = jnp.where(dest >= 0, place * kept + jnp.maximum(dest, 0) % kept, blocks)
        store[slot] = grad * grad_scale
    half = keep_ref.shape[0]
    keep_ref[...] = store[0:half]
    send_ref[...] = store[half : 2 * half].astype(bf16)


def gradient(meta, x_all, upstream, kept, dp):
    side = meta.shape[1]
    blocks = dp * kept
    half = blocks // 2
    return pl.pallas_call(
        functools.partial(gradient_kernel, kept, dp),
        out_shape=(
            jax.ShapeDtypeStruct((half, side, side), f32),
            jax.ShapeDtypeStruct((half, side, side), bf16),
        ),
        in_specs=[SMEM, VMEM, VMEM],
        out_specs=(VMEM, VMEM),
        scratch_shapes=[pltpu.VMEM((blocks + 1, side, side), f32)],
        compiler_params=params(),
        cost_estimate=pl.CostEstimate(
            flops=2 * blocks * upstream.shape[0] * side * side,
            bytes_accessed=16 * 1024 * 1024,
            transcendentals=0,
        ),
        name="weight_gradient",
    )(meta, x_all, upstream)


def halving_reduce(keep, send, dp):
    step = 1
    while True:
        came = lax.ppermute(send, "dp", [(i, i ^ step) for i in range(dp)])
        step *= 2
        if step == dp:
            return keep, came
        total = keep + came.astype(f32)
        half = total.shape[0] // 2
        keep, send = total[:half], total[half:].astype(bf16)


def forward_kernel(kept, ids, meta_s, *refs):
    count = len(ids)
    packs = refs[:count]
    x_ref, out_ref, acc = refs[count:]
    side = packs[0].shape[1]
    pitch = side + TILE
    per = x_ref.shape[2] // side
    acc[...] = jnp.zeros_like(acc)
    for at, ident in enumerate(ids):
        for s in range(kept):
            row = meta_s[ident * kept + s, 0]
            col = meta_s[ident * kept + s, 1]
            x = x_ref[row // per, :, pl.ds(pl.multiple_of((row % per) * side, side), side)]
            part = jnp.dot(
                x, packs[at][s * pitch : s * pitch + side, :], preferred_element_type=f32
            )
            place = pl.ds(pl.multiple_of(col * side, side), side)
            acc[:, place] = acc[:, place] + part
    out_ref[...] = (acc[...] * grad_scale).astype(bf16)


def forward(meta, packs, ids, x_all, kept, hidden):
    tokens = x_all.shape[1]
    side = meta.shape[1]
    return pl.pallas_call(
        functools.partial(forward_kernel, kept, ids),
        out_shape=jax.ShapeDtypeStruct((tokens, hidden), bf16),
        in_specs=[SMEM] + [VMEM] * (len(ids) + 1),
        out_specs=VMEM,
        scratch_shapes=[pltpu.VMEM((tokens, hidden), f32)],
        compiler_params=params(),
        cost_estimate=pl.CostEstimate(
            flops=2 * len(ids) * kept * tokens * side * side,
            bytes_accessed=24 * 1024 * 1024,
            transcendentals=0,
        ),
        name="hidden_out",
    )(meta, *packs, x_all)


def update_kernel(
    dp, meta_s, keep_ref, came_ref, w_ref, one_ref, two_ref, left_ref, right_ref,
    new_w, new_one, new_two,
):
    kept, side = w_ref.shape[0], w_ref.shape[1]
    travel = 3 * side
    me = lax.axis_index("dp")
    source = [jnp.int32(-1)] * kept

    def place(source, dest, here, code):
        mine = here & (dest >= 0) & (jnp.maximum(dest, 0) // kept == me)
        slot = jnp.maximum(dest, 0) % kept
        found = [jnp.where(mine & (slot == q), code, source[q]) for q in range(kept)]
        return found, code + mine.astype(jnp.int32)

    for s in range(kept):
        source, _ = place(source, meta_s[s, 2], True, jnp.int32(s))
    for side_at, other in ((kept, me - 1), (kept + kept // 2, me + 1)):
        here = (other >= 0) & (other < dp)
        gap = jnp.where(here, jnp.bitwise_xor(jnp.clip(other, 0, dp - 1), me), 0)
        code = jnp.int32(side_at)
        for s in range(kept):
            source, code = place(source, meta_s[gap * kept + s, 2], here, code)

    for q in range(kept):

        def write(weight, one, two, q=q):
            grad = keep_ref[q] + came_ref[q].astype(f32)
            first = beta_first * one + (1.0 - beta_first) * grad
            second = beta_second * two + (1.0 - beta_second) * grad * grad
            stepped = weight - learn_rate * first / (jnp.sqrt(second) + epsilon)
            new_w[q] = stepped.astype(bf16)
            new_one[q] = first
            new_two[q] = second

        @pl.when(source[q] < 0)
        def _(q=q):
            new_w[q] = jnp.zeros((side, side), bf16)
            new_one[q] = jnp.zeros((side, side), f32)
            new_two[q] = jnp.zeros((side, side), f32)

        @pl.when((source[q] >= 0) & (source[q] < kept))
        def _(q=q):
            s = jnp.clip(source[q], 0, kept - 1)
            write(w_ref[s].astype(f32), one_ref[s], two_ref[s])

        for ref, first_code in ((left_ref, kept), (right_ref, kept + kept // 2)):

            @pl.when((source[q] >= first_code) & (source[q] < first_code + kept // 2))
            def _(q=q, ref=ref, first_code=first_code):
                rank = jnp.clip(source[q] - first_code, 0, kept // 2 - 1)
                base = pl.multiple_of(rank * travel, TILE)
                write(
                    ref[pl.ds(base, side), :].astype(f32),
                    ref[pl.ds(base + side, side), :].astype(f32),
                    ref[pl.ds(base + 2 * side, side), :].astype(f32),
                )


def update(meta, keep, came, weight, one, two, from_left, from_right, dp):
    shape = weight.shape
    return pl.pallas_call(
        functools.partial(update_kernel, dp),
        out_shape=(
            jax.ShapeDtypeStruct(shape, bf16),
            jax.ShapeDtypeStruct(shape, f32),
            jax.ShapeDtypeStruct(shape, f32),
        ),
        in_specs=[SMEM] + [VMEM] * 7,
        out_specs=(VMEM,) * 3,
        compiler_params=params(),
        name="adam_update",
    )(meta, keep, came, weight, one, two, from_left, from_right)


def body(weight, moment_one, moment_two, block_row, block_col, dest_slot, tokens, upstream):
    kept = weight.shape[0]
    dp = lax.axis_size("dp")
    slices = lax.axis_size("mp")
    x_all = lax.all_gather(tokens, "mp", axis=0)
    packed, to_left, to_right = pack(
        block_row, block_col, dest_slot, weight, moment_one, moment_two
    )
    packs, ids = [packed], [0]
    bit = dp // 2
    while bit:
        packs = packs + [
            lax.ppermute(p, "dp", [(i, i ^ bit) for i in range(dp)]) for p in packs
        ]
        ids = ids + [i ^ bit for i in ids]
        bit //= 2
    from_left = lax.ppermute(to_right, "dp", [(i, i + 1) for i in range(dp - 1)])
    from_right = lax.ppermute(to_left, "dp", [(i + 1, i) for i in range(dp - 1)])
    ids = tuple(ids)
    shares, meta = backward(packs, ids, upstream, kept, slices, tokens.shape[1])
    input_grad = line_reduce(shares, "mp")
    keep, send = gradient(meta, x_all, upstream, kept, dp)
    hidden_out = forward(meta, packs, ids, x_all, kept, upstream.shape[1])
    keep, came = halving_reduce(keep, send, dp)
    new_weight, new_first, new_second = update(
        meta, keep, came, weight, moment_one, moment_two, from_left, from_right, dp
    )
    return (new_weight, new_first, new_second, hidden_out, input_grad)


def solution(mesh):
    blocks = P(("dp", "mp"), None, None)
    ints = P(("dp", "mp"))
    acts = P("dp", "mp")
    return jax.shard_map(
        body,
        mesh=mesh,
        in_specs=(blocks, blocks, blocks, ints, ints, ints, acts, acts),
        out_specs=(blocks, blocks, blocks, acts, acts),
        check_vma=False,
    )
```

time: 211 us -> 113 us (0.54)
  waiting for transfers between devices: 106 us -> 43.7 us
  local copies, waits for them, and re-layouts: 42 us -> 9.38 us
  starting transfers between devices: 3.24 us -> 29.8 us
  other arithmetic: 25.1 us -> 4.76 us
  Pallas kernels: 0 us -> 10.4 us
  blocking collectives: 9.46 us -> 0 us
  matrix products: 9.35 us -> 0 us
    reduce_scatter x2 -> x0, waiting for transfers between devices: 65.1 us -> none  [the longest x1 58.9 us: body(): lax.psum_scatter(partial_in, 'mp', scatter_dimension=1, tiled=True)]
    ppermute x2 -> x18, waiting for transfers between devices: 0.01 us -> 43 us  [the longest x3 28.8 us: line_reduce(): right = lax.ppermute(to_right, axis, [(i, i + 1) for i in range(step)])]
    all_gather x2 -> x1, waiting for transfers between devices: 40.3 us -> 0.01 us  [body(): x_all = lax.all_gather(tokens, 'mp', axis=0)]
    ppermute x2 -> x18, starting transfers between devices: 3.08 us -> 29.7 us  [the longest x3 13.6 us: line_reduce(): right = lax.ppermute(to_right, axis, [(i, i + 1) for i in range(step)])]
    scatter-add x2 -> x0, other arithmetic: 12.4 us -> none  [the longest x1 6.22 us: body(): row_sums = jax.ops.segment_sum(backward, all_rows, num_segments=block_rows)]
    pallas_call x0 -> x5, Pallas kernels: none -> 10.4 us  [the longest x1 3.38 us: forward(): pl.pallas_call(functools.partial(forward_kernel, kept, ids), out_shape=ja...]
    unnamed x1 -> x0, blocking collectives: 9.46 us -> none
    dot_general x7 -> x0, matrix products: 9.35 us -> none  [the longest x1 2.87 us: body(): jnp.einsum('tbk,tbj->bkj', x_blocks, d_blocks, preferred_element_type=jnp...]
  transfers between devices with their start and end apart: 6 -> 19, of which waited for: 4 -> 7; matrix products, arithmetic and copies ran while one was open for 33% -> 4% of each run, Pallas kernels for 0% -> 7%
where the time goes in v1:
time: 113 us; the launch traced here: 112 us
  waiting for transfers between devices  43.7 us (39%)
  starting transfers between devices  29.8 us (26%)
  between operations  14.4 us (13%)
  Pallas kernels  10.4 us (9%)
  local copies, waits for them, and re-layouts  9.38 us (8%)
  other arithmetic  4.76 us (4%)
    ppermute x3, waiting for transfers between devices, line_reduce(): right = lax.ppermute(to_right, axis, [(i, i + 1) for i in range(step)])  28.8 us
    ppermute x3, starting transfers between devices, line_reduce(): right = lax.ppermute(to_right, axis, [(i, i + 1) for i in range(step)])  13.6 us
    unnamed x56, local copies, waits for them, and re-layouts  9.3 us
    ppermute x7, starting transfers between devices, body(): lax.ppermute(p, 'dp', [(i, i ^ bit) for i in range(dp)])  6.69 us
    ppermute x7, waiting for transfers between devices, body(): lax.ppermute(p, 'dp', [(i, i ^ bit) for i in range(dp)])  6.6 us
    ppermute x3, waiting for transfers between devices, halving_reduce(): came = lax.ppermute(send, 'dp', [(i, i ^ step) for i in range(dp)])  3.98 us
    ppermute x3, waiting for transfers between devices, line_reduce(): lax.ppermute(to_left, axis, [(n - 1 - i, n - 2 - i) for i in range(step)])  3.63 us
    ppermute x3, starting transfers between devices, line_reduce(): lax.ppermute(to_left, axis, [(n - 1 - i, n - 2 - i) for i in range(step)])  3.56 us
  transfers between devices with their start and end apart: 19, of which 7 were waited for; matrix products, arithmetic and copies ran while one was open for 4% of the time, Pallas kernels for 7%

profile of v1, /device:TPU:0, one launch (start us, length us, event | category | flops | bytes accessed | tf_op | source)
XLA Modules:
  0.0 112.3 jit_solution(6052418901748327417)
XLA Ops:
  7.2 0.0 all-gather.3.cloned.1.call-start
  7.2 0.7 all-gather.3.cloned.1.call-update
  7.9 0.0 copy-start.3
  7.9 0.9 copy-done.3
  8.9 0.9 copy-done.5
  9.8 0.9 copy-done.19
  10.7 0.7 copy-done.21
  11.4 0.7 copy-done.22
  12.0 0.7 copy-done.23
  12.7 0.7 pack_blocks.1
  13.4 0.0 copy-start.24
  13.4 0.7 copy-done.24
  14.1 0.7 copy-done.26
  14.7 3.0 %collective-permute-start = (bf16[576,128]{1,0:T(8,128)(2,1)S(1)}, bf16[576,128]{1,0:T(8,128)(2,1)S(1)}, u32[]{:S(2)}, u32[]{:S(2)}) collective-permute-start(bf16[576,128]{1,0:T(8,128)(2,1)S(1)} %get-tuple-element.18.refs_0_), channel_id=1, source_target_pairs={{0,16},{4,20},{8,24},{12,28},{16,0},{20,4},{24,8},{28,12},{1,17},{... | collective-permute-start | bytes 442376 | tf_op jit(solution)/shard_map/ppermute | solution.py:347
  17.7 1.5 %collective-permute-start.1 = (bf16[576,128]{1,0:T(8,128)(2,1)S(1)}, bf16[576,128]{1,0:T(8,128)(2,1)S(1)}, u32[]{:S(2)}, u32[]{:S(2)}) collective-permute-start(bf16[576,128]{1,0:T(8,128)(2,1)S(1)} %get-tuple-element.18.refs_0_), channel_id=1, source_target_pairs={{0,8},{4,12},{8,0},{12,4},{16,24},{20,28},{24,16},{28,20},{1,9},{5... | collective-permute-start | bytes 442376 | tf_op jit(solution)/shard_map/ppermute | solution.py:347
  19.2 2.4 %collective-permute-done.refs_1_ = bf16[576,128]{1,0:T(8,128)(2,1)S(1)} collective-permute-done((bf16[576,128]{1,0:T(8,128)(2,1)S(1)}, bf16[576,128]{1,0:T(8,128)(2,1)S(1)}, u32[]{:S(2)}, u32[]{:S(2)}) %collective-permute-start) | collective-permute-done | bytes 147488 | tf_op jit(solution)/shard_map/ppermute | solution.py:347
  21.6 1.7 %collective-permute-start.2 = (bf16[576,128]{1,0:T(8,128)(2,1)S(1)}, bf16[576,128]{1,0:T(8,128)(2,1)S(1)}, u32[]{:S(2)}, u32[]{:S(2)}) collective-permute-start(bf16[576,128]{1,0:T(8,128)(2,1)S(1)} %collective-permute-done.refs_1_), channel_id=1, source_target_pairs={{0,8},{4,12},{8,0},{12,4},{16,24},{20,28},{24,16},{28,20},{1,9},{5... | collective-permute-start | bytes 442376 | tf_op jit(solution)/shard_map/ppermute | solution.py:347
  23.3 0.0 collective-permute-start.3
  23.3 0.5 collective-permute-start.4
  23.8 0.0 collective-permute-done.1.refs_2_
  23.8 0.0 collective-permute-start.5
  23.8 2.9 %collective-permute-done.2.refs_3_ = bf16[576,128]{1,0:T(8,128)(2,1)S(1)} collective-permute-done((bf16[576,128]{1,0:T(8,128)(2,1)S(1)}, bf16[576,128]{1,0:T(8,128)(2,1)S(1)}, u32[]{:S(2)}, u32[]{:S(2)}) %collective-permute-start.2) | collective-permute-done | bytes 147488 | tf_op jit(solution)/shard_map/ppermute | solution.py:347
  26.7 0.0 collective-permute-start.6
  26.7 0.0 collective-permute-done.3.refs_4_
  26.7 0.0 collective-permute-done.4.refs_5_
  26.7 0.0 collective-permute-done.5.refs_6_
  26.8 1.3 %collective-permute-done.6.refs_7_ = bf16[576,128]{1,0:T(8,128)(2,1)S(1)} collective-permute-done((bf16[576,128]{1,0:T(8,128)(2,1)S(1)}, bf16[576,128]{1,0:T(8,128)(2,1)S(1)}, u32[]{:S(2)}, u32[]{:S(2)}) %collective-permute-start.6) | collective-permute-done | bytes 147488 | tf_op jit(solution)/shard_map/ppermute | solution.py:347
  28.1 1.5 %copy-done.1 = bf16[128,7168]{1,0:T(8,128)(2,1)S(1)} copy-done((bf16[128,7168]{1,0:T(8,128)(2,1)S(1)}, bf16[128,7168]{1,0:T(8,128)(2,1)}, u32[]{:S(2)}) %copy-start.1) | copy-done | bytes 1835032
  29.6 2.3 %input_gradient.1 = (f32[128,2048]{1,0:T(8,128)S(1)}, bf16[128,2048]{1,0:T(8,128)(2,1)S(1)}, bf16[128,2048]{1,0:T(8,128)(2,1)S(1)}, bf16[128,2048]{1,0:T(8,128)(2,1)S(1)}, s32[32,128]{1,0:T(8,128)S(1)}) custom-call(bf16[576,128]{1,0:T(8,128)(2,1)S(1)} %get-tuple-element.18.refs_0_, bf16[576,128]{1,0:T(8,128)(2,1)S(1)} %collective-permute-done.refs_1_, ...), custom_call_target="tpu_custom_call" | custom-call | flops 134217728 | bytes 25165824 | tf_op jit(solution)/shard_map/input_gradient/pallas_call | solution.py:125
  32.0 0.0 copy-start.2
  32.0 4.0 %collective-permute-start.12 = (bf16[128,2048]{1,0:T(8,128)(2,1)S(1)}, bf16[128,2048]{1,0:T(8,128)(2,1)S(1)}, u32[]{:S(2)}, u32[]{:S(2)}) collective-permute-start(bf16[128,2048]{1,0:T(8,128)(2,1)S(1)} %get-tuple-element.30), channel_id=1, source_target_pairs={{0,1},{4,5},{8,9},{12,13},{16,17},{20,21},{24,25},{28,29}} | collective-permute-start | bytes 1572872 | tf_op jit(solution)/shard_map/ppermute | solution.py:154
  36.0 0.7 collective-permute-start.15
  36.7 22.5 %collective-permute-done.12 = bf16[128,2048]{1,0:T(8,128)(2,1)S(1)} collective-permute-done((bf16[128,2048]{1,0:T(8,128)(2,1)S(1)}, bf16[128,2048]{1,0:T(8,128)(2,1)S(1)}, u32[]{:S(2)}, u32[]{:S(2)}) %collective-permute-start.12) | collective-permute-done | bytes 524320 | tf_op jit(solution)/shard_map/ppermute | solution.py:154
  59.2 0.0 collective-permute-done.15
  59.2 1.3 %fusion = (bf16[128,2048]{1,0:T(8,128)(2,1)}, bf16[128,2048]{1,0:T(8,128)(2,1)}) fusion(bf16[128,2048]{1,0:T(8,128)(2,1)S(1)} %get-tuple-element.29, bf16[128,2048]{1,0:T(8,128)(2,1)S(1)} %collective-permute-done.12, bf16[128,2048]{1,0:T(8,128)(2,1)S(1)} %collective-permute-done.15), kind=kLoop, calls=%fused_computation.2 | loop fusion | flops 1835008 | bytes 2621440 | tf_op jit(solution)/shard_map/convert_element_type | solution.py:152
  60.5 5.2 %collective-permute-start.13 = (bf16[128,2048]{1,0:T(8,128)(2,1)}, bf16[128,2048]{1,0:T(8,128)(2,1)}, u32[]{:S(2)}, u32[]{:S(2)}) collective-permute-start(bf16[128,2048]{1,0:T(8,128)(2,1)} %get-tuple-element.31), channel_id=1, source_target_pairs={{0,1},{1,2},{4,5},{5,6},{8,9},{9,10},{12,13},{13,14},{16,17},{17,1... | collective-permute-start | bytes 1572872 | tf_op jit(solution)/shard_map/ppermute | solution.py:154
  65.7 1.4 %collective-permute-start.16 = (bf16[128,2048]{1,0:T(8,128)(2,1)}, bf16[128,2048]{1,0:T(8,128)(2,1)}, u32[]{:S(2)}, u32[]{:S(2)}) collective-permute-start(bf16[128,2048]{1,0:T(8,128)(2,1)} %get-tuple-element.32), channel_id=1, source_target_pairs={{3,2},{2,1},{7,6},{6,5},{11,10},{10,9},{15,14},{14,13},{19,18},{18... | collective-permute-start | bytes 1572872 | tf_op jit(solution)/shard_map/ppermute | solution.py:155
  67.1 1.6 %copy-done = bf16[512,2048]{1,0:T(8,128)(2,1)S(1)} copy-done((bf16[512,2048]{1,0:T(8,128)(2,1)S(1)}, bf16[512,2048]{1,0:T(8,128)(2,1)}, u32[]{:S(2)}) %copy-start) | copy-done | bytes 2097176
  68.7 2.0 %weight_gradient.1 = (f32[16,128,128]{2,1,0:T(8,128)S(1)}, bf16[16,128,128]{2,1,0:T(8,128)(2,1)S(1)}) custom-call(s32[32,128]{1,0:T(8,128)S(1)} %get-tuple-element.19.meta_s, bf16[4,128,2048]{2,1,0:T(8,128)(2,1)S(1)} %bitcast.1, bf16[128,7168]{1,0:T(8,128)(2,1)S(1)} %copy-done.2), custom_call_target="tpu_custom_call" | custom-call | flops 134217728 | bytes 16777216 | tf_op jit(solution)/shard_map/weight_gradient/pallas_call | solution.py:189
  70.7 0.1 collective-permute-start.7
  70.8 6.3 %collective-permute-done.13 = bf16[128,2048]{1,0:T(8,128)(2,1)} collective-permute-done((bf16[128,2048]{1,0:T(8,128)(2,1)}, bf16[128,2048]{1,0:T(8,128)(2,1)}, u32[]{:S(2)}, u32[]{:S(2)}) %collective-permute-start.13) | collective-permute-done | bytes 524320 | tf_op jit(solution)/shard_map/ppermute | solution.py:154
  77.0 1.2 %add_convert_fusion.2 = bf16[128,2048]{1,0:T(8,128)(2,1)S(1)} fusion(bf16[128,2048]{1,0:T(8,128)(2,1)} %collective-permute-done.13, bf16[128,2048]{1,0:T(8,128)(2,1)S(1)} %copy-done.18), kind=kLoop, calls=%fused_computation.6 | loop fusion | flops 1048576 | bytes 1572864 | tf_op jit(solution)/shard_map/convert_element_type | solution.py:152
  78.2 4.4 %collective-permute-start.14 = (bf16[128,2048]{1,0:T(8,128)(2,1)S(1)}, bf16[128,2048]{1,0:T(8,128)(2,1)S(1)}, u32[]{:S(2)}, u32[]{:S(2)}) collective-permute-start(bf16[128,2048]{1,0:T(8,128)(2,1)S(1)} %add_convert_fusion.2), channel_id=1, source_target_pairs={{0,1},{1,2},{2,3},{4,5},{5,6},{6,7},{8,9},{9,10},{10,11},{12,13},{... | collective-permute-start | bytes 1572872 | tf_op jit(solution)/shard_map/ppermute | solution.py:154
  82.6 0.0 collective-permute-done.16
  82.7 1.2 %add_convert_fusion.1 = bf16[128,2048]{1,0:T(8,128)(2,1)S(1)} fusion(bf16[128,2048]{1,0:T(8,128)(2,1)} %collective-permute-done.16, bf16[128,2048]{1,0:T(8,128)(2,1)S(1)} %copy-done.16), kind=kLoop, calls=%fused_computation.5 | loop fusion | flops 1048576 | bytes 1572864 | tf_op jit(solution)/shard_map/convert_element_type | solution.py:153
  83.8 0.0 copy-start.27
  83.8 0.0 copy-start.25
  83.9 1.4 %collective-permute-start.17 = (bf16[128,2048]{1,0:T(8,128)(2,1)S(1)}, bf16[128,2048]{1,0:T(8,128)(2,1)S(1)}, u32[]{:S(2)}, u32[]{:S(2)}) collective-permute-start(bf16[128,2048]{1,0:T(8,128)(2,1)S(1)} %add_convert_fusion.1), channel_id=1, source_target_pairs={{3,2},{2,1},{1,0},{7,6},{6,5},{5,4},{11,10},{10,9},{9,8},{15,14},{... | collective-permute-start | bytes 1572872 | tf_op jit(solution)/shard_map/ppermute | solution.py:155
  85.3 0.0 collective-permute-done.7
  85.3 0.1 convert_add_fusion.2
  85.5 1.6 %collective-permute-start.8 = (bf16[8,128,128]{2,1,0:T(8,128)(2,1)S(1)}, bf16[8,128,128]{2,1,0:T(8,128)(2,1)S(1)}, u32[]{:S(2)}, u32[]{:S(2)}) collective-permute-start(bf16[8,128,128]{2,1,0:T(8,128)(2,1)S(1)} %slice.25), channel_id=1, source_target_pairs={{0,8},{4,12},{8,0},{12,4},{16,24},{20,28},{24,16},{28,20},{1,9},{5... | collective-permute-start | bytes 786440 | tf_op jit(solution)/shard_map/ppermute | solution.py:211
  87.0 1.3 %collective-permute-start.10 = (bf16[768,128]{1,0:T(8,128)(2,1)S(1)}, bf16[768,128]{1,0:T(8,128)(2,1)S(1)}, u32[]{:S(2)}, u32[]{:S(2)}) collective-permute-start(bf16[768,128]{1,0:T(8,128)(2,1)S(1)} %copy-done.27), channel_id=1, source_target_pairs={{0,4},{4,8},{8,12},{12,16},{16,20},{20,24},{24,28},{1,5},{5,9},{9,... | collective-permute-start | bytes 589832 | tf_op jit(solution)/shard_map/ppermute | solution.py:351
  88.4 1.4 %collective-permute-start.11 = (bf16[768,128]{1,0:T(8,128)(2,1)S(1)}, bf16[768,128]{1,0:T(8,128)(2,1)S(1)}, u32[]{:S(2)}, u32[]{:S(2)}) collective-permute-start(bf16[768,128]{1,0:T(8,128)(2,1)S(1)} %copy-done.25), channel_id=1, source_target_pairs={{4,0},{8,4},{12,8},{16,12},{20,16},{24,20},{28,24},{5,1},{9,5},{13... | collective-permute-start | bytes 589832 | tf_op jit(solution)/shard_map/ppermute | solution.py:352
  89.8 4.0 %collective-permute-done.8 = bf16[8,128,128]{2,1,0:T(8,128)(2,1)S(1)} collective-permute-done((bf16[8,128,128]{2,1,0:T(8,128)(2,1)S(1)}, bf16[8,128,128]{2,1,0:T(8,128)(2,1)S(1)}, u32[]{:S(2)}, u32[]{:S(2)}) %collective-permute-start.8) | collective-permute-done | bytes 262176 | tf_op jit(solution)/shard_map/ppermute | solution.py:211
  93.8 1.5 %collective-permute-start.9 = (bf16[4,128,128]{2,1,0:T(8,128)(2,1)S(1)}, bf16[4,128,128]{2,1,0:T(8,128)(2,1)S(1)}, u32[]{:S(2)}, u32[]{:S(2)}) collective-permute-start(bf16[4,128,128]{2,1,0:T(8,128)(2,1)S(1)} %slice.26), channel_id=1, source_target_pairs={{0,16},{4,20},{8,24},{12,28},{16,0},{20,4},{24,8},{28,12},{1,17},{... | collective-permute-start | bytes 393224 | tf_op jit(solution)/shard_map/ppermute | solution.py:211
  95.4 0.0 collective-permute-done.14
  95.4 3.6 %collective-permute-done.17 = bf16[128,2048]{1,0:T(8,128)(2,1)S(1)} collective-permute-done((bf16[128,2048]{1,0:T(8,128)(2,1)S(1)}, bf16[128,2048]{1,0:T(8,128)(2,1)S(1)}, u32[]{:S(2)}, u32[]{:S(2)}) %collective-permute-start.17) | collective-permute-done | bytes 524320 | tf_op jit(solution)/shard_map/ppermute | solution.py:155
  99.0 1.0 add_convert_fusion
  100.0 0.0 copy-start.4
  100.0 0.0 copy-start.6
  100.0 0.0 copy-start.20
  100.1 3.4 %hidden_out.1 = bf16[128,7168]{1,0:T(8,128)(2,1)} custom-call(s32[32,128]{1,0:T(8,128)S(1)} %get-tuple-element.19.meta_s, bf16[576,128]{1,0:T(8,128)(2,1)S(1)} %get-tuple-element.18.refs_0_, bf16[576,128]{1,0:T(8,128)(2,1)S(1)} %collective-permute-done.refs_1_, bf16[576,128]{1,0:T(8,128)(2,1)S(1)} %collective-permute-done.1.refs_2_, ...), custom_call_target="tpu_custom_call" | custom-call | flops 134217728 | bytes 25165824 | tf_op jit(solution)/shard_map/hidden_out/pallas_call | solution.py:244
  103.5 0.0 collective-permute-done.10.left_ref
  103.5 2.0 %adam_update.1 = (bf16[4,128,128]{2,1,0:T(8,128)(2,1)}, f32[4,128,128]{2,1,0:T(8,128)}, f32[4,128,128]{2,1,0:T(8,128)}) custom-call(s32[32,128]{1,0:T(8,128)S(1)} %get-tuple-element.19.meta_s, f32[4,128,128]{2,1,0:T(8,128)S(1)} %slice.20.keep_ref, bf16[4,128,128]{2,1,0:T(8,128)(2,1)S(1)} %collective-permute-done.9.came_ref, ...), custom_call_target="tpu_custom_call" | custom-call | tf_op jit(solution)/shard_map/adam_update/pallas_call | solution.py:321
  (45 shorter events, 0.2 us)
Async XLA Ops:
  7.2 59.9 %all-gather.3.cloned.1.call-start = ((), (), s32[]{:S(2)}) async-start(), calls=%async_computation | async-start | bytes 2621440 | tf_op jit(solution)/shard_map/all_gather | solution.py:339
  7.9 1.0 copy-start.3
  8.9 0.9 copy-start.5
  9.8 0.9 copy-start.19
  10.7 0.7 copy-start.21
  11.4 0.7 copy-start.22
  12.0 0.7 copy-start.23
  13.4 0.7 copy-start.24
  14.1 0.7 copy-start.26
  14.7 6.8 %collective-permute-start = (bf16[576,128]{1,0:T(8,128)(2,1)S(1)}, bf16[576,128]{1,0:T(8,128)(2,1)S(1)}, u32[]{:S(2)}, u32[]{:S(2)}) collective-permute-start(bf16[576,128]{1,0:T(8,128)(2,1)S(1)} %get-tuple-element.18.refs_0_), channel_id=1, source_target_pairs={{0,16},{4,20},{8,24},{12,28},{16,0},{20,4},{24,8},{28,12},{1,17},{... | collective-permute-start | bytes 442376 | tf_op jit(solution)/shard_map/ppermute | solution.py:347
  17.7 6.1 %collective-permute-start.1 = (bf16[576,128]{1,0:T(8,128)(2,1)S(1)}, bf16[576,128]{1,0:T(8,128)(2,1)S(1)}, u32[]{:S(2)}, u32[]{:S(2)}) collective-permute-start(bf16[576,128]{1,0:T(8,128)(2,1)S(1)} %get-tuple-element.18.refs_0_), channel_id=1, source_target_pairs={{0,8},{4,12},{8,0},{12,4},{16,24},{20,28},{24,16},{28,20},{1,9},{5... | collective-permute-start | bytes 442376 | tf_op jit(solution)/shard_map/ppermute | solution.py:347
  21.6 5.1 %collective-permute-start.2 = (bf16[576,128]{1,0:T(8,128)(2,1)S(1)}, bf16[576,128]{1,0:T(8,128)(2,1)S(1)}, u32[]{:S(2)}, u32[]{:S(2)}) collective-permute-start(bf16[576,128]{1,0:T(8,128)(2,1)S(1)} %collective-permute-done.refs_1_), channel_id=1, source_target_pairs={{0,8},{4,12},{8,0},{12,4},{16,24},{20,28},{24,16},{28,20},{1,9},{5... | collective-permute-start | bytes 442376 | tf_op jit(solution)/shard_map/ppermute | solution.py:347
  23.3 3.4 %collective-permute-start.3 = (bf16[576,128]{1,0:T(8,128)(2,1)S(1)}, bf16[576,128]{1,0:T(8,128)(2,1)S(1)}, u32[]{:S(2)}, u32[]{:S(2)}) collective-permute-start(bf16[576,128]{1,0:T(8,128)(2,1)S(1)} %get-tuple-element.18.refs_0_), channel_id=1, source_target_pairs={{0,4},{4,0},{8,12},{12,8},{16,20},{20,16},{24,28},{28,24},{1,5},{5... | collective-permute-start | bytes 442376 | tf_op jit(solution)/shard_map/ppermute | solution.py:347
  23.3 3.4 %collective-permute-start.4 = (bf16[576,128]{1,0:T(8,128)(2,1)S(1)}, bf16[576,128]{1,0:T(8,128)(2,1)S(1)}, u32[]{:S(2)}, u32[]{:S(2)}) collective-permute-start(bf16[576,128]{1,0:T(8,128)(2,1)S(1)} %collective-permute-done.refs_1_), channel_id=1, source_target_pairs={{0,4},{4,0},{8,12},{12,8},{16,20},{20,16},{24,28},{28,24},{1,5},{5... | collective-permute-start | bytes 442376 | tf_op jit(solution)/shard_map/ppermute | solution.py:347
  23.8 3.0 %collective-permute-start.5 = (bf16[576,128]{1,0:T(8,128)(2,1)S(1)}, bf16[576,128]{1,0:T(8,128)(2,1)S(1)}, u32[]{:S(2)}, u32[]{:S(2)}) collective-permute-start(bf16[576,128]{1,0:T(8,128)(2,1)S(1)} %collective-permute-done.1.refs_2_), channel_id=1, source_target_pairs={{0,4},{4,0},{8,12},{12,8},{16,20},{20,16},{24,28},{28,24},{1,5},{5... | collective-permute-start | bytes 442376 | tf_op jit(solution)/shard_map/ppermute | solution.py:347
  26.7 1.4 %collective-permute-start.6 = (bf16[576,128]{1,0:T(8,128)(2,1)S(1)}, bf16[576,128]{1,0:T(8,128)(2,1)S(1)}, u32[]{:S(2)}, u32[]{:S(2)}) collective-permute-start(bf16[576,128]{1,0:T(8,128)(2,1)S(1)} %collective-permute-done.2.refs_3_), channel_id=1, source_target_pairs={{0,4},{4,0},{8,12},{12,8},{16,20},{20,16},{24,28},{28,24},{1,5},{5... | collective-permute-start | bytes 442376 | tf_op jit(solution)/shard_map/ppermute | solution.py:347
  26.7 33.7 %copy-start.7 = (bf16[576,128]{1,0:T(8,128)(2,1)}, bf16[576,128]{1,0:T(8,128)(2,1)S(1)}, u32[]{:S(2)}) copy-start(bf16[576,128]{1,0:T(8,128)(2,1)S(1)} %collective-permute-done.3.refs_4_) | copy-start | bytes 442372
  26.7 33.7 %copy-start.9 = (bf16[576,128]{1,0:T(8,128)(2,1)}, bf16[576,128]{1,0:T(8,128)(2,1)S(1)}, u32[]{:S(2)}) copy-start(bf16[576,128]{1,0:T(8,128)(2,1)S(1)} %collective-permute-done.4.refs_5_) | copy-start | bytes 442372
  26.7 33.7 %copy-start.11 = (bf16[576,128]{1,0:T(8,128)(2,1)}, bf16[576,128]{1,0:T(8,128)(2,1)S(1)}, u32[]{:S(2)}) copy-start(bf16[576,128]{1,0:T(8,128)(2,1)S(1)} %collective-permute-done.5.refs_6_) | copy-start | bytes 442372
  28.1 1.5 %copy-start.1 = (bf16[128,7168]{1,0:T(8,128)(2,1)S(1)}, bf16[128,7168]{1,0:T(8,128)(2,1)}, u32[]{:S(2)}) copy-start(bf16[128,7168]{1,0:T(8,128)(2,1)} %up_ref.1) | copy-start | bytes 5505028
  29.6 30.9 %copy-start.13 = (bf16[576,128]{1,0:T(8,128)(2,1)}, bf16[576,128]{1,0:T(8,128)(2,1)S(1)}, u32[]{:S(2)}) copy-start(bf16[576,128]{1,0:T(8,128)(2,1)S(1)} %collective-permute-done.6.refs_7_) | copy-start | bytes 442372
  31.9 28.5 %copy-start.15 = (bf16[128,2048]{1,0:T(8,128)(2,1)}, bf16[128,2048]{1,0:T(8,128)(2,1)S(1)}, u32[]{:S(2)}) copy-start(bf16[128,2048]{1,0:T(8,128)(2,1)S(1)} %get-tuple-element.30) | copy-start | bytes 1572868
  31.9 33.7 %copy-start.17 = (bf16[128,2048]{1,0:T(8,128)(2,1)}, bf16[128,2048]{1,0:T(8,128)(2,1)S(1)}, u32[]{:S(2)}) copy-start(bf16[128,2048]{1,0:T(8,128)(2,1)S(1)} %get-tuple-element.28) | copy-start | bytes 1572868
  32.0 35.2 %copy-start.2 = (bf16[128,7168]{1,0:T(8,128)(2,1)S(1)}, bf16[128,7168]{1,0:T(8,128)(2,1)}, u32[]{:S(2)}) copy-start(bf16[128,7168]{1,0:T(8,128)(2,1)} %up_ref.1) | copy-start | bytes 5505028
  32.0 27.2 %collective-permute-start.12 = (bf16[128,2048]{1,0:T(8,128)(2,1)S(1)}, bf16[128,2048]{1,0:T(8,128)(2,1)S(1)}, u32[]{:S(2)}, u32[]{:S(2)}) collective-permute-start(bf16[128,2048]{1,0:T(8,128)(2,1)S(1)} %get-tuple-element.30), channel_id=1, source_target_pairs={{0,1},{4,5},{8,9},{12,13},{16,17},{20,21},{24,25},{28,29}} | collective-permute-start | bytes 1572872 | tf_op jit(solution)/shard_map/ppermute | solution.py:154
  36.0 23.2 %collective-permute-start.15 = (bf16[128,2048]{1,0:T(8,128)(2,1)S(1)}, bf16[128,2048]{1,0:T(8,128)(2,1)S(1)}, u32[]{:S(2)}, u32[]{:S(2)}) collective-permute-start(bf16[128,2048]{1,0:T(8,128)(2,1)S(1)} %get-tuple-element.28), channel_id=1, source_target_pairs={{3,2},{7,6},{11,10},{15,14},{19,18},{23,22},{27,26},{31,30}} | collective-permute-start | bytes 1572872 | tf_op jit(solution)/shard_map/ppermute | solution.py:155
  60.5 16.6 %collective-permute-start.13 = (bf16[128,2048]{1,0:T(8,128)(2,1)}, bf16[128,2048]{1,0:T(8,128)(2,1)}, u32[]{:S(2)}, u32[]{:S(2)}) collective-permute-start(bf16[128,2048]{1,0:T(8,128)(2,1)} %get-tuple-element.31), channel_id=1, source_target_pairs={{0,1},{1,2},{4,5},{5,6},{8,9},{9,10},{12,13},{13,14},{16,17},{17,1... | collective-permute-start | bytes 1572872 | tf_op jit(solution)/shard_map/ppermute | solution.py:154
  65.7 17.0 %collective-permute-start.16 = (bf16[128,2048]{1,0:T(8,128)(2,1)}, bf16[128,2048]{1,0:T(8,128)(2,1)}, u32[]{:S(2)}, u32[]{:S(2)}) collective-permute-start(bf16[128,2048]{1,0:T(8,128)(2,1)} %get-tuple-element.32), channel_id=1, source_target_pairs={{3,2},{2,1},{7,6},{6,5},{11,10},{10,9},{15,14},{14,13},{19,18},{18... | collective-permute-start | bytes 1572872 | tf_op jit(solution)/shard_map/ppermute | solution.py:155
  67.1 1.6 %copy-start = (bf16[512,2048]{1,0:T(8,128)(2,1)S(1)}, bf16[512,2048]{1,0:T(8,128)(2,1)}, u32[]{:S(2)}) copy-start(bf16[512,2048]{1,0:T(8,128)(2,1)} %all-gather.3.cloned.1.call-done) | copy-start | bytes 6291460
  68.7 8.3 %copy-start.18 = (bf16[128,2048]{1,0:T(8,128)(2,1)S(1)}, bf16[128,2048]{1,0:T(8,128)(2,1)}, u32[]{:S(2)}) copy-start(bf16[128,2048]{1,0:T(8,128)(2,1)} %copy-done.17) | copy-start | bytes 1572868
  68.7 13.9 %copy-start.16 = (bf16[128,2048]{1,0:T(8,128)(2,1)S(1)}, bf16[128,2048]{1,0:T(8,128)(2,1)}, u32[]{:S(2)}) copy-start(bf16[128,2048]{1,0:T(8,128)(2,1)} %copy-done.15) | copy-start | bytes 1572868
  70.7 14.6 %collective-permute-start.7 = (bf16[16,128,128]{2,1,0:T(8,128)(2,1)S(1)}, bf16[16,128,128]{2,1,0:T(8,128)(2,1)S(1)}, u32[]{:S(2)}, u32[]{:S(2)}) collective-permute-start(bf16[16,128,128]{2,1,0:T(8,128)(2,1)S(1)} %get-tuple-element.21), channel_id=1, source_target_pairs={{0,4},{4,0},{8,12},{12,8},{16,20},{20,16},{24,28},{28,24},{1,5},{5... | collective-permute-start | bytes 1572872 | tf_op jit(solution)/shard_map/ppermute | solution.py:211
  78.2 17.2 %collective-permute-start.14 = (bf16[128,2048]{1,0:T(8,128)(2,1)S(1)}, bf16[128,2048]{1,0:T(8,128)(2,1)S(1)}, u32[]{:S(2)}, u32[]{:S(2)}) collective-permute-start(bf16[128,2048]{1,0:T(8,128)(2,1)S(1)} %add_convert_fusion.2), channel_id=1, source_target_pairs={{0,1},{1,2},{2,3},{4,5},{5,6},{6,7},{8,9},{9,10},{10,11},{12,13},{... | collective-permute-start | bytes 1572872 | tf_op jit(solution)/shard_map/ppermute | solution.py:154
  83.8 3.2 %copy-start.27 = (bf16[768,128]{1,0:T(8,128)(2,1)S(1)}, bf16[768,128]{1,0:T(8,128)(2,1)}, u32[]{:S(2)}) copy-start(bf16[768,128]{1,0:T(8,128)(2,1)} %copy-done.26) | copy-start | bytes 589828
  83.8 4.5 %copy-start.25 = (bf16[768,128]{1,0:T(8,128)(2,1)S(1)}, bf16[768,128]{1,0:T(8,128)(2,1)}, u32[]{:S(2)}) copy-start(bf16[768,128]{1,0:T(8,128)(2,1)} %copy-done.24) | copy-start | bytes 589828
  83.9 15.2 %collective-permute-start.17 = (bf16[128,2048]{1,0:T(8,128)(2,1)S(1)}, bf16[128,2048]{1,0:T(8,128)(2,1)S(1)}, u32[]{:S(2)}, u32[]{:S(2)}) collective-permute-start(bf16[128,2048]{1,0:T(8,128)(2,1)S(1)} %add_convert_fusion.1), channel_id=1, source_target_pairs={{3,2},{2,1},{1,0},{7,6},{6,5},{5,4},{11,10},{10,9},{9,8},{15,14},{... | collective-permute-start | bytes 1572872 | tf_op jit(solution)/shard_map/ppermute | solution.py:155
  85.5 8.3 %collective-permute-start.8 = (bf16[8,128,128]{2,1,0:T(8,128)(2,1)S(1)}, bf16[8,128,128]{2,1,0:T(8,128)(2,1)S(1)}, u32[]{:S(2)}, u32[]{:S(2)}) collective-permute-start(bf16[8,128,128]{2,1,0:T(8,128)(2,1)S(1)} %slice.25), channel_id=1, source_target_pairs={{0,8},{4,12},{8,0},{12,4},{16,24},{20,28},{24,16},{28,20},{1,9},{5... | collective-permute-start | bytes 786440 | tf_op jit(solution)/shard_map/ppermute | solution.py:211
  87.0 16.4 %collective-permute-start.10 = (bf16[768,128]{1,0:T(8,128)(2,1)S(1)}, bf16[768,128]{1,0:T(8,128)(2,1)S(1)}, u32[]{:S(2)}, u32[]{:S(2)}) collective-permute-start(bf16[768,128]{1,0:T(8,128)(2,1)S(1)} %copy-done.27), channel_id=1, source_target_pairs={{0,4},{4,8},{8,12},{12,16},{16,20},{20,24},{24,28},{1,5},{5,9},{9,... | collective-permute-start | bytes 589832 | tf_op jit(solution)/shard_map/ppermute | solution.py:351
  88.3 11.7 %copy-start.8 = (bf16[576,128]{1,0:T(8,128)(2,1)S(1)}, bf16[576,128]{1,0:T(8,128)(2,1)}, u32[]{:S(2)}) copy-start(bf16[576,128]{1,0:T(8,128)(2,1)} %copy-done.7) | copy-start | bytes 442372
  88.3 11.7 %copy-start.10 = (bf16[576,128]{1,0:T(8,128)(2,1)S(1)}, bf16[576,128]{1,0:T(8,128)(2,1)}, u32[]{:S(2)}) copy-start(bf16[576,128]{1,0:T(8,128)(2,1)} %copy-done.9) | copy-start | bytes 442372
  88.3 11.7 %copy-start.12 = (bf16[576,128]{1,0:T(8,128)(2,1)S(1)}, bf16[576,128]{1,0:T(8,128)(2,1)}, u32[]{:S(2)}) copy-start(bf16[576,128]{1,0:T(8,128)(2,1)} %copy-done.11) | copy-start | bytes 442372
  88.3 11.7 %copy-start.14 = (bf16[576,128]{1,0:T(8,128)(2,1)S(1)}, bf16[576,128]{1,0:T(8,128)(2,1)}, u32[]{:S(2)}) copy-start(bf16[576,128]{1,0:T(8,128)(2,1)} %copy-done.13) | copy-start | bytes 442372
  88.4 15.1 %collective-permute-start.11 = (bf16[768,128]{1,0:T(8,128)(2,1)S(1)}, bf16[768,128]{1,0:T(8,128)(2,1)S(1)}, u32[]{:S(2)}, u32[]{:S(2)}) collective-permute-start(bf16[768,128]{1,0:T(8,128)(2,1)S(1)} %copy-done.25), channel_id=1, source_target_pairs={{4,0},{8,4},{12,8},{16,12},{20,16},{24,20},{28,24},{5,1},{9,5},{13... | collective-permute-start | bytes 589832 | tf_op jit(solution)/shard_map/ppermute | solution.py:352
  93.8 9.6 %collective-permute-start.9 = (bf16[4,128,128]{2,1,0:T(8,128)(2,1)S(1)}, bf16[4,128,128]{2,1,0:T(8,128)(2,1)S(1)}, u32[]{:S(2)}, u32[]{:S(2)}) collective-permute-start(bf16[4,128,128]{2,1,0:T(8,128)(2,1)S(1)} %slice.26), channel_id=1, source_target_pairs={{0,16},{4,20},{8,24},{12,28},{16,0},{20,4},{24,8},{28,12},{1,17},{... | collective-permute-start | bytes 393224 | tf_op jit(solution)/shard_map/ppermute | solution.py:211
  100.0 3.5 %copy-start.4 = (f32[4,128,128]{2,1,0:T(8,128)S(1)}, f32[4,128,128]{2,1,0:T(8,128)}, u32[]{:S(2)}) copy-start(f32[4,128,128]{2,1,0:T(8,128)} %one_ref.3) | copy-start | bytes 786436
  100.0 3.5 %copy-start.6 = (f32[4,128,128]{2,1,0:T(8,128)S(1)}, f32[4,128,128]{2,1,0:T(8,128)}, u32[]{:S(2)}) copy-start(f32[4,128,128]{2,1,0:T(8,128)} %two_ref.3) | copy-start | bytes 786436
  100.0 3.5 %copy-start.20 = (bf16[4,128,128]{2,1,0:T(8,128)(2,1)S(1)}, bf16[4,128,128]{2,1,0:T(8,128)(2,1)}, u32[]{:S(2)}) copy-start(bf16[4,128,128]{2,1,0:T(8,128)(2,1)} %w_ref.3) | copy-start | bytes 393220
Sparse Core Ops, SparseCore 0:
  9.6 56.8 all-gather.2

commit v2 on v1

--- a/solution.py
+++ b/solution.py
@@ -10,7 +10,6 @@
 
 D = 8192
 TILE = 16
-VMEM_LIMIT = 48 * 1024 * 1024
 
 learn_rate = 0.02
 beta_first = 0.9
@@ -21,33 +20,74 @@
 f32 = jnp.float32
 bf16 = jnp.bfloat16
 VMEM = pl.BlockSpec(memory_space=pltpu.VMEM)
+ANY = pl.BlockSpec(memory_space=pl.ANY)
 SMEM = pl.BlockSpec(memory_space=pltpu.SMEM)
 
 
-def params():
-    return pltpu.CompilerParams(vmem_limit_bytes=VMEM_LIMIT)
+def params(mib=32):
+    return pltpu.CompilerParams(vmem_limit_bytes=mib * 1024 * 1024)
 
 
 def lanes(ref, index, width):
     return ref[:, pl.ds(pl.multiple_of(index * width, width), width)]
 
 
-def pack_kernel(row_s, col_s, dest_s, w_ref, one_ref, two_ref, pack_ref, left_ref, right_ref):
+def pack_kernel(row_h, col_h, dest_h, w_h, pack_ref, row_s, col_s, dest_s, w_ref, sems):
+    kept, side = w_ref.shape[0], w_ref.shape[1]
+    pitch = side + TILE
+    copies = [
+        pltpu.make_async_copy(source, target, sems.at[i])
+        for i, (source, target) in enumerate(
+            ((row_h, row_s), (col_h, col_s), (dest_h, dest_s), (w_h, w_ref))
+        )
+    ]
+    for copy in copies:
+        copy.start()
+    for copy in copies:
+        copy.wait()
+    lane = lax.broadcasted_iota(jnp.int32, (TILE, side), 1)
+    for s in range(kept):
+        tile = jnp.where(lane == 0, row_s[s], jnp.where(lane == 1, col_s[s], dest_s[s]))
+        pack_ref[s * pitch : s * pitch + side, :] = w_ref[s]
+        pack_ref[s * pitch + side : (s + 1) * pitch, :] = tile.astype(f32).astype(bf16)
+
+
+def pack(rows, cols, dests, weight):
+    kept, side, _ = weight.shape
+    return pl.pallas_call(
+        pack_kernel,
+        out_shape=jax.ShapeDtypeStruct((kept * (side + TILE), side), bf16),
+        in_specs=[ANY] * 4,
+        out_specs=VMEM,
+        scratch_shapes=[pltpu.SMEM((kept,), jnp.int32)] * 3
+        + [pltpu.VMEM(weight.shape, bf16), pltpu.SemaphoreType.DMA((4,))],
+        compiler_params=params(60),
+        cost_estimate=pl.CostEstimate(flops=0, bytes_accessed=0, transcendentals=0),
+        name="pack_blocks",
+    )(rows, cols, dests, weight)
+
+
+def leave_kernel(dest_h, w_h, one_h, two_h, left_ref, right_ref, dest_s, w_ref, one_ref, two_ref, sems):
     kept, side = w_ref.shape[0], w_ref.shape[1]
     half = kept // 2
     me = lax.axis_index("dp")
-    lane = lax.broadcasted_iota(jnp.int32, (TILE, side), 1)
-    pitch = side + TILE
     travel = 3 * side
+    copies = [
+        pltpu.make_async_copy(source, target, sems.at[i])
+        for i, (source, target) in enumerate(
+            ((dest_h, dest_s), (w_h, w_ref), (one_h, one_ref), (two_h, two_ref))
+        )
+    ]
+    for copy in copies:
+        copy.start()
     left_ref[...] = jnp.zeros_like(left_ref)
     right_ref[...] = jnp.zeros_like(right_ref)
+    for copy in copies:
+        copy.wait()
     to_left = jnp.int32(0)
     to_right = jnp.int32(0)
     for s in range(kept):
         dest = dest_s[s]
-        tile = jnp.where(lane == 0, row_s[s], jnp.where(lane == 1, col_s[s], dest))
-        pack_ref[s * pitch : s * pitch + side, :] = w_ref[s]
-        pack_ref[s * pitch + side : (s + 1) * pitch, :] = tile.astype(f32).astype(bf16)
         goal = jnp.where(dest >= 0, dest // kept, me)
         for ref, count, going in (
             (left_ref, to_left, goal < me),
@@ -65,27 +105,43 @@
         to_right = to_right + (goal > me).astype(jnp.int32)
 
 
-def pack(rows, cols, dests, weight, one, two):
+def leave(dests, weight, one, two):
     kept, side, _ = weight.shape
     travel = jax.ShapeDtypeStruct((kept // 2 * 3 * side, side), bf16)
     return pl.pallas_call(
-        pack_kernel,
-        out_shape=(jax.ShapeDtypeStruct((kept * (side + TILE), side), bf16), travel, travel),
-        in_specs=[SMEM, SMEM, SMEM, VMEM, VMEM, VMEM],
-        out_specs=(VMEM, VMEM, VMEM),
-        compiler_params=params(),
-        name="pack_blocks",
-    )(rows, cols, dests, weight, one, two)
+        leave_kernel,
+        out_shape=(travel, travel),
+        in_specs=[ANY] * 4,
+        out_specs=(VMEM, VMEM),
+        scratch_shapes=[
+            pltpu.SMEM((kept,), jnp.int32),
+            pltpu.VMEM(weight.shape, bf16),
+            pltpu.VMEM(weight.shape, f32),
+            pltpu.VMEM(weight.shape, f32),
+            pltpu.SemaphoreType.DMA((4,)),
+        ],
+        compiler_params=params(8),
+        cost_estimate=pl.CostEstimate(flops=0, bytes_accessed=0, transcendentals=0),
+        name="leaving_blocks",
+    )(dests, weight, one, two)
+
+
+def line_gather(own, axis):
+    n = lax.axis_size(axis)
+    below, above = [own], [own]
+    for step in range(1, n):
+        below.append(lax.ppermute(below[-1], axis, [(i, i + 1) for i in range(step - 1, n - 1)]))
+        above.append(lax.ppermute(above[-1], axis, [(i + 1, i) for i in range(n - step)]))
+    return (*below[1:], *above[1:])
 
 
 def backward_kernel(kept, ids, slices, *refs):
     count = len(ids)
-    packs = refs[:count]
-    up_ref = refs[count]
+    packs, up_ref = refs[:count], refs[count]
     shares = refs[count + 1 : count + 1 + slices]
     meta_ref = refs[count + 1 + slices]
     acc, meta_s, sem = refs[count + 2 + slices :]
-    side = packs[0].shape[1]
+    side = meta_ref.shape[1]
     pitch = side + TILE
     width = shares[0].shape[1]
     for at, ident in enumerate(ids):
@@ -109,10 +165,16 @@
             )
             place = pl.ds(pl.multiple_of(row * side, side), side)
             acc[:, place] = acc[:, place] + part
-    me = lax.axis_index("mp")
-    for k in range(slices):
-        share = lanes(acc, lax.rem(me + k, slices), width) * grad_scale
+    for k, quarter in enumerate(share_order(lax.axis_index("mp"), slices)):
+        share = lanes(acc, quarter, width) * grad_scale
         shares[k][...] = share.astype(shares[k].dtype)
+
+
+def share_order(me, slices):
+    if slices == 4:
+        low = me < 2
+        return (me, jnp.where(low, 3, 0), jnp.where(low, 2, 1), jnp.bitwise_xor(me, 1))
+    return tuple(lax.rem(me + k, slices) for k in range(slices))
 
 
 def backward(packs, ids, upstream, kept, slices, features):
@@ -133,11 +195,7 @@
             pltpu.SemaphoreType.DMA,
         ],
         compiler_params=params(),
-        cost_estimate=pl.CostEstimate(
-            flops=2 * blocks * tokens * side * side,
-            bytes_accessed=24 * 1024 * 1024,
-            transcendentals=0,
-        ),
+        cost_estimate=pl.CostEstimate(flops=0, bytes_accessed=0, transcendentals=0),
         name="input_gradient",
     )(*packs, upstream)
     return outs[:slices], outs[slices]
@@ -158,13 +216,69 @@
     return (shares[0] + right.astype(f32) + left.astype(f32)).astype(bf16)
 
 
-def gradient_kernel(kept, dp, meta_s, x_ref, up_ref, keep_ref, send_ref, store):
+def four_gather(own, axis):
+    inner, outward = [(1, 2), (2, 1)], [(1, 0), (2, 3)]
+    near = lax.ppermute(own, axis, [(0, 1), (1, 0), (2, 3), (3, 2)])
+    middle = lax.ppermute(own, axis, inner)
+    near, middle = lax.optimization_barrier((near, middle))
+    near_on = lax.ppermute(near, axis, inner)
+    middle_on = lax.ppermute(middle, axis, outward)
+    near_on, middle_on = lax.optimization_barrier((near_on, middle_on))
+    last = lax.ppermute(near_on, axis, outward)
+    return near, middle, near_on, middle_on, last
+
+
+def after(value, *others):
+    return lax.optimization_barrier((value, *others))[0]
+
+
+def plus(share, came):
+    return (share.astype(f32) + came.astype(f32)).astype(bf16)
+
+
+def token_copies(slices, own, came, x_ref, sems):
+    me = lax.axis_index("mp")
+    todo = [(None, own, me)]
+    if slices == 4:
+        near, middle, near_on, middle_on, last = came
+        outer = lax.rem(me, 3) == 0
+        todo.append((None, near, jnp.bitwise_xor(me, 1)))
+        todo.append((outer, middle_on, jnp.where(me == 0, 2, 1)))
+        todo.append((outer, last, 3 - me))
+        todo.append((jnp.logical_not(outer), middle, 3 - me))
+        todo.append((jnp.logical_not(outer), near_on, jnp.where(me == 1, 3, 0)))
+    else:
+        for k in range(1, slices):
+            todo.append((me >= k, came[k - 1], jnp.maximum(me - k, 0)))
+            todo.append((me + k < slices, came[slices + k - 2], jnp.minimum(me + k, slices - 1)))
+    return [
+        (when, pltpu.make_async_copy(source, x_ref.at[at], sems.at[i]))
+        for i, (when, source, at) in enumerate(todo)
+    ]
+
+
+def run(when, action):
+    if when is None:
+        action()
+    else:
+        pl.when(when)(action)
+
+
+def gradient_kernel(kept, dp, slices, meta_s, up_h, own_h, *refs):
+    came, (keep_ref, send_ref, x_ref, up_ref, store, sems) = refs[:-6], refs[-6:]
     side = keep_ref.shape[1]
     per = x_ref.shape[2] // side
     blocks = dp * kept
-    bits = dp.bit_length() - 1
     me = lax.axis_index("dp")
+    up_copy = pltpu.make_async_copy(up_h, up_ref, sems.at[len(came) + 1])
+    copies = token_copies(slices, own_h, came, x_ref, sems)
+    up_copy.start()
+    for when, copy in copies:
+        run(when, copy.start)
     store[0:blocks] = jnp.zeros((blocks, side, side), f32)
+    up_copy.wait()
+    for when, copy in copies:
+        run(when, copy.wait)
     for b in range(blocks):
         row, col, dest = meta_s[b, 0], meta_s[b, 1], meta_s[b, 2]
         x = x_ref[row // per, :, pl.ds(pl.multiple_of((row % per) * side, side), side)]
@@ -172,9 +286,7 @@
             x, lanes(up_ref, col, side), (((0,), (0,)), ((), ())), preferred_element_type=f32
         )
         gap = jnp.bitwise_xor(jnp.maximum(dest, 0) // kept, me)
-        place = jnp.int32(0)
-        for bit in range(bits):
-            place = place * 2 + (lax.shift_right_logical(gap, bit) & 1)
+        place = (gap & 1) * (dp // 2) + lax.shift_right_logical(gap, 1)
         slot = jnp.where(dest >= 0, place * kept + jnp.maximum(dest, 0) % kept, blocks)
         store[slot] = grad * grad_scale
     half = keep_ref.shape[0]
@@ -182,49 +294,55 @@
     send_ref[...] = store[half : 2 * half].astype(bf16)
 
 
-def gradient(meta, x_all, upstream, kept, dp):
+def gradient(meta, own, came, upstream, kept, dp, slices):
     side = meta.shape[1]
     blocks = dp * kept
     half = blocks // 2
     return pl.pallas_call(
-        functools.partial(gradient_kernel, kept, dp),
+        functools.partial(gradient_kernel, kept, dp, slices),
         out_shape=(
             jax.ShapeDtypeStruct((half, side, side), f32),
             jax.ShapeDtypeStruct((half, side, side), bf16),
         ),
-        in_specs=[SMEM, VMEM, VMEM],
+        in_specs=[SMEM] + [ANY] * (2 + len(came)),
         out_specs=(VMEM, VMEM),
-        scratch_shapes=[pltpu.VMEM((blocks + 1, side, side), f32)],
+        scratch_shapes=[
+            pltpu.VMEM((slices, *own.shape), bf16),
+            pltpu.VMEM(upstream.shape, bf16),
+            pltpu.VMEM((blocks + 1, side, side), f32),
+            pltpu.SemaphoreType.DMA((len(came) + 2,)),
+        ],
         compiler_params=params(),
-        cost_estimate=pl.CostEstimate(
-            flops=2 * blocks * upstream.shape[0] * side * side,
-            bytes_accessed=16 * 1024 * 1024,
-            transcendentals=0,
-        ),
+        cost_estimate=pl.CostEstimate(flops=0, bytes_accessed=0, transcendentals=0),
         name="weight_gradient",
-    )(meta, x_all, upstream)
-
-
-def halving_reduce(keep, send, dp):
-    step = 1
-    while True:
-        came = lax.ppermute(send, "dp", [(i, i ^ step) for i in range(dp)])
-        step *= 2
-        if step == dp:
-            return keep, came
-        total = keep + came.astype(f32)
-        half = total.shape[0] // 2
-        keep, send = total[:half], total[half:].astype(bf16)
-
-
-def forward_kernel(kept, ids, meta_s, *refs):
+    )(meta, upstream, own, *came)
+
+
+def slot_reduce(keep, send, kept, dp):
+    came = lax.ppermute(send, "dp", [(i, i ^ 1) for i in range(dp)])
+    total = keep + came.astype(f32)
+    totals = [total[:kept]]
+    for gap in range(1, dp // 2):
+        totals.append(total[gap * kept : (gap + 1) * kept].astype(bf16))
+    parts = totals[:1]
+    for gap in range(1, dp // 2):
+        parts.append(lax.ppermute(totals[gap], "dp", [(i, i ^ (2 * gap)) for i in range(dp)]))
+    return parts, totals
+
+
+def forward_kernel(kept, ids, slices, meta_s, *refs):
     count = len(ids)
-    packs = refs[:count]
-    x_ref, out_ref, acc = refs[count:]
+    packs, own_h, came = refs[:count], refs[count], refs[count + 1 : -4]
+    out_ref, x_ref, acc, sems = refs[-4:]
     side = packs[0].shape[1]
     pitch = side + TILE
     per = x_ref.shape[2] // side
+    copies = token_copies(slices, own_h, came, x_ref, sems)
+    for when, copy in copies:
+        run(when, copy.start)
     acc[...] = jnp.zeros_like(acc)
+    for when, copy in copies:
+        run(when, copy.wait)
     for at, ident in enumerate(ids):
         for s in range(kept):
             row = meta_s[ident * kept + s, 0]
@@ -238,29 +356,29 @@
     out_ref[...] = (acc[...] * grad_scale).astype(bf16)
 
 
-def forward(meta, packs, ids, x_all, kept, hidden):
-    tokens = x_all.shape[1]
+def forward(meta, packs, ids, own, came, kept, slices, hidden):
+    tokens = own.shape[0]
     side = meta.shape[1]
     return pl.pallas_call(
-        functools.partial(forward_kernel, kept, ids),
+        functools.partial(forward_kernel, kept, ids, slices),
         out_shape=jax.ShapeDtypeStruct((tokens, hidden), bf16),
-        in_specs=[SMEM] + [VMEM] * (len(ids) + 1),
+        in_specs=[SMEM] + [VMEM] * len(ids) + [ANY] * (1 + len(came)),
         out_specs=VMEM,
-        scratch_shapes=[pltpu.VMEM((tokens, hidden), f32)],
+        scratch_shapes=[
+            pltpu.VMEM((slices, *own.shape), bf16),
+            pltpu.VMEM((tokens, hidden), f32),
+            pltpu.SemaphoreType.DMA((len(came) + 1,)),
+        ],
         compiler_params=params(),
-        cost_estimate=pl.CostEstimate(
-            flops=2 * len(ids) * kept * tokens * side * side,
-            bytes_accessed=24 * 1024 * 1024,
-            transcendentals=0,
-        ),
+        cost_estimate=pl.CostEstimate(flops=0, bytes_accessed=0, transcendentals=0),
         name="hidden_out",
-    )(meta, *packs, x_all)
+    )(meta, *packs, own, *came)
 
 
 def update_kernel(
-    dp, meta_s, keep_ref, came_ref, w_ref, one_ref, two_ref, left_ref, right_ref,
-    new_w, new_one, new_two,
+    dp, meta_s, w_ref, one_ref, two_ref, left_ref, right_ref, *refs
 ):
+    parts, (new_w, new_one, new_two) = refs[:-3], refs[-3:]
     kept, side = w_ref.shape[0], w_ref.shape[1]
     travel = 3 * side
     me = lax.axis_index("dp")
@@ -284,7 +402,9 @@
     for q in range(kept):
 
         def write(weight, one, two, q=q):
-            grad = keep_ref[q] + came_ref[q].astype(f32)
+            grad = parts[0][q]
+            for part in parts[1:]:
+                grad = grad + part[q].astype(f32)
             first = beta_first * one + (1.0 - beta_first) * grad
             second = beta_second * two + (1.0 - beta_second) * grad * grad
             stepped = weight - learn_rate * first / (jnp.sqrt(second) + epsilon)
@@ -316,7 +436,7 @@
                 )
 
 
-def update(meta, keep, came, weight, one, two, from_left, from_right, dp):
+def update(meta, parts, weight, one, two, from_left, from_right, dp):
     shape = weight.shape
     return pl.pallas_call(
         functools.partial(update_kernel, dp),
@@ -325,22 +445,21 @@
             jax.ShapeDtypeStruct(shape, f32),
             jax.ShapeDtypeStruct(shape, f32),
         ),
-        in_specs=[SMEM] + [VMEM] * 7,
+        in_specs=[SMEM] + [VMEM] * (5 + len(parts)),
         out_specs=(VMEM,) * 3,
         compiler_params=params(),
+        cost_estimate=pl.CostEstimate(flops=0, bytes_accessed=0, transcendentals=0),
         name="adam_update",
-    )(meta, keep, came, weight, one, two, from_left, from_right)
+    )(meta, weight, one, two, from_left, from_right, *parts)
 
 
 def body(weight, moment_one, moment_two, block_row, block_col, dest_slot, tokens, upstream):
     kept = weight.shape[0]
     dp = lax.axis_size("dp")
     slices = lax.axis_size("mp")
-    x_all = lax.all_gather(tokens, "mp", axis=0)
-    packed, to_left, to_right = pack(
-        block_row, block_col, dest_slot, weight, moment_one, moment_two
-    )
-    packs, ids = [packed], [0]
+    four = slices == 4
+    came = four_gather(tokens, "mp") if four else line_gather(tokens, "mp")
+    packs, ids = [pack(block_row, block_col, dest_slot, weight)], [0]
     bit = dp // 2
     while bit:
         packs = packs + [
@@ -348,16 +467,46 @@
         ]
         ids = ids + [i ^ bit for i in ids]
         bit //= 2
+    ids = tuple(ids)
+    if four:
+        packs[-1] = after(packs[-1], came[0], came[1])
+    shares, meta = backward(packs, ids, upstream, kept, slices, tokens.shape[1])
+    if four:
+        own, far, second, near = shares
+        ends, inner = [(0, 1), (3, 2)], [(1, 2), (2, 1)]
+        came_far = lax.ppermute(far, "mp", ends)
+        dest_leave = after(dest_slot, meta, came[2])
+    else:
+        dest_leave = dest_slot
+    to_left, to_right = leave(dest_leave, weight, moment_one, moment_two)
     from_left = lax.ppermute(to_right, "dp", [(i, i + 1) for i in range(dp - 1)])
     from_right = lax.ppermute(to_left, "dp", [(i + 1, i) for i in range(dp - 1)])
-    ids = tuple(ids)
-    shares, meta = backward(packs, ids, upstream, kept, slices, tokens.shape[1])
-    input_grad = line_reduce(shares, "mp")
-    keep, send = gradient(meta, x_all, upstream, kept, dp)
-    hidden_out = forward(meta, packs, ids, x_all, kept, upstream.shape[1])
-    keep, came = halving_reduce(keep, send, dp)
+    if four:
+        sum_far = plus(after(far, from_left, from_right), came_far)
+        passed_far = lax.ppermute(sum_far, "mp", inner)
+        came_second = lax.ppermute(after(second, sum_far), "mp", ends)
+        meta_grad = after(meta, sum_far)
+    else:
+        meta_grad = meta
+    keep, send = gradient(meta_grad, tokens, came, upstream, kept, dp, slices)
+    parts, totals = slot_reduce(keep, send, kept, dp)
+    if four:
+        passed_far, came_second = lax.optimization_barrier((passed_far, came_second))
+        sum_second = plus(after(second, *totals), came_second)
+        sum_near = plus(near, passed_far)
+        sum_second, sum_near = lax.optimization_barrier((sum_second, sum_near))
+        passed_second = lax.ppermute(sum_second, "mp", inner)
+        came_near = lax.ppermute(sum_near, "mp", ends + [(1, 0), (2, 3)])
+        meta_out = after(meta, sum_second, sum_near)
+        input_grad = (own + came_near.astype(f32) + passed_second.astype(f32)).astype(bf16)
+    else:
+        meta_out = meta
+        input_grad = line_reduce(shares, "mp")
+    hidden_out = forward(
+        meta_out, packs, ids, tokens, came, kept, slices, upstream.shape[1]
+    )
     new_weight, new_first, new_second = update(
-        meta, keep, came, weight, moment_one, moment_two, from_left, from_right, dp
+        meta, parts, weight, moment_one, moment_two, from_left, from_right, dp
     )
     return (new_weight, new_first, new_second, hidden_out, input_grad)
 

time: 113 us -> 83.1 us (0.74)
  waiting for transfers between devices: 43.7 us -> 25.4 us
  between operations: 14.4 us -> 0.87 us
  starting transfers between devices: 29.8 us -> 38.9 us
  local copies, waits for them, and re-layouts: 9.38 us -> 2.48 us
  other arithmetic: 4.76 us -> 1.68 us
  Pallas kernels: 10.4 us -> 12.7 us
    ppermute x9 -> x14, waiting for transfers between devices: 36.4 us -> 14.5 us  [the longest x1 6.64 us: body(): came_second = lax.ppermute(after(second, sum_far), 'mp', ends)]
    ppermute x9 -> x14, starting transfers between devices: 20.3 us -> 31.1 us  [the longest x1 7.88 us: body(): came_far = lax.ppermute(far, 'mp', ends)]
    unnamed x56 -> x16, local copies, waits for them, and re-layouts: 9.3 us -> 2.43 us
    convert_element_type x4 -> x3, other arithmetic: 4.6 us -> 1.5 us  [the longest x1 0.98 us: body(): (own + came_near.astype(f32) + passed_second.astype(f32)).astype(bf16)]
    ppermute x7, waiting for transfers between devices: 6.6 us -> 9.02 us  [body(): lax.ppermute(p, 'dp', [(i, i ^ bit) for i in range(dp)])]
    pallas_call x3 -> x4, Pallas kernels: 6.03 us -> 8.32 us  [the longest x1 3.63 us: forward(): pl.pallas_call(functools.partial(forward_kernel, kept, ids, slices), out_...]
    ppermute x7, starting transfers between devices: 6.69 us -> 4.68 us  [body(): lax.ppermute(p, 'dp', [(i, i ^ bit) for i in range(dp)])]
    ppermute x1, waiting for transfers between devices: 0.01 us -> 1.89 us  [body(): lax.ppermute(to_left, 'dp', [(i + 1, i) for i in range(dp - 1)])]
  transfers between devices with their start and end apart: 19 -> 23, of which waited for: 7 -> 12; matrix products, arithmetic and copies ran while one was open for 4% -> 0% of each run, Pallas kernels for 7% -> 15%
where the time goes in v2:
time: 83.1 us; the launch traced here: 82.1 us
  starting transfers between devices  38.9 us (47%)
  waiting for transfers between devices  25.4 us (31%)
  Pallas kernels  12.7 us (15%)
  local copies, waits for them, and re-layouts  2.48 us (3%)
  other arithmetic  1.68 us (2%)
  between operations  0.87 us (1%)
    ppermute x7, waiting for transfers between devices, body(): lax.ppermute(p, 'dp', [(i, i ^ bit) for i in range(dp)])  9.02 us
    ppermute x1, starting transfers between devices, body(): came_far = lax.ppermute(far, 'mp', ends)  7.88 us
    ppermute x1, starting transfers between devices, body(): came_second = lax.ppermute(after(second, sum_far), 'mp', ends)  6.9 us
    ppermute x1, waiting for transfers between devices, body(): came_second = lax.ppermute(after(second, sum_far), 'mp', ends)  6.64 us
    ppermute x7, starting transfers between devices, body(): lax.ppermute(p, 'dp', [(i, i ^ bit) for i in range(dp)])  4.68 us
    pallas_call x1, Pallas kernels, forward(): pl.pallas_call(functools.partial(forward_kernel, kept, ids, slices), out_...  3.63 us
    ppermute x3, starting transfers between devices, slot_reduce(): lax.ppermute(totals[gap], 'dp', [(i, i ^ 2 * gap) for i in range(dp)])  3.55 us
    ppermute x1, waiting for transfers between devices, body(): came_far = lax.ppermute(far, 'mp', ends)  3.38 us
  transfers between devices with their start and end apart: 23, of which 12 were waited for; matrix products, arithmetic and copies ran while one was open for 0% of the time, Pallas kernels for 15%

profile of v2, /device:TPU:0, one launch (start us, length us, event | category | flops | bytes accessed | tf_op | source)
XLA Modules:
  0.0 82.1 jit_solution(9798763957225037939)
XLA Ops:
  0.6 0.0 copy-start.7
  0.6 0.0 copy-start.4
  0.7 3.1 %collective-permute-start.7 = (bf16[128,2048]{1,0:T(8,128)(2,1)}, bf16[128,2048]{1,0:T(8,128)(2,1)S(1)}, u32[]{:S(2)}, u32[]{:S(2)}) collective-permute-start(bf16[128,2048]{1,0:T(8,128)(2,1)} %refs_8_.3), channel_id=1, source_target_pairs={{0,1},{1,0},{2,3},{3,2},{4,5},{5,4},{6,7},{7,6},{8,9},{9,8},{10,11... | collective-permute-start | bytes 1572872 | tf_op jit(solution)/shard_map/ppermute | solution.py:221
  3.7 0.7 collective-permute-start.8
  4.4 1.6 %pack_blocks.1.refs_0_ = bf16[576,128]{1,0:T(8,128)(2,1)} custom-call(s32[4]{0:T(128)} %row_h.1, s32[4]{0:T(128)} %col_h.1, s32[4]{0:T(128)} %dest_h.2, bf16[4,128,128]{2,1,0:T(8,128)(2,1)} %w_ref.1), custom_call_target="tpu_custom_call" | custom-call | tf_op jit(solution)/shard_map/pack_blocks/pallas_call | solution.py:57
  6.1 1.6 %collective-permute-start = (bf16[576,128]{1,0:T(8,128)(2,1)}, bf16[576,128]{1,0:T(8,128)(2,1)S(1)}, u32[]{:S(2)}, u32[]{:S(2)}) collective-permute-start(bf16[576,128]{1,0:T(8,128)(2,1)} %pack_blocks.1.refs_0_), channel_id=1, source_target_pairs={{0,16},{4,20},{8,24},{12,28},{16,0},{20,4},{24,8},{28,12},{1,17},{... | collective-permute-start | bytes 442376 | tf_op jit(solution)/shard_map/ppermute | solution.py:466
  7.6 4.0 %collective-permute-done.refs_1_ = bf16[576,128]{1,0:T(8,128)(2,1)S(1)} collective-permute-done((bf16[576,128]{1,0:T(8,128)(2,1)}, bf16[576,128]{1,0:T(8,128)(2,1)S(1)}, u32[]{:S(2)}, u32[]{:S(2)}) %collective-permute-start) | collective-permute-done | bytes 147488 | tf_op jit(solution)/shard_map/ppermute | solution.py:466
  11.6 1.5 %collective-permute-start.2 = (bf16[576,128]{1,0:T(8,128)(2,1)S(1)}, bf16[576,128]{1,0:T(8,128)(2,1)S(1)}, u32[]{:S(2)}, u32[]{:S(2)}) collective-permute-start(bf16[576,128]{1,0:T(8,128)(2,1)S(1)} %collective-permute-done.refs_1_), channel_id=1, source_target_pairs={{0,8},{4,12},{8,0},{12,4},{16,24},{20,28},{24,16},{28,20},{1,9},{5... | collective-permute-start | bytes 442376 | tf_op jit(solution)/shard_map/ppermute | solution.py:466
  13.1 0.5 collective-permute-start.1
  13.7 4.0 %collective-permute-done.2.refs_3_ = bf16[576,128]{1,0:T(8,128)(2,1)S(1)} collective-permute-done((bf16[576,128]{1,0:T(8,128)(2,1)S(1)}, bf16[576,128]{1,0:T(8,128)(2,1)S(1)}, u32[]{:S(2)}, u32[]{:S(2)}) %collective-permute-start.2) | collective-permute-done | bytes 147488 | tf_op jit(solution)/shard_map/ppermute | solution.py:466
  17.6 0.0 collective-permute-start.6
  17.6 0.0 collective-permute-done.7.refs_0_.refs_9_
  17.6 0.0 collective-permute-done.8.refs_1_.refs_10_
  17.6 1.3 %collective-permute-start.10 = (bf16[128,2048]{1,0:T(8,128)(2,1)S(1)}, bf16[128,2048]{1,0:T(8,128)(2,1)S(1)}, u32[]{:S(2)}, u32[]{:S(2)}) collective-permute-start(bf16[128,2048]{1,0:T(8,128)(2,1)S(1)} %collective-permute-done.8.refs_1_.refs_10_), channel_id=1, source_target_pairs={{1,0},{2,3},{5,4},{6,7},{9,8},{10,11},{13,12},{14,15},{17,16},{18,... | collective-permute-start | bytes 1572872 | tf_op jit(solution)/shard_map/ppermute | solution.py:225
  18.9 0.7 collective-permute-start.9
  19.6 0.6 collective-permute-start.3
  20.2 0.0 collective-permute-done.1.refs_2_
  20.2 0.1 collective-permute-start.4
  20.3 0.0 collective-permute-done.6.refs_7_
  20.3 0.4 collective-permute-start.5
  20.7 0.7 collective-permute-done.3.refs_4_
  21.4 0.2 collective-permute-done.4.refs_5_
  21.6 0.2 collective-permute-done.5.refs_6_
  21.8 1.5 %copy-done = bf16[128,7168]{1,0:T(8,128)(2,1)S(1)} copy-done((bf16[128,7168]{1,0:T(8,128)(2,1)S(1)}, bf16[128,7168]{1,0:T(8,128)(2,1)}, u32[]{:S(2)}) %copy-start) | copy-done | bytes 1835032
  23.3 0.9 %copy-done.3 = bf16[576,128]{1,0:T(8,128)(2,1)S(1)} copy-done((bf16[576,128]{1,0:T(8,128)(2,1)S(1)}, bf16[576,128]{1,0:T(8,128)(2,1)}, u32[]{:S(2)}) %copy-start.3) | copy-done | bytes 147480
  24.2 2.3 %input_gradient.1 = (f32[128,2048]{1,0:T(8,128)S(1)}, bf16[128,2048]{1,0:T(8,128)(2,1)S(1)}, bf16[128,2048]{1,0:T(8,128)(2,1)S(1)}, bf16[128,2048]{1,0:T(8,128)(2,1)S(1)}, s32[32,128]{1,0:T(8,128)S(1)}) custom-call(bf16[576,128]{1,0:T(8,128)(2,1)S(1)} %copy-done.3, bf16[576,128]{1,0:T(8,128)(2,1)S(1)} %collective-permute-done.refs_1_, ...), custom_call_target="tpu_custom_call" | custom-call | tf_op jit(solution)/shard_map/input_gradient/pallas_call | solution.py:187
  26.5 0.0 copy-start.1
  26.5 7.9 %collective-permute-start.13 = (bf16[128,2048]{1,0:T(8,128)(2,1)S(1)}, bf16[128,2048]{1,0:T(8,128)(2,1)S(1)}, u32[]{:S(2)}, u32[]{:S(2)}) collective-permute-start(bf16[128,2048]{1,0:T(8,128)(2,1)S(1)} %get-tuple-element.41), channel_id=1, source_target_pairs={{0,1},{3,2},{4,5},{7,6},{8,9},{11,10},{12,13},{15,14},{16,17},{19,... | collective-permute-start | bytes 1572872 | tf_op jit(solution)/shard_map/ppermute | solution.py:477
  34.4 1.0 %collective-permute-done.10.refs_3_.refs_12_ = bf16[128,2048]{1,0:T(8,128)(2,1)S(1)} collective-permute-done((bf16[128,2048]{1,0:T(8,128)(2,1)S(1)}, bf16[128,2048]{1,0:T(8,128)(2,1)S(1)}, u32[]{:S(2)}, u32[]{:S(2)}) %collective-permute-start.10) | collective-permute-done | bytes 524320 | tf_op jit(solution)/shard_map/ppermute | solution.py:225
  35.5 0.0 collective-permute-done.9.refs_2_.refs_11_
  35.5 0.0 copy-done.7
  35.5 0.0 copy-done.4
  35.5 0.0 copy-done.5
  35.5 0.7 leaving_blocks.1
  36.2 1.8 %collective-permute-start.11 = (bf16[768,128]{1,0:T(8,128)(2,1)S(1)}, bf16[768,128]{1,0:T(8,128)(2,1)S(1)}, u32[]{:S(2)}, u32[]{:S(2)}) collective-permute-start(bf16[768,128]{1,0:T(8,128)(2,1)S(1)} %get-tuple-element.38), channel_id=1, source_target_pairs={{0,4},{4,8},{8,12},{12,16},{16,20},{20,24},{24,28},{1,5},{5,9},{9,... | collective-permute-start | bytes 589832 | tf_op jit(solution)/shard_map/ppermute | solution.py:482
  38.0 1.3 %collective-permute-start.12 = (bf16[768,128]{1,0:T(8,128)(2,1)S(1)}, bf16[768,128]{1,0:T(8,128)(2,1)S(1)}, u32[]{:S(2)}, u32[]{:S(2)}) collective-permute-start(bf16[768,128]{1,0:T(8,128)(2,1)S(1)} %get-tuple-element.39), channel_id=1, source_target_pairs={{4,0},{8,4},{12,8},{16,12},{20,16},{24,20},{28,24},{5,1},{9,5},{13... | collective-permute-start | bytes 589832 | tf_op jit(solution)/shard_map/ppermute | solution.py:483
  39.3 1.3 %collective-permute-start.14 = (bf16[128,2048]{1,0:T(8,128)(2,1)S(1)}, bf16[128,2048]{1,0:T(8,128)(2,1)S(1)}, u32[]{:S(2)}, u32[]{:S(2)}) collective-permute-start(bf16[128,2048]{1,0:T(8,128)(2,1)S(1)} %collective-permute-done.9.refs_2_.refs_11_), channel_id=1, source_target_pairs={{1,0},{2,3},{5,4},{6,7},{9,8},{10,11},{13,12},{14,15},{17,16},{18,... | collective-permute-start | bytes 1572872 | tf_op jit(solution)/shard_map/ppermute | solution.py:227
  40.6 0.0 collective-permute-done.11.left_ref
  40.7 1.9 %collective-permute-done.12.right_ref = bf16[768,128]{1,0:T(8,128)(2,1)S(1)} collective-permute-done((bf16[768,128]{1,0:T(8,128)(2,1)S(1)}, bf16[768,128]{1,0:T(8,128)(2,1)S(1)}, u32[]{:S(2)}, u32[]{:S(2)}) %collective-permute-start.12) | collective-permute-done | bytes 196640 | tf_op jit(solution)/shard_map/ppermute | solution.py:483
  42.5 3.4 %collective-permute-done.13 = bf16[128,2048]{1,0:T(8,128)(2,1)S(1)} collective-permute-done((bf16[128,2048]{1,0:T(8,128)(2,1)S(1)}, bf16[128,2048]{1,0:T(8,128)(2,1)S(1)}, u32[]{:S(2)}, u32[]{:S(2)}) %collective-permute-start.13) | collective-permute-done | bytes 524320 | tf_op jit(solution)/shard_map/ppermute | solution.py:477
  45.9 0.1 add_convert_fusion.3
  46.1 0.7 collective-permute-start.19
  46.8 6.9 %collective-permute-start.20 = (bf16[128,2048]{1,0:T(8,128)(2,1)S(1)}, bf16[128,2048]{1,0:T(8,128)(2,1)S(1)}, u32[]{:S(2)}, u32[]{:S(2)}) collective-permute-start(bf16[128,2048]{1,0:T(8,128)(2,1)S(1)} %get-tuple-element.50), channel_id=1, source_target_pairs={{0,1},{3,2},{4,5},{7,6},{8,9},{11,10},{12,13},{15,14},{16,17},{19,... | collective-permute-start | bytes 1572872 | tf_op jit(solution)/shard_map/ppermute | solution.py:487
  53.7 1.3 %collective-permute-done.14.refs_4_.refs_13_ = bf16[128,2048]{1,0:T(8,128)(2,1)S(1)} collective-permute-done((bf16[128,2048]{1,0:T(8,128)(2,1)S(1)}, bf16[128,2048]{1,0:T(8,128)(2,1)S(1)}, u32[]{:S(2)}, u32[]{:S(2)}) %collective-permute-start.14) | collective-permute-done | bytes 524320 | tf_op jit(solution)/shard_map/ppermute | solution.py:227
  55.0 2.4 %weight_gradient.1 = (f32[16,128,128]{2,1,0:T(8,128)S(1)}, bf16[16,128,128]{2,1,0:T(8,128)(2,1)S(1)}) custom-call(s32[32,128]{1,0:T(8,128)S(1)} %get-tuple-element.57.meta_s, bf16[128,7168]{1,0:T(8,128)(2,1)S(1)} %copy-done.1, bf16[128,2048]{1,0:T(8,128)(2,1)S(1)} %copy-done.2, bf16[128,2048]{1,0:T(8,128)(2,1)S(1)} %collective-permute-done.7.refs_0_.refs_9_, ...), custom_call_target="tpu_custom_call" | custom-call | tf_op jit(solution)/shard_map/weight_gradient/pallas_call | solution.py:301
  57.4 1.8 %collective-permute-start.15 = (bf16[16,128,128]{2,1,0:T(8,128)(2,1)S(1)}, bf16[16,128,128]{2,1,0:T(8,128)(2,1)S(1)}, u32[]{:S(2)}, u32[]{:S(2)}) collective-permute-start(bf16[16,128,128]{2,1,0:T(8,128)(2,1)S(1)} %get-tuple-element.45), channel_id=1, source_target_pairs={{0,4},{4,0},{8,12},{12,8},{16,20},{20,16},{24,28},{28,24},{1,5},{5... | collective-permute-start | bytes 1572872 | tf_op jit(solution)/shard_map/ppermute | solution.py:322
  59.2 6.6 %collective-permute-done.20 = bf16[128,2048]{1,0:T(8,128)(2,1)S(1)} collective-permute-done((bf16[128,2048]{1,0:T(8,128)(2,1)S(1)}, bf16[128,2048]{1,0:T(8,128)(2,1)S(1)}, u32[]{:S(2)}, u32[]{:S(2)}) %collective-permute-start.20) | collective-permute-done | bytes 524320 | tf_op jit(solution)/shard_map/ppermute | solution.py:487
  65.8 0.0 collective-permute-done.19
  65.8 0.0 collective-permute-done.15
  65.8 0.2 fusion
  66.1 0.4 add_convert_fusion.1
  66.5 2.5 %collective-permute-start.21 = (bf16[128,2048]{1,0:T(8,128)(2,1)S(1)}, bf16[128,2048]{1,0:T(8,128)(2,1)S(1)}, u32[]{:S(2)}, u32[]{:S(2)}) collective-permute-start(bf16[128,2048]{1,0:T(8,128)(2,1)S(1)} %get-tuple-element.56), channel_id=1, source_target_pairs={{0,1},{3,2},{1,0},{2,3},{4,5},{7,6},{5,4},{6,7},{8,9},{11,10},{9,8... | collective-permute-start | bytes 1572872 | tf_op jit(solution)/shard_map/ppermute | solution.py:499
  69.0 0.7 collective-permute-start.22
  69.7 1.0 %collective-permute-start.16 = (bf16[4,128,128]{2,1,0:T(8,128)(2,1)S(1)}, bf16[4,128,128]{2,1,0:T(8,128)(2,1)S(1)}, u32[]{:S(2)}, u32[]{:S(2)}) collective-permute-start(bf16[4,128,128]{2,1,0:T(8,128)(2,1)S(1)} %get-tuple-element.63), channel_id=1, source_target_pairs={{0,8},{4,12},{8,0},{12,4},{16,24},{20,28},{24,16},{28,20},{1,9},{5... | collective-permute-start | bytes 393224 | tf_op jit(solution)/shard_map/ppermute | solution.py:329
  70.7 0.7 collective-permute-start.17
  71.4 1.9 %collective-permute-start.18 = (bf16[4,128,128]{2,1,0:T(8,128)(2,1)S(1)}, bf16[4,128,128]{2,1,0:T(8,128)(2,1)S(1)}, u32[]{:S(2)}, u32[]{:S(2)}) collective-permute-start(bf16[4,128,128]{2,1,0:T(8,128)(2,1)S(1)} %get-tuple-element.61), channel_id=1, source_target_pairs={{0,24},{4,28},{8,16},{12,20},{16,8},{20,12},{24,0},{28,4},{1,25},{... | collective-permute-start | bytes 393224 | tf_op jit(solution)/shard_map/ppermute | solution.py:329
  73.3 3.6 %hidden_out.1 = bf16[128,7168]{1,0:T(8,128)(2,1)} custom-call(s32[32,128]{1,0:T(8,128)S(1)} %get-tuple-element.57.meta_s, bf16[576,128]{1,0:T(8,128)(2,1)S(1)} %copy-done.3, bf16[576,128]{1,0:T(8,128)(2,1)S(1)} %collective-permute-done.refs_1_, bf16[576,128]{1,0:T(8,128)(2,1)S(1)} %collective-permute-done.1.refs_2_, ...), custom_call_target="tpu_custom_call" | custom-call | tf_op jit(solution)/shard_map/hidden_out/pallas_call | solution.py:362
  76.9 0.0 collective-permute-done.16.refs_1_
  76.9 2.0 %collective-permute-done.17.refs_2_ = bf16[4,128,128]{2,1,0:T(8,128)(2,1)S(1)} collective-permute-done((bf16[4,128,128]{2,1,0:T(8,128)(2,1)S(1)}, bf16[4,128,128]{2,1,0:T(8,128)(2,1)S(1)}, u32[]{:S(2)}, u32[]{:S(2)}) %collective-permute-start.17) | collective-permute-done | bytes 131104 | tf_op jit(solution)/shard_map/ppermute | solution.py:329
  78.9 0.0 collective-permute-done.18.refs_3_
  78.9 2.0 %adam_update.1 = (bf16[4,128,128]{2,1,0:T(8,128)(2,1)}, f32[4,128,128]{2,1,0:T(8,128)}, f32[4,128,128]{2,1,0:T(8,128)}) custom-call(s32[32,128]{1,0:T(8,128)S(1)} %get-tuple-element.57.meta_s, bf16[4,128,128]{2,1,0:T(8,128)(2,1)S(1)} %copy-done.4, f32[4,128,128]{2,1,0:T(8,128)S(1)} %copy-done.5, f32[4,128,128]{2,1,0:T(8,128)S(1)} %copy-done.6, ...), custom_call_target="tpu_custom_call" | custom-call | tf_op jit(solution)/shard_map/adam_update/pallas_call | solution.py:441
  80.9 0.1 collective-permute-done.21
  81.1 0.0 collective-permute-done.22
  81.1 1.0 %add_convert_fusion = bf16[128,2048]{1,0:T(8,128)(2,1)} fusion(bf16[128,2048]{1,0:T(8,128)(2,1)S(1)} %collective-permute-done.22, f32[128,2048]{1,0:T(8,128)S(1)} %get-tuple-element.58, bf16[128,2048]{1,0:T(8,128)(2,1)S(1)} %collective-permute-done.21), kind=kLoop, calls=%fused_computation | loop fusion | flops 1310720 | bytes 2621440 | tf_op jit(solution)/shard_map/convert_element_type | solution.py:501
  (10 shorter events, 0.1 us)
Async XLA Ops:
  0.6 34.8 %copy-start.7 = (s32[4]{0:T(128)S(1)}, s32[4]{0:T(128)}, u32[]{:S(2)}) copy-start(s32[4]{0:T(128)} %dest_h.2) | copy-start | bytes 52
  0.6 34.8 %copy-start.4 = (bf16[4,128,128]{2,1,0:T(8,128)(2,1)S(1)}, bf16[4,128,128]{2,1,0:T(8,128)(2,1)}, u32[]{:S(2)}) copy-start(bf16[4,128,128]{2,1,0:T(8,128)(2,1)} %w_ref.1) | copy-start | bytes 393220
  0.7 17.0 %collective-permute-start.7 = (bf16[128,2048]{1,0:T(8,128)(2,1)}, bf16[128,2048]{1,0:T(8,128)(2,1)S(1)}, u32[]{:S(2)}, u32[]{:S(2)}) collective-permute-start(bf16[128,2048]{1,0:T(8,128)(2,1)} %refs_8_.3), channel_id=1, source_target_pairs={{0,1},{1,0},{2,3},{3,2},{4,5},{5,4},{6,7},{7,6},{8,9},{9,8},{10,11... | collective-permute-start | bytes 1572872 | tf_op jit(solution)/shard_map/ppermute | solution.py:221
  3.7 13.9 %collective-permute-start.8 = (bf16[128,2048]{1,0:T(8,128)(2,1)}, bf16[128,2048]{1,0:T(8,128)(2,1)S(1)}, u32[]{:S(2)}, u32[]{:S(2)}) collective-permute-start(bf16[128,2048]{1,0:T(8,128)(2,1)} %refs_8_.3), channel_id=1, source_target_pairs={{1,2},{2,1},{5,6},{6,5},{9,10},{10,9},{13,14},{14,13},{17,18},{18,... | collective-permute-start | bytes 1572872 | tf_op jit(solution)/shard_map/ppermute | solution.py:222
  6.1 5.6 %collective-permute-start = (bf16[576,128]{1,0:T(8,128)(2,1)}, bf16[576,128]{1,0:T(8,128)(2,1)S(1)}, u32[]{:S(2)}, u32[]{:S(2)}) collective-permute-start(bf16[576,128]{1,0:T(8,128)(2,1)} %pack_blocks.1.refs_0_), channel_id=1, source_target_pairs={{0,16},{4,20},{8,24},{12,28},{16,0},{20,4},{24,8},{28,12},{1,17},{... | collective-permute-start | bytes 442376 | tf_op jit(solution)/shard_map/ppermute | solution.py:466
  11.6 6.0 %collective-permute-start.2 = (bf16[576,128]{1,0:T(8,128)(2,1)S(1)}, bf16[576,128]{1,0:T(8,128)(2,1)S(1)}, u32[]{:S(2)}, u32[]{:S(2)}) collective-permute-start(bf16[576,128]{1,0:T(8,128)(2,1)S(1)} %collective-permute-done.refs_1_), channel_id=1, source_target_pairs={{0,8},{4,12},{8,0},{12,4},{16,24},{20,28},{24,16},{28,20},{1,9},{5... | collective-permute-start | bytes 442376 | tf_op jit(solution)/shard_map/ppermute | solution.py:466
  13.1 7.1 %collective-permute-start.1 = (bf16[576,128]{1,0:T(8,128)(2,1)}, bf16[576,128]{1,0:T(8,128)(2,1)S(1)}, u32[]{:S(2)}, u32[]{:S(2)}) collective-permute-start(bf16[576,128]{1,0:T(8,128)(2,1)} %pack_blocks.1.refs_0_), channel_id=1, source_target_pairs={{0,8},{4,12},{8,0},{12,4},{16,24},{20,28},{24,16},{28,20},{1,9},{5... | collective-permute-start | bytes 442376 | tf_op jit(solution)/shard_map/ppermute | solution.py:466
  17.6 2.7 %collective-permute-start.6 = (bf16[576,128]{1,0:T(8,128)(2,1)S(1)}, bf16[576,128]{1,0:T(8,128)(2,1)S(1)}, u32[]{:S(2)}, u32[]{:S(2)}) collective-permute-start(bf16[576,128]{1,0:T(8,128)(2,1)S(1)} %collective-permute-done.2.refs_3_), channel_id=1, source_target_pairs={{0,4},{4,0},{8,12},{12,8},{16,20},{20,16},{24,28},{28,24},{1,5},{5... | collective-permute-start | bytes 442376 | tf_op jit(solution)/shard_map/ppermute | solution.py:466
  17.6 17.8 %collective-permute-start.10 = (bf16[128,2048]{1,0:T(8,128)(2,1)S(1)}, bf16[128,2048]{1,0:T(8,128)(2,1)S(1)}, u32[]{:S(2)}, u32[]{:S(2)}) collective-permute-start(bf16[128,2048]{1,0:T(8,128)(2,1)S(1)} %collective-permute-done.8.refs_1_.refs_10_), channel_id=1, source_target_pairs={{1,0},{2,3},{5,4},{6,7},{9,8},{10,11},{13,12},{14,15},{17,16},{18,... | collective-permute-start | bytes 1572872 | tf_op jit(solution)/shard_map/ppermute | solution.py:225
  18.9 16.5 %collective-permute-start.9 = (bf16[128,2048]{1,0:T(8,128)(2,1)S(1)}, bf16[128,2048]{1,0:T(8,128)(2,1)S(1)}, u32[]{:S(2)}, u32[]{:S(2)}) collective-permute-start(bf16[128,2048]{1,0:T(8,128)(2,1)S(1)} %collective-permute-done.7.refs_0_.refs_9_), channel_id=1, source_target_pairs={{1,2},{2,1},{5,6},{6,5},{9,10},{10,9},{13,14},{14,13},{17,18},{18,... | collective-permute-start | bytes 1572872 | tf_op jit(solution)/shard_map/ppermute | solution.py:224
  19.6 1.8 %collective-permute-start.3 = (bf16[576,128]{1,0:T(8,128)(2,1)}, bf16[576,128]{1,0:T(8,128)(2,1)S(1)}, u32[]{:S(2)}, u32[]{:S(2)}) collective-permute-start(bf16[576,128]{1,0:T(8,128)(2,1)} %pack_blocks.1.refs_0_), channel_id=1, source_target_pairs={{0,4},{4,0},{8,12},{12,8},{16,20},{20,16},{24,28},{28,24},{1,5},{5... | collective-permute-start | bytes 442376 | tf_op jit(solution)/shard_map/ppermute | solution.py:466
  20.2 1.4 %collective-permute-start.4 = (bf16[576,128]{1,0:T(8,128)(2,1)S(1)}, bf16[576,128]{1,0:T(8,128)(2,1)S(1)}, u32[]{:S(2)}, u32[]{:S(2)}) collective-permute-start(bf16[576,128]{1,0:T(8,128)(2,1)S(1)} %collective-permute-done.refs_1_), channel_id=1, source_target_pairs={{0,4},{4,0},{8,12},{12,8},{16,20},{20,16},{24,28},{28,24},{1,5},{5... | collective-permute-start | bytes 442376 | tf_op jit(solution)/shard_map/ppermute | solution.py:466
  20.3 1.5 %collective-permute-start.5 = (bf16[576,128]{1,0:T(8,128)(2,1)S(1)}, bf16[576,128]{1,0:T(8,128)(2,1)S(1)}, u32[]{:S(2)}, u32[]{:S(2)}) collective-permute-start(bf16[576,128]{1,0:T(8,128)(2,1)S(1)} %collective-permute-done.1.refs_2_), channel_id=1, source_target_pairs={{0,4},{4,0},{8,12},{12,8},{16,20},{20,16},{24,28},{28,24},{1,5},{5... | collective-permute-start | bytes 442376 | tf_op jit(solution)/shard_map/ppermute | solution.py:466
  21.8 1.5 %copy-start = (bf16[128,7168]{1,0:T(8,128)(2,1)S(1)}, bf16[128,7168]{1,0:T(8,128)(2,1)}, u32[]{:S(2)}) copy-start(bf16[128,7168]{1,0:T(8,128)(2,1)} %up_h.1) | copy-start | bytes 5505028
  23.3 0.9 %copy-start.3 = (bf16[576,128]{1,0:T(8,128)(2,1)S(1)}, bf16[576,128]{1,0:T(8,128)(2,1)}, u32[]{:S(2)}) copy-start(bf16[576,128]{1,0:T(8,128)(2,1)} %pack_blocks.1.refs_0_) | copy-start | bytes 442372
  24.2 11.3 %copy-start.5 = (f32[4,128,128]{2,1,0:T(8,128)S(1)}, f32[4,128,128]{2,1,0:T(8,128)}, u32[]{:S(2)}) copy-start(f32[4,128,128]{2,1,0:T(8,128)} %one_ref.1) | copy-start | bytes 786436
  24.2 11.3 %copy-start.6 = (f32[4,128,128]{2,1,0:T(8,128)S(1)}, f32[4,128,128]{2,1,0:T(8,128)}, u32[]{:S(2)}) copy-start(f32[4,128,128]{2,1,0:T(8,128)} %two_ref.1) | copy-start | bytes 786436
  24.2 30.8 %copy-start.2 = (bf16[128,2048]{1,0:T(8,128)(2,1)S(1)}, bf16[128,2048]{1,0:T(8,128)(2,1)}, u32[]{:S(2)}) copy-start(bf16[128,2048]{1,0:T(8,128)(2,1)} %refs_8_.3) | copy-start | bytes 1572868
  26.5 28.5 %copy-start.1 = (bf16[128,7168]{1,0:T(8,128)(2,1)S(1)}, bf16[128,7168]{1,0:T(8,128)(2,1)}, u32[]{:S(2)}) copy-start(bf16[128,7168]{1,0:T(8,128)(2,1)} %up_h.1) | copy-start | bytes 5505028
  26.5 19.4 %collective-permute-start.13 = (bf16[128,2048]{1,0:T(8,128)(2,1)S(1)}, bf16[128,2048]{1,0:T(8,128)(2,1)S(1)}, u32[]{:S(2)}, u32[]{:S(2)}) collective-permute-start(bf16[128,2048]{1,0:T(8,128)(2,1)S(1)} %get-tuple-element.41), channel_id=1, source_target_pairs={{0,1},{3,2},{4,5},{7,6},{8,9},{11,10},{12,13},{15,14},{16,17},{19,... | collective-permute-start | bytes 1572872 | tf_op jit(solution)/shard_map/ppermute | solution.py:477
  36.2 4.5 %collective-permute-start.11 = (bf16[768,128]{1,0:T(8,128)(2,1)S(1)}, bf16[768,128]{1,0:T(8,128)(2,1)S(1)}, u32[]{:S(2)}, u32[]{:S(2)}) collective-permute-start(bf16[768,128]{1,0:T(8,128)(2,1)S(1)} %get-tuple-element.38), channel_id=1, source_target_pairs={{0,4},{4,8},{8,12},{12,16},{16,20},{20,24},{24,28},{1,5},{5,9},{9,... | collective-permute-start | bytes 589832 | tf_op jit(solution)/shard_map/ppermute | solution.py:482
  38.0 4.5 %collective-permute-start.12 = (bf16[768,128]{1,0:T(8,128)(2,1)S(1)}, bf16[768,128]{1,0:T(8,128)(2,1)S(1)}, u32[]{:S(2)}, u32[]{:S(2)}) collective-permute-start(bf16[768,128]{1,0:T(8,128)(2,1)S(1)} %get-tuple-element.39), channel_id=1, source_target_pairs={{4,0},{8,4},{12,8},{16,12},{20,16},{24,20},{28,24},{5,1},{9,5},{13... | collective-permute-start | bytes 589832 | tf_op jit(solution)/shard_map/ppermute | solution.py:483
  39.3 15.6 %collective-permute-start.14 = (bf16[128,2048]{1,0:T(8,128)(2,1)S(1)}, bf16[128,2048]{1,0:T(8,128)(2,1)S(1)}, u32[]{:S(2)}, u32[]{:S(2)}) collective-permute-start(bf16[128,2048]{1,0:T(8,128)(2,1)S(1)} %collective-permute-done.9.refs_2_.refs_11_), channel_id=1, source_target_pairs={{1,0},{2,3},{5,4},{6,7},{9,8},{10,11},{13,12},{14,15},{17,16},{18,... | collective-permute-start | bytes 1572872 | tf_op jit(solution)/shard_map/ppermute | solution.py:227
  46.1 19.7 %collective-permute-start.19 = (bf16[128,2048]{1,0:T(8,128)(2,1)S(1)}, bf16[128,2048]{1,0:T(8,128)(2,1)S(1)}, u32[]{:S(2)}, u32[]{:S(2)}) collective-permute-start(bf16[128,2048]{1,0:T(8,128)(2,1)S(1)} %add_convert_fusion.3), channel_id=1, source_target_pairs={{1,2},{2,1},{5,6},{6,5},{9,10},{10,9},{13,14},{14,13},{17,18},{18,... | collective-permute-start | bytes 1572872 | tf_op jit(solution)/shard_map/ppermute | solution.py:486
  46.8 19.0 %collective-permute-start.20 = (bf16[128,2048]{1,0:T(8,128)(2,1)S(1)}, bf16[128,2048]{1,0:T(8,128)(2,1)S(1)}, u32[]{:S(2)}, u32[]{:S(2)}) collective-permute-start(bf16[128,2048]{1,0:T(8,128)(2,1)S(1)} %get-tuple-element.50), channel_id=1, source_target_pairs={{0,1},{3,2},{4,5},{7,6},{8,9},{11,10},{12,13},{15,14},{16,17},{19,... | collective-permute-start | bytes 1572872 | tf_op jit(solution)/shard_map/ppermute | solution.py:487
  57.4 8.4 %collective-permute-start.15 = (bf16[16,128,128]{2,1,0:T(8,128)(2,1)S(1)}, bf16[16,128,128]{2,1,0:T(8,128)(2,1)S(1)}, u32[]{:S(2)}, u32[]{:S(2)}) collective-permute-start(bf16[16,128,128]{2,1,0:T(8,128)(2,1)S(1)} %get-tuple-element.45), channel_id=1, source_target_pairs={{0,4},{4,0},{8,12},{12,8},{16,20},{20,16},{24,28},{28,24},{1,5},{5... | collective-permute-start | bytes 1572872 | tf_op jit(solution)/shard_map/ppermute | solution.py:322
  66.5 14.6 %collective-permute-start.21 = (bf16[128,2048]{1,0:T(8,128)(2,1)S(1)}, bf16[128,2048]{1,0:T(8,128)(2,1)S(1)}, u32[]{:S(2)}, u32[]{:S(2)}) collective-permute-start(bf16[128,2048]{1,0:T(8,128)(2,1)S(1)} %get-tuple-element.56), channel_id=1, source_target_pairs={{0,1},{3,2},{1,0},{2,3},{4,5},{7,6},{5,4},{6,7},{8,9},{11,10},{9,8... | collective-permute-start | bytes 1572872 | tf_op jit(solution)/shard_map/ppermute | solution.py:499
  69.0 12.1 %collective-permute-start.22 = (bf16[128,2048]{1,0:T(8,128)(2,1)S(1)}, bf16[128,2048]{1,0:T(8,128)(2,1)S(1)}, u32[]{:S(2)}, u32[]{:S(2)}) collective-permute-start(bf16[128,2048]{1,0:T(8,128)(2,1)S(1)} %get-tuple-element.55), channel_id=1, source_target_pairs={{1,2},{2,1},{5,6},{6,5},{9,10},{10,9},{13,14},{14,13},{17,18},{18,... | collective-permute-start | bytes 1572872 | tf_op jit(solution)/shard_map/ppermute | solution.py:498
  69.7 7.2 %collective-permute-start.16 = (bf16[4,128,128]{2,1,0:T(8,128)(2,1)S(1)}, bf16[4,128,128]{2,1,0:T(8,128)(2,1)S(1)}, u32[]{:S(2)}, u32[]{:S(2)}) collective-permute-start(bf16[4,128,128]{2,1,0:T(8,128)(2,1)S(1)} %get-tuple-element.63), channel_id=1, source_target_pairs={{0,8},{4,12},{8,0},{12,4},{16,24},{20,28},{24,16},{28,20},{1,9},{5... | collective-permute-start | bytes 393224 | tf_op jit(solution)/shard_map/ppermute | solution.py:329
  70.7 8.2 %collective-permute-start.17 = (bf16[4,128,128]{2,1,0:T(8,128)(2,1)S(1)}, bf16[4,128,128]{2,1,0:T(8,128)(2,1)S(1)}, u32[]{:S(2)}, u32[]{:S(2)}) collective-permute-start(bf16[4,128,128]{2,1,0:T(8,128)(2,1)S(1)} %get-tuple-element.62), channel_id=1, source_target_pairs={{0,16},{4,20},{8,24},{12,28},{16,0},{20,4},{24,8},{28,12},{1,17},{... | collective-permute-start | bytes 393224 | tf_op jit(solution)/shard_map/ppermute | solution.py:329
  71.4 7.5 %collective-permute-start.18 = (bf16[4,128,128]{2,1,0:T(8,128)(2,1)S(1)}, bf16[4,128,128]{2,1,0:T(8,128)(2,1)S(1)}, u32[]{:S(2)}, u32[]{:S(2)}) collective-permute-start(bf16[4,128,128]{2,1,0:T(8,128)(2,1)S(1)} %get-tuple-element.61), channel_id=1, source_target_pairs={{0,24},{4,28},{8,16},{12,20},{16,8},{20,12},{24,0},{28,4},{1,25},{... | collective-permute-start | bytes 393224 | tf_op jit(solution)/shard_map/ppermute | solution.py:329

commit v3 on v2

--- a/solution.py
+++ b/solution.py
@@ -22,9 +22,10 @@
 VMEM = pl.BlockSpec(memory_space=pltpu.VMEM)
 ANY = pl.BlockSpec(memory_space=pl.ANY)
 SMEM = pl.BlockSpec(memory_space=pltpu.SMEM)
-
-
-def params(mib=32):
+HBM = pl.BlockSpec(memory_space=pltpu.HBM)
+
+
+def params(mib=24):
     return pltpu.CompilerParams(vmem_limit_bytes=mib * 1024 * 1024)
 
 
@@ -65,6 +66,31 @@
         cost_estimate=pl.CostEstimate(flops=0, bytes_accessed=0, transcendentals=0),
         name="pack_blocks",
     )(rows, cols, dests, weight)
+
+
+def hold_kernel(count, *refs):
+    sems = refs[-1]
+    copies = [
+        pltpu.make_async_copy(refs[i], refs[count + i], sems.at[i]) for i in range(count)
+    ]
+    for copy in copies:
+        copy.start()
+    for copy in copies:
+        copy.wait()
+
+
+def hold(*arrays):
+    count = len(arrays)
+    return pl.pallas_call(
+        functools.partial(hold_kernel, count),
+        out_shape=tuple(jax.ShapeDtypeStruct(a.shape, a.dtype) for a in arrays),
+        in_specs=[ANY] * count,
+        out_specs=(VMEM,) * count,
+        scratch_shapes=[pltpu.SemaphoreType.DMA((count,))],
+        compiler_params=params(8),
+        cost_estimate=pl.CostEstimate(flops=0, bytes_accessed=0, transcendentals=0),
+        name="hold_arrays",
+    )(*arrays)
 
 
 def leave_kernel(dest_h, w_h, one_h, two_h, left_ref, right_ref, dest_s, w_ref, one_ref, two_ref, sems):
@@ -138,9 +164,13 @@
 def backward_kernel(kept, ids, slices, *refs):
     count = len(ids)
     packs, up_ref = refs[:count], refs[count]
-    shares = refs[count + 1 : count + 1 + slices]
-    meta_ref = refs[count + 1 + slices]
-    acc, meta_s, sem = refs[count + 2 + slices :]
+    acc, meta_s, *held, sems = refs[-3 - slices :]
+    if slices == 4:
+        middle_ref, refs = refs[count + 1], refs[count + 2 : -3 - slices]
+        mix_ref = refs[slices + 1]
+    else:
+        refs = refs[count + 1 : -3 - slices]
+    shares, meta_ref = refs[:slices], refs[slices]
     side = meta_ref.shape[1]
     pitch = side + TILE
     width = shares[0].shape[1]
@@ -149,7 +179,7 @@
             tile = packs[at][s * pitch + side : (s + 1) * pitch, :].astype(f32)
             row = ident * kept + s
             meta_ref[row : row + 1, :] = tile[0:1, :].astype(jnp.int32)
-    copy = pltpu.make_async_copy(meta_ref, meta_s, sem)
+    copy = pltpu.make_async_copy(meta_ref, meta_s, sems.at[slices])
     copy.start()
     acc[...] = jnp.zeros_like(acc)
     copy.wait()
@@ -165,9 +195,25 @@
             )
             place = pl.ds(pl.multiple_of(row * side, side), side)
             acc[:, place] = acc[:, place] + part
-    for k, quarter in enumerate(share_order(lax.axis_index("mp"), slices)):
+    order = share_order(lax.axis_index("mp"), slices)
+    copies = [pltpu.make_async_copy(held[k], shares[k], sems.at[k]) for k in range(slices)]
+    for k, quarter in enumerate(order):
         share = lanes(acc, quarter, width) * grad_scale
-        shares[k][...] = share.astype(shares[k].dtype)
+        held[k][...] = share.astype(held[k].dtype)
+        copies[k].start()
+    if slices == 4:
+        outer = lax.rem(lax.axis_index("mp"), 3) == 0
+
+        @pl.when(outer)
+        def _():
+            mix_ref[...] = held[1][...]
+
+        @pl.when(jnp.logical_not(outer))
+        def _():
+            mix_ref[...] = middle_ref[...]
+
+    for copy in copies:
+        copy.wait()
 
 
 def share_order(me, slices):
@@ -177,28 +223,30 @@
     return tuple(lax.rem(me + k, slices) for k in range(slices))
 
 
-def backward(packs, ids, upstream, kept, slices, features):
+def backward(packs, ids, upstream, middle, kept, slices, features):
     tokens = upstream.shape[0]
     side = packs[0].shape[1]
     blocks = len(ids) * kept
     shares = [
         jax.ShapeDtypeStruct((tokens, features), f32 if k == 0 else bf16) for k in range(slices)
     ]
+    mixed = [jax.ShapeDtypeStruct((tokens, features), bf16) for _ in middle]
     outs = pl.pallas_call(
         functools.partial(backward_kernel, kept, ids, slices),
-        out_shape=(*shares, jax.ShapeDtypeStruct((blocks, side), jnp.int32)),
-        in_specs=[VMEM] * (len(ids) + 1),
-        out_specs=(VMEM,) * (slices + 1),
+        out_shape=(*shares, jax.ShapeDtypeStruct((blocks, side), jnp.int32), *mixed),
+        in_specs=[VMEM] * (len(ids) + 1 + len(middle)),
+        out_specs=(HBM,) * slices + (VMEM,) * (1 + len(mixed)),
         scratch_shapes=[
             pltpu.VMEM((tokens, slices * features), f32),
             pltpu.SMEM((blocks, side), jnp.int32),
-            pltpu.SemaphoreType.DMA,
+            *(pltpu.VMEM(share.shape, share.dtype) for share in shares),
+            pltpu.SemaphoreType.DMA((slices + 1,)),
         ],
         compiler_params=params(),
         cost_estimate=pl.CostEstimate(flops=0, bytes_accessed=0, transcendentals=0),
         name="input_gradient",
-    )(*packs, upstream)
-    return outs[:slices], outs[slices]
+    )(*packs, upstream, *middle)
+    return outs[:slices], outs[slices], outs[slices + 1 :]
 
 
 def line_reduce(shares, axis):
@@ -216,20 +264,63 @@
     return (shares[0] + right.astype(f32) + left.astype(f32)).astype(bf16)
 
 
-def four_gather(own, axis):
-    inner, outward = [(1, 2), (2, 1)], [(1, 0), (2, 3)]
-    near = lax.ppermute(own, axis, [(0, 1), (1, 0), (2, 3), (3, 2)])
-    middle = lax.ppermute(own, axis, inner)
-    near, middle = lax.optimization_barrier((near, middle))
-    near_on = lax.ppermute(near, axis, inner)
-    middle_on = lax.ppermute(middle, axis, outward)
-    near_on, middle_on = lax.optimization_barrier((near_on, middle_on))
-    last = lax.ppermute(near_on, axis, outward)
-    return near, middle, near_on, middle_on, last
-
-
 def after(value, *others):
     return lax.optimization_barrier((value, *others))[0]
+
+
+def sum_kernel(far_h, came_h, sum_ref, far_ref, came_ref, sems):
+    @pl.when(lax.rem(lax.axis_index("mp"), 3) != 0)
+    def _():
+        copies = [
+            pltpu.make_async_copy(far_h, far_ref, sems.at[0]),
+            pltpu.make_async_copy(came_h, came_ref, sems.at[1]),
+        ]
+        for copy in copies:
+            copy.start()
+        for copy in copies:
+            copy.wait()
+        sum_ref[...] = (far_ref[...].astype(f32) + came_ref[...].astype(f32)).astype(bf16)
+
+
+def inner_sum(far, came):
+    return pl.pallas_call(
+        sum_kernel,
+        out_shape=jax.ShapeDtypeStruct(far.shape, bf16),
+        in_specs=[ANY] * 2,
+        out_specs=VMEM,
+        scratch_shapes=[
+            pltpu.VMEM(far.shape, bf16),
+            pltpu.VMEM(far.shape, bf16),
+            pltpu.SemaphoreType.DMA((2,)),
+        ],
+        compiler_params=params(),
+        cost_estimate=pl.CostEstimate(flops=0, bytes_accessed=0, transcendentals=0),
+        name="inner_sum",
+    )(far, came)
+
+
+def choose_kernel(outer_h, inner_h, mixed_ref, sem):
+    outer = lax.rem(lax.axis_index("mp"), 3) == 0
+    for when, source in ((outer, outer_h), (jnp.logical_not(outer), inner_h)):
+
+        @pl.when(when)
+        def _(source=source):
+            copy = pltpu.make_async_copy(source, mixed_ref, sem)
+            copy.start()
+            copy.wait()
+
+
+def choose(at_outer, at_inner):
+    return pl.pallas_call(
+        choose_kernel,
+        out_shape=jax.ShapeDtypeStruct(at_outer.shape, bf16),
+        in_specs=[ANY] * 2,
+        out_specs=VMEM,
+        scratch_shapes=[pltpu.SemaphoreType.DMA],
+        compiler_params=params(),
+        cost_estimate=pl.CostEstimate(flops=0, bytes_accessed=0, transcendentals=0),
+        name="choose_sent",
+    )(at_outer, at_inner)
 
 
 def plus(share, came):
@@ -240,11 +331,11 @@
     me = lax.axis_index("mp")
     todo = [(None, own, me)]
     if slices == 4:
-        near, middle, near_on, middle_on, last = came
+        near, middle, near_on, mixed, mixed_on = came
         outer = lax.rem(me, 3) == 0
         todo.append((None, near, jnp.bitwise_xor(me, 1)))
-        todo.append((outer, middle_on, jnp.where(me == 0, 2, 1)))
-        todo.append((outer, last, 3 - me))
+        todo.append((outer, mixed, jnp.where(me == 0, 2, 1)))
+        todo.append((outer, mixed_on, 3 - me))
         todo.append((jnp.logical_not(outer), middle, 3 - me))
         todo.append((jnp.logical_not(outer), near_on, jnp.where(me == 1, 3, 0)))
     else:
@@ -458,8 +549,16 @@
     dp = lax.axis_size("dp")
     slices = lax.axis_size("mp")
     four = slices == 4
-    came = four_gather(tokens, "mp") if four else line_gather(tokens, "mp")
+    pairs, inner = [(0, 1), (1, 0), (2, 3), (3, 2)], [(1, 2), (2, 1)]
+    inward, outward = [(0, 1), (3, 2)], [(1, 0), (2, 3)]
+
     packs, ids = [pack(block_row, block_col, dest_slot, weight)], [0]
+    if four:
+        own_tokens = after(tokens, packs[0])
+        near = lax.ppermute(own_tokens, "mp", pairs)
+        middle = lax.ppermute(own_tokens, "mp", inner)
+    else:
+        came = line_gather(tokens, "mp")
     bit = dp // 2
     while bit:
         packs = packs + [
@@ -467,47 +566,62 @@
         ]
         ids = ids + [i ^ bit for i in ids]
         bit //= 2
+        if bit == 1:
+            held = hold(after(upstream, packs[1]), packs[0])
+            packs[-1] = after(packs[-1], *held)
+            packs[0], up_held = held[1], held[0]
     ids = tuple(ids)
+    middles = ()
     if four:
-        packs[-1] = after(packs[-1], came[0], came[1])
-    shares, meta = backward(packs, ids, upstream, kept, slices, tokens.shape[1])
+        near, middle, packs[-1] = lax.optimization_barrier((near, middle, packs[-1]))
+        middles = (middle,)
+    shares, meta, mixed = backward(
+        packs, ids, up_held, middles, kept, slices, tokens.shape[1]
+    )
+
+    dest_leave = dest_slot
     if four:
-        own, far, second, near = shares
-        ends, inner = [(0, 1), (3, 2)], [(1, 2), (2, 1)]
-        came_far = lax.ppermute(far, "mp", ends)
-        dest_leave = after(dest_slot, meta, came[2])
-    else:
-        dest_leave = dest_slot
+        outer = lax.rem(lax.axis_index("mp"), 3) == 0
+        own_share, far, second, first = shares
+        mixed = lax.ppermute(mixed[0], "mp", inward + outward)
+        near_on = lax.ppermute(after(near, meta), "mp", inner)
+        dest_leave = after(dest_slot, meta)
     to_left, to_right = leave(dest_leave, weight, moment_one, moment_two)
     from_left = lax.ppermute(to_right, "dp", [(i, i + 1) for i in range(dp - 1)])
     from_right = lax.ppermute(to_left, "dp", [(i + 1, i) for i in range(dp - 1)])
+    meta_grad = meta
     if four:
-        sum_far = plus(after(far, from_left, from_right), came_far)
+        far, mixed, from_left, from_right = lax.optimization_barrier(
+            (far, mixed, from_left, from_right)
+        )
+        sum_far = inner_sum(far, mixed)
+        mixed_on = choose(after(second, sum_far), near_on)
+        sum_far, mixed_on = lax.optimization_barrier((sum_far, mixed_on))
+        mixed_on = lax.ppermute(mixed_on, "mp", inward + outward)
         passed_far = lax.ppermute(sum_far, "mp", inner)
-        came_second = lax.ppermute(after(second, sum_far), "mp", ends)
-        meta_grad = after(meta, sum_far)
-    else:
-        meta_grad = meta
+        came = (near, middle, near_on, mixed, mixed_on)
     keep, send = gradient(meta_grad, tokens, came, upstream, kept, dp, slices)
     parts, totals = slot_reduce(keep, send, kept, dp)
+    meta_out = meta
     if four:
-        passed_far, came_second = lax.optimization_barrier((passed_far, came_second))
-        sum_second = plus(after(second, *totals), came_second)
-        sum_near = plus(near, passed_far)
-        sum_second, sum_near = lax.optimization_barrier((sum_second, sum_near))
+        sum_second = plus(after(second, send), mixed_on)
+        sum_first = plus(after(first, send), passed_far)
+        sum_second, sum_first = lax.optimization_barrier((sum_second, sum_first))
         passed_second = lax.ppermute(sum_second, "mp", inner)
-        came_near = lax.ppermute(sum_near, "mp", ends + [(1, 0), (2, 3)])
-        meta_out = after(meta, sum_second, sum_near)
-        input_grad = (own + came_near.astype(f32) + passed_second.astype(f32)).astype(bf16)
-    else:
-        meta_out = meta
-        input_grad = line_reduce(shares, "mp")
+        came_first = lax.ppermute(sum_first, "mp", inward + outward)
+        meta_out = after(meta, sum_second, sum_first, *totals)
     hidden_out = forward(
         meta_out, packs, ids, tokens, came, kept, slices, upstream.shape[1]
     )
     new_weight, new_first, new_second = update(
         meta, parts, weight, moment_one, moment_two, from_left, from_right, dp
     )
+    if four:
+        input_grad = (
+            after(own_share, hidden_out, new_weight) + came_first.astype(f32) + passed_second.astype(f32)
+        ).astype(bf16)
+    else:
+        input_grad = line_reduce(shares, "mp")
     return (new_weight, new_first, new_second, hidden_out, input_grad)
 
 

time: 83.1 us -> 72.8 us (0.88)
  starting transfers between devices: 38.9 us -> 27 us
  waiting for transfers between devices: 25.4 us -> 26.7 us
    ppermute x8 -> x6, starting transfers between devices: 24.4 us -> 13.2 us  [the longest x1 4.45 us: body(): mixed = lax.ppermute(mixed[0], 'mp', inward + outward)]
    ppermute x7, waiting for transfers between devices: 9.02 us -> 4.89 us  [body(): lax.ppermute(p, 'dp', [(i, i ^ bit) for i in range(dp)])]
    ppermute x8 -> x6, waiting for transfers between devices: 12.5 us -> 15.7 us  [the longest x1 12 us: body(): mixed_on = lax.ppermute(mixed_on, 'mp', inward + outward)]
    ppermute x1, waiting for transfers between devices: 1.89 us -> 3.75 us  [body(): lax.ppermute(to_left, 'dp', [(i + 1, i) for i in range(dp - 1)])]
    ppermute x1, starting transfers between devices: 1.77 us -> 0.18 us  [slot_reduce(): came = lax.ppermute(send, 'dp', [(i, i ^ 1) for i in range(dp)])]
    ppermute x7, starting transfers between devices: 4.68 us -> 6.08 us  [body(): lax.ppermute(p, 'dp', [(i, i ^ bit) for i in range(dp)])]
  transfers between devices with their start and end apart: 23 -> 21, of which waited for: 12 -> 9; matrix products, arithmetic and copies ran while one was open for 0% -> 1% of each run, Pallas kernels for 15% -> 13%
where the time goes in v3:
time: 72.8 us; the launch traced here: 71.8 us
  starting transfers between devices  27 us (37%)
  waiting for transfers between devices  26.7 us (37%)
  Pallas kernels  13.4 us (18%)
  local copies, waits for them, and re-layouts  2.49 us (3%)
  other arithmetic  1.42 us (2%)
  between operations  0.9 us (1%)
    ppermute x1, waiting for transfers between devices, body(): mixed_on = lax.ppermute(mixed_on, 'mp', inward + outward)  12 us
    ppermute x7, starting transfers between devices, body(): lax.ppermute(p, 'dp', [(i, i ^ bit) for i in range(dp)])  6.08 us
    ppermute x7, waiting for transfers between devices, body(): lax.ppermute(p, 'dp', [(i, i ^ bit) for i in range(dp)])  4.89 us
    ppermute x1, starting transfers between devices, body(): mixed = lax.ppermute(mixed[0], 'mp', inward + outward)  4.45 us
    ppermute x1, starting transfers between devices, body(): mixed_on = lax.ppermute(mixed_on, 'mp', inward + outward)  3.81 us
    ppermute x1, waiting for transfers between devices, body(): lax.ppermute(to_left, 'dp', [(i + 1, i) for i in range(dp - 1)])  3.75 us
    pallas_call x1, Pallas kernels, forward(): pl.pallas_call(functools.partial(forward_kernel, kept, ids, slices), out_...  3.66 us
    ppermute x3, starting transfers between devices, slot_reduce(): lax.ppermute(totals[gap], 'dp', [(i, i ^ 2 * gap) for i in range(dp)])  3.55 us
  transfers between devices with their start and end apart: 21, of which 9 were waited for; matrix products, arithmetic and copies ran while one was open for 1% of the time, Pallas kernels for 13%

profile of v3, /device:TPU:0, one launch (start us, length us, event | category | flops | bytes accessed | tf_op | source)
XLA Modules:
  0.0 71.8 jit_solution(8312933598293901712)
XLA Ops:
  0.6 1.6 %pack_blocks.1.refs_1_ = bf16[576,128]{1,0:T(8,128)(2,1)} custom-call(s32[4]{0:T(128)} %row_h.1, s32[4]{0:T(128)} %col_h.1, s32[4]{0:T(128)} %dest_h.2, bf16[4,128,128]{2,1,0:T(8,128)(2,1)} %w_ref.1), custom_call_target="tpu_custom_call" | custom-call | tf_op jit(solution)/shard_map/pack_blocks/pallas_call | solution.py:58
  2.3 3.0 %collective-permute-start = (bf16[576,128]{1,0:T(8,128)(2,1)}, bf16[576,128]{1,0:T(8,128)(2,1)S(1)}, u32[]{:S(2)}, u32[]{:S(2)}) collective-permute-start(bf16[576,128]{1,0:T(8,128)(2,1)} %pack_blocks.1.refs_1_), channel_id=1, source_target_pairs={{0,16},{4,20},{8,24},{12,28},{16,0},{20,4},{24,8},{28,12},{1,17},{... | collective-permute-start | bytes 442376 | tf_op jit(solution)/shard_map/ppermute | solution.py:565
  5.3 1.6 %collective-permute-start.6 = (bf16[128,2048]{1,0:T(8,128)(2,1)}, bf16[128,2048]{1,0:T(8,128)(2,1)S(1)}, u32[]{:S(2)}, u32[]{:S(2)}) collective-permute-start(bf16[128,2048]{1,0:T(8,128)(2,1)} %refs_8_.1), channel_id=1, source_target_pairs={{0,1},{1,0},{2,3},{3,2},{4,5},{5,4},{6,7},{7,6},{8,9},{9,8},{10,11... | collective-permute-start | bytes 1572872 | tf_op jit(solution)/shard_map/ppermute | solution.py:558
  6.9 0.7 collective-permute-start.7
  7.6 1.8 %collective-permute-done.refs_1_ = bf16[576,128]{1,0:T(8,128)(2,1)S(1)} collective-permute-done((bf16[576,128]{1,0:T(8,128)(2,1)}, bf16[576,128]{1,0:T(8,128)(2,1)S(1)}, u32[]{:S(2)}, u32[]{:S(2)}) %collective-permute-start) | collective-permute-done | bytes 147488 | tf_op jit(solution)/shard_map/ppermute | solution.py:565
  9.3 1.7 %collective-permute-start.2 = (bf16[576,128]{1,0:T(8,128)(2,1)S(1)}, bf16[576,128]{1,0:T(8,128)(2,1)S(1)}, u32[]{:S(2)}, u32[]{:S(2)}) collective-permute-start(bf16[576,128]{1,0:T(8,128)(2,1)S(1)} %collective-permute-done.refs_1_), channel_id=1, source_target_pairs={{0,8},{4,12},{8,0},{12,4},{16,24},{20,28},{24,16},{28,20},{1,9},{5... | collective-permute-start | bytes 442376 | tf_op jit(solution)/shard_map/ppermute | solution.py:565
  11.1 0.3 collective-permute-start.1
  11.4 1.5 %copy-done = bf16[128,7168]{1,0:T(8,128)(2,1)S(1)} copy-done((bf16[128,7168]{1,0:T(8,128)(2,1)S(1)}, bf16[128,7168]{1,0:T(8,128)(2,1)}, u32[]{:S(2)}) %copy-start) | copy-done | bytes 1835032
  12.9 0.9 %copy-done.6 = bf16[576,128]{1,0:T(8,128)(2,1)S(1)} copy-done((bf16[576,128]{1,0:T(8,128)(2,1)S(1)}, bf16[576,128]{1,0:T(8,128)(2,1)}, u32[]{:S(2)}) %copy-start.6) | copy-done | bytes 147480
  13.8 0.3 hold_arrays.1
  14.1 0.0 copy-start.3
  14.1 0.0 copy-start.4
  14.1 0.0 copy-start.5
  14.2 0.0 copy-start.7
  14.2 1.8 %collective-permute-done.2.refs_3_ = bf16[576,128]{1,0:T(8,128)(2,1)S(1)} collective-permute-done((bf16[576,128]{1,0:T(8,128)(2,1)S(1)}, bf16[576,128]{1,0:T(8,128)(2,1)S(1)}, u32[]{:S(2)}, u32[]{:S(2)}) %collective-permute-start.2) | collective-permute-done | bytes 147488 | tf_op jit(solution)/shard_map/ppermute | solution.py:565
  16.0 0.0 collective-permute-start.8
  16.0 0.5 collective-permute-start.3
  16.5 1.1 %collective-permute-done.1.refs_2_ = bf16[576,128]{1,0:T(8,128)(2,1)S(1)} collective-permute-done((bf16[576,128]{1,0:T(8,128)(2,1)}, bf16[576,128]{1,0:T(8,128)(2,1)S(1)}, u32[]{:S(2)}, u32[]{:S(2)}) %collective-permute-start.1) | collective-permute-done | bytes 147488 | tf_op jit(solution)/shard_map/ppermute | solution.py:565
  17.5 0.0 collective-permute-start.4
  17.5 0.0 collective-permute-done.8.refs_7_
  17.5 0.5 collective-permute-start.5
  18.1 0.8 %collective-permute-done.6.refs_0_.refs_9_ = bf16[128,2048]{1,0:T(8,128)(2,1)S(1)} collective-permute-done((bf16[128,2048]{1,0:T(8,128)(2,1)}, bf16[128,2048]{1,0:T(8,128)(2,1)S(1)}, u32[]{:S(2)}, u32[]{:S(2)}) %collective-permute-start.6) | collective-permute-done | bytes 524320 | tf_op jit(solution)/shard_map/ppermute | solution.py:558
  18.9 0.0 collective-permute-done.7.refs_9_.refs_1_.refs_10_
  18.9 0.0 collective-permute-done.3.refs_4_
  18.9 0.0 collective-permute-done.4.refs_5_
  18.9 0.2 collective-permute-done.5.refs_6_
  19.1 2.6 %input_gradient.1 = (f32[128,2048]{1,0:T(8,128)S(1)}, bf16[128,2048]{1,0:T(8,128)(2,1)S(1)}, bf16[128,2048]{1,0:T(8,128)(2,1)S(1)}, bf16[128,2048]{1,0:T(8,128)(...) custom-call(bf16[576,128]{1,0:T(8,128)(2,1)S(1)} %get-tuple-element.42.refs_0_, ...), custom_call_target="tpu_custom_call" | custom-call | tf_op jit(solution)/shard_map/input_gradient/pallas_call | solution.py:234
  21.7 4.5 %collective-permute-start.9 = (bf16[128,2048]{1,0:T(8,128)(2,1)S(1)}, bf16[128,2048]{1,0:T(8,128)(2,1)S(1)}, u32[]{:S(2)}, u32[]{:S(2)}) collective-permute-start(bf16[128,2048]{1,0:T(8,128)(2,1)S(1)} %get-tuple-element.50), channel_id=1, source_target_pairs={{0,1},{3,2},{1,0},{2,3},{4,5},{7,6},{5,4},{6,7},{8,9},{11,10},{9,8... | collective-permute-start | bytes 1572872 | tf_op jit(solution)/shard_map/ppermute | solution.py:586
  26.2 0.8 %collective-permute-start.12 = (bf16[128,2048]{1,0:T(8,128)(2,1)S(1)}, bf16[128,2048]{1,0:T(8,128)(2,1)S(1)}, u32[]{:S(2)}, u32[]{:S(2)}) collective-permute-start(bf16[128,2048]{1,0:T(8,128)(2,1)S(1)} %collective-permute-done.6.refs_0_.refs_9_), channel_id=1, source_target_pairs={{1,2},{2,1},{5,6},{6,5},{9,10},{10,9},{13,14},{14,13},{17,18},{18,... | collective-permute-start | bytes 1572872 | tf_op jit(solution)/shard_map/ppermute | solution.py:587
  27.0 0.0 copy-done.3
  27.0 0.0 copy-done.4
  27.0 0.0 copy-done.5
  27.1 0.7 leaving_blocks.1
  27.7 1.3 %collective-permute-start.10 = (bf16[768,128]{1,0:T(8,128)(2,1)S(1)}, bf16[768,128]{1,0:T(8,128)(2,1)S(1)}, u32[]{:S(2)}, u32[]{:S(2)}) collective-permute-start(bf16[768,128]{1,0:T(8,128)(2,1)S(1)} %get-tuple-element.52), channel_id=1, source_target_pairs={{0,4},{4,8},{8,12},{12,16},{16,20},{20,24},{24,28},{1,5},{5,9},{9,... | collective-permute-start | bytes 589832 | tf_op jit(solution)/shard_map/ppermute | solution.py:590
  29.0 1.3 %collective-permute-start.11 = (bf16[768,128]{1,0:T(8,128)(2,1)S(1)}, bf16[768,128]{1,0:T(8,128)(2,1)S(1)}, u32[]{:S(2)}, u32[]{:S(2)}) collective-permute-start(bf16[768,128]{1,0:T(8,128)(2,1)S(1)} %get-tuple-element.53), channel_id=1, source_target_pairs={{4,0},{8,4},{12,8},{16,12},{20,16},{24,20},{28,24},{5,1},{9,5},{13... | collective-permute-start | bytes 589832 | tf_op jit(solution)/shard_map/ppermute | solution.py:591
  30.3 0.0 collective-permute-done.10.left_ref
  30.3 3.7 %collective-permute-done.11.right_ref = bf16[768,128]{1,0:T(8,128)(2,1)S(1)} collective-permute-done((bf16[768,128]{1,0:T(8,128)(2,1)S(1)}, bf16[768,128]{1,0:T(8,128)(2,1)S(1)}, u32[]{:S(2)}, u32[]{:S(2)}) %collective-permute-start.11) | collective-permute-done | bytes 196640 | tf_op jit(solution)/shard_map/ppermute | solution.py:591
  34.1 2.8 %collective-permute-done.9.came_h.refs_3_.refs_12_ = bf16[128,2048]{1,0:T(8,128)(2,1)S(1)} collective-permute-done((bf16[128,2048]{1,0:T(8,128)(2,1)S(1)}, bf16[128,2048]{1,0:T(8,128)(2,1)S(1)}, u32[]{:S(2)}, u32[]{:S(2)}) %collective-permute-start.9) | collective-permute-done | bytes 524320 | tf_op jit(solution)/shard_map/ppermute | solution.py:586
  36.9 0.0 collective-permute-done.12.inner_h.refs_2_.refs_11_
  36.9 0.1 choose_sent.1
  37.0 3.8 %collective-permute-start.13 = (bf16[128,2048]{1,0:T(8,128)(2,1)S(1)}, bf16[128,2048]{1,0:T(8,128)(2,1)S(1)}, u32[]{:S(2)}, u32[]{:S(2)}) collective-permute-start(bf16[128,2048]{1,0:T(8,128)(2,1)S(1)} %choose_sent.1), channel_id=1, source_target_pairs={{0,1},{3,2},{1,0},{2,3},{4,5},{7,6},{5,4},{6,7},{8,9},{11,10},{9,8... | collective-permute-start | bytes 1572872 | tf_op jit(solution)/shard_map/ppermute | solution.py:600
  40.8 0.7 collective-permute-start.18
  41.5 12.0 %collective-permute-done.13.refs_4_.refs_13_ = bf16[128,2048]{1,0:T(8,128)(2,1)S(1)} collective-permute-done((bf16[128,2048]{1,0:T(8,128)(2,1)S(1)}, bf16[128,2048]{1,0:T(8,128)(2,1)S(1)}, u32[]{:S(2)}, u32[]{:S(2)}) %collective-permute-start.13) | collective-permute-done | bytes 524320 | tf_op jit(solution)/shard_map/ppermute | solution.py:600
  53.5 0.0 copy-done.2
  53.5 2.4 %weight_gradient.1 = (f32[16,128,128]{2,1,0:T(8,128)S(1)}, bf16[16,128,128]{2,1,0:T(8,128)(2,1)S(1)}) custom-call(s32[32,128]{1,0:T(8,128)S(1)} %get-tuple-element.74.meta_s, bf16[128,7168]{1,0:T(8,128)(2,1)S(1)} %copy-done.1, bf16[128,2048]{1,0:T(8,128)(2,1)S(1)} %copy-done.2, bf16[128,2048]{1,0:T(8,128)(2,1)S(1)} %collective-permute-done.6.refs_0_.refs_9_, ...), custom_call_target="tpu_custom_call" | custom-call | tf_op jit(solution)/shard_map/weight_gradient/pallas_call | solution.py:392
  55.9 0.2 collective-permute-start.14
  56.1 0.1 add_convert_fusion.2
  56.2 0.0 collective-permute-done.18
  56.3 0.1 add_convert_fusion.1
  56.4 1.9 %collective-permute-start.19 = (bf16[128,2048]{1,0:T(8,128)(2,1)S(1)}, bf16[128,2048]{1,0:T(8,128)(2,1)S(1)}, u32[]{:S(2)}, u32[]{:S(2)}) collective-permute-start(bf16[128,2048]{1,0:T(8,128)(2,1)S(1)} %add_convert_fusion.1), channel_id=1, source_target_pairs={{0,1},{3,2},{1,0},{2,3},{4,5},{7,6},{5,4},{6,7},{8,9},{11,10},{9,8... | collective-permute-start | bytes 1572872 | tf_op jit(solution)/shard_map/ppermute | solution.py:611
  58.3 0.7 collective-permute-start.20
  58.9 0.0 collective-permute-done.14
  59.0 0.2 fusion
  59.2 1.5 %collective-permute-start.15 = (bf16[4,128,128]{2,1,0:T(8,128)(2,1)S(1)}, bf16[4,128,128]{2,1,0:T(8,128)(2,1)S(1)}, u32[]{:S(2)}, u32[]{:S(2)}) collective-permute-start(bf16[4,128,128]{2,1,0:T(8,128)(2,1)S(1)} %get-tuple-element.81), channel_id=1, source_target_pairs={{0,8},{4,12},{8,0},{12,4},{16,24},{20,28},{24,16},{28,20},{1,9},{5... | collective-permute-start | bytes 393224 | tf_op jit(solution)/shard_map/ppermute | solution.py:420
  60.6 0.0 collective-permute-start.16
  60.6 2.1 %collective-permute-start.17 = (bf16[4,128,128]{2,1,0:T(8,128)(2,1)S(1)}, bf16[4,128,128]{2,1,0:T(8,128)(2,1)S(1)}, u32[]{:S(2)}, u32[]{:S(2)}) collective-permute-start(bf16[4,128,128]{2,1,0:T(8,128)(2,1)S(1)} %get-tuple-element.79), channel_id=1, source_target_pairs={{0,24},{4,28},{8,16},{12,20},{16,8},{20,12},{24,0},{28,4},{1,25},{... | collective-permute-start | bytes 393224 | tf_op jit(solution)/shard_map/ppermute | solution.py:420
  62.8 3.7 %hidden_out.1 = bf16[128,7168]{1,0:T(8,128)(2,1)} custom-call(s32[32,128]{1,0:T(8,128)S(1)} %get-tuple-element.74.meta_s, bf16[576,128]{1,0:T(8,128)(2,1)S(1)} %get-tuple-element.42.refs_0_, bf16[576,128]{1,0:T(8,128)(2,1)S(1)} %collective-permute-done.refs_1_, bf16[576,128]{1,0:T(8,128)(2,1)S(1)} %collective-permute-done.1.refs_2_, ...), custom_call_target="tpu_custom_call" | custom-call | tf_op jit(solution)/shard_map/hidden_out/pallas_call | solution.py:453
  66.4 0.0 collective-permute-done.15.refs_1_
  66.4 2.3 %collective-permute-done.16.refs_2_ = bf16[4,128,128]{2,1,0:T(8,128)(2,1)S(1)} collective-permute-done((bf16[4,128,128]{2,1,0:T(8,128)(2,1)S(1)}, bf16[4,128,128]{2,1,0:T(8,128)(2,1)S(1)}, u32[]{:S(2)}, u32[]{:S(2)}) %collective-permute-start.16) | collective-permute-done | bytes 131104 | tf_op jit(solution)/shard_map/ppermute | solution.py:420
  68.8 0.0 collective-permute-done.17.refs_3_
  68.8 2.0 %adam_update.1 = (bf16[4,128,128]{2,1,0:T(8,128)(2,1)}, f32[4,128,128]{2,1,0:T(8,128)}, f32[4,128,128]{2,1,0:T(8,128)}) custom-call(s32[32,128]{1,0:T(8,128)S(1)} %get-tuple-element.74.meta_s, bf16[4,128,128]{2,1,0:T(8,128)(2,1)S(1)} %copy-done.3, f32[4,128,128]{2,1,0:T(8,128)S(1)} %copy-done.4, f32[4,128,128]{2,1,0:T(8,128)S(1)} %copy-done.5, ...), custom_call_target="tpu_custom_call" | custom-call | tf_op jit(solution)/shard_map/adam_update/pallas_call | solution.py:532
  70.8 0.0 collective-permute-done.19
  70.8 0.0 collective-permute-done.20
  70.8 1.0 %add_convert_fusion = bf16[128,2048]{1,0:T(8,128)(2,1)} fusion(bf16[128,2048]{1,0:T(8,128)(2,1)S(1)} %collective-permute-done.20, f32[128,2048]{1,0:T(8,128)S(1)} %get-tuple-element.76, bf16[128,2048]{1,0:T(8,128)(2,1)S(1)} %collective-permute-done.19), kind=kLoop, calls=%fused_computation | loop fusion | flops 1310720 | bytes 2621440 | tf_op jit(solution)/shard_map/convert_element_type | solution.py:622
  (9 shorter events, 0.1 us)
Async XLA Ops:
  2.3 7.1 %collective-permute-start = (bf16[576,128]{1,0:T(8,128)(2,1)}, bf16[576,128]{1,0:T(8,128)(2,1)S(1)}, u32[]{:S(2)}, u32[]{:S(2)}) collective-permute-start(bf16[576,128]{1,0:T(8,128)(2,1)} %pack_blocks.1.refs_1_), channel_id=1, source_target_pairs={{0,16},{4,20},{8,24},{12,28},{16,0},{20,4},{24,8},{28,12},{1,17},{... | collective-permute-start | bytes 442376 | tf_op jit(solution)/shard_map/ppermute | solution.py:565
  5.3 13.6 %collective-permute-start.6 = (bf16[128,2048]{1,0:T(8,128)(2,1)}, bf16[128,2048]{1,0:T(8,128)(2,1)S(1)}, u32[]{:S(2)}, u32[]{:S(2)}) collective-permute-start(bf16[128,2048]{1,0:T(8,128)(2,1)} %refs_8_.1), channel_id=1, source_target_pairs={{0,1},{1,0},{2,3},{3,2},{4,5},{5,4},{6,7},{7,6},{8,9},{9,8},{10,11... | collective-permute-start | bytes 1572872 | tf_op jit(solution)/shard_map/ppermute | solution.py:558
  6.9 12.0 %collective-permute-start.7 = (bf16[128,2048]{1,0:T(8,128)(2,1)}, bf16[128,2048]{1,0:T(8,128)(2,1)S(1)}, u32[]{:S(2)}, u32[]{:S(2)}) collective-permute-start(bf16[128,2048]{1,0:T(8,128)(2,1)} %refs_8_.1), channel_id=1, source_target_pairs={{1,2},{2,1},{5,6},{6,5},{9,10},{10,9},{13,14},{14,13},{17,18},{18,... | collective-permute-start | bytes 1572872 | tf_op jit(solution)/shard_map/ppermute | solution.py:559
  9.3 6.6 %collective-permute-start.2 = (bf16[576,128]{1,0:T(8,128)(2,1)S(1)}, bf16[576,128]{1,0:T(8,128)(2,1)S(1)}, u32[]{:S(2)}, u32[]{:S(2)}) collective-permute-start(bf16[576,128]{1,0:T(8,128)(2,1)S(1)} %collective-permute-done.refs_1_), channel_id=1, source_target_pairs={{0,8},{4,12},{8,0},{12,4},{16,24},{20,28},{24,16},{28,20},{1,9},{5... | collective-permute-start | bytes 442376 | tf_op jit(solution)/shard_map/ppermute | solution.py:565
  11.1 6.5 %collective-permute-start.1 = (bf16[576,128]{1,0:T(8,128)(2,1)}, bf16[576,128]{1,0:T(8,128)(2,1)S(1)}, u32[]{:S(2)}, u32[]{:S(2)}) collective-permute-start(bf16[576,128]{1,0:T(8,128)(2,1)} %pack_blocks.1.refs_1_), channel_id=1, source_target_pairs={{0,8},{4,12},{8,0},{12,4},{16,24},{20,28},{24,16},{28,20},{1,9},{5... | collective-permute-start | bytes 442376 | tf_op jit(solution)/shard_map/ppermute | solution.py:565
  11.4 1.5 %copy-start = (bf16[128,7168]{1,0:T(8,128)(2,1)S(1)}, bf16[128,7168]{1,0:T(8,128)(2,1)}, u32[]{:S(2)}) copy-start(bf16[128,7168]{1,0:T(8,128)(2,1)} %up_h.1) | copy-start | bytes 5505028
  12.9 0.9 %copy-start.6 = (bf16[576,128]{1,0:T(8,128)(2,1)S(1)}, bf16[576,128]{1,0:T(8,128)(2,1)}, u32[]{:S(2)}) copy-start(bf16[576,128]{1,0:T(8,128)(2,1)} %pack_blocks.1.refs_1_) | copy-start | bytes 442372
  14.1 12.9 %copy-start.3 = (bf16[4,128,128]{2,1,0:T(8,128)(2,1)S(1)}, bf16[4,128,128]{2,1,0:T(8,128)(2,1)}, u32[]{:S(2)}) copy-start(bf16[4,128,128]{2,1,0:T(8,128)(2,1)} %w_ref.1) | copy-start | bytes 393220
  14.1 12.9 %copy-start.4 = (f32[4,128,128]{2,1,0:T(8,128)S(1)}, f32[4,128,128]{2,1,0:T(8,128)}, u32[]{:S(2)}) copy-start(f32[4,128,128]{2,1,0:T(8,128)} %one_ref.1) | copy-start | bytes 786436
  14.1 12.9 %copy-start.5 = (f32[4,128,128]{2,1,0:T(8,128)S(1)}, f32[4,128,128]{2,1,0:T(8,128)}, u32[]{:S(2)}) copy-start(f32[4,128,128]{2,1,0:T(8,128)} %two_ref.1) | copy-start | bytes 786436
  14.2 12.9 %copy-start.7 = (s32[4]{0:T(128)S(1)}, s32[4]{0:T(128)}, u32[]{:S(2)}) copy-start(s32[4]{0:T(128)} %dest_h.2) | copy-start | bytes 52
  16.0 1.6 %collective-permute-start.8 = (bf16[576,128]{1,0:T(8,128)(2,1)S(1)}, bf16[576,128]{1,0:T(8,128)(2,1)S(1)}, u32[]{:S(2)}, u32[]{:S(2)}) collective-permute-start(bf16[576,128]{1,0:T(8,128)(2,1)S(1)} %collective-permute-done.2.refs_3_), channel_id=1, source_target_pairs={{0,4},{4,0},{8,12},{12,8},{16,20},{20,16},{24,28},{28,24},{1,5},{5... | collective-permute-start | bytes 442376 | tf_op jit(solution)/shard_map/ppermute | solution.py:565
  16.0 2.9 %collective-permute-start.3 = (bf16[576,128]{1,0:T(8,128)(2,1)S(1)}, bf16[576,128]{1,0:T(8,128)(2,1)S(1)}, u32[]{:S(2)}, u32[]{:S(2)}) collective-permute-start(bf16[576,128]{1,0:T(8,128)(2,1)S(1)} %get-tuple-element.42.refs_0_), channel_id=1, source_target_pairs={{0,4},{4,0},{8,12},{12,8},{16,20},{20,16},{24,28},{28,24},{1,5},{5... | collective-permute-start | bytes 442376 | tf_op jit(solution)/shard_map/ppermute | solution.py:565
  17.5 1.4 %collective-permute-start.4 = (bf16[576,128]{1,0:T(8,128)(2,1)S(1)}, bf16[576,128]{1,0:T(8,128)(2,1)S(1)}, u32[]{:S(2)}, u32[]{:S(2)}) collective-permute-start(bf16[576,128]{1,0:T(8,128)(2,1)S(1)} %collective-permute-done.refs_1_), channel_id=1, source_target_pairs={{0,4},{4,0},{8,12},{12,8},{16,20},{20,16},{24,28},{28,24},{1,5},{5... | collective-permute-start | bytes 442376 | tf_op jit(solution)/shard_map/ppermute | solution.py:565
  17.5 1.6 %collective-permute-start.5 = (bf16[576,128]{1,0:T(8,128)(2,1)S(1)}, bf16[576,128]{1,0:T(8,128)(2,1)S(1)}, u32[]{:S(2)}, u32[]{:S(2)}) collective-permute-start(bf16[576,128]{1,0:T(8,128)(2,1)S(1)} %collective-permute-done.1.refs_2_), channel_id=1, source_target_pairs={{0,4},{4,0},{8,12},{12,8},{16,20},{20,16},{24,28},{28,24},{1,5},{5... | collective-permute-start | bytes 442376 | tf_op jit(solution)/shard_map/ppermute | solution.py:565
  21.7 15.2 %collective-permute-start.9 = (bf16[128,2048]{1,0:T(8,128)(2,1)S(1)}, bf16[128,2048]{1,0:T(8,128)(2,1)S(1)}, u32[]{:S(2)}, u32[]{:S(2)}) collective-permute-start(bf16[128,2048]{1,0:T(8,128)(2,1)S(1)} %get-tuple-element.50), channel_id=1, source_target_pairs={{0,1},{3,2},{1,0},{2,3},{4,5},{7,6},{5,4},{6,7},{8,9},{11,10},{9,8... | collective-permute-start | bytes 1572872 | tf_op jit(solution)/shard_map/ppermute | solution.py:586
  26.2 27.3 %copy-start.1 = (bf16[128,7168]{1,0:T(8,128)(2,1)S(1)}, bf16[128,7168]{1,0:T(8,128)(2,1)}, u32[]{:S(2)}) copy-start(bf16[128,7168]{1,0:T(8,128)(2,1)} %up_h.1) | copy-start | bytes 5505028
  26.2 27.3 %copy-start.2 = (bf16[128,2048]{1,0:T(8,128)(2,1)S(1)}, bf16[128,2048]{1,0:T(8,128)(2,1)}, u32[]{:S(2)}) copy-start(bf16[128,2048]{1,0:T(8,128)(2,1)} %refs_8_.1) | copy-start | bytes 1572868
  26.2 10.7 %collective-permute-start.12 = (bf16[128,2048]{1,0:T(8,128)(2,1)S(1)}, bf16[128,2048]{1,0:T(8,128)(2,1)S(1)}, u32[]{:S(2)}, u32[]{:S(2)}) collective-permute-start(bf16[128,2048]{1,0:T(8,128)(2,1)S(1)} %collective-permute-done.6.refs_0_.refs_9_), channel_id=1, source_target_pairs={{1,2},{2,1},{5,6},{6,5},{9,10},{10,9},{13,14},{14,13},{17,18},{18,... | collective-permute-start | bytes 1572872 | tf_op jit(solution)/shard_map/ppermute | solution.py:587
  27.7 2.6 %collective-permute-start.10 = (bf16[768,128]{1,0:T(8,128)(2,1)S(1)}, bf16[768,128]{1,0:T(8,128)(2,1)S(1)}, u32[]{:S(2)}, u32[]{:S(2)}) collective-permute-start(bf16[768,128]{1,0:T(8,128)(2,1)S(1)} %get-tuple-element.52), channel_id=1, source_target_pairs={{0,4},{4,8},{8,12},{12,16},{16,20},{20,24},{24,28},{1,5},{5,9},{9,... | collective-permute-start | bytes 589832 | tf_op jit(solution)/shard_map/ppermute | solution.py:590
  29.0 5.1 %collective-permute-start.11 = (bf16[768,128]{1,0:T(8,128)(2,1)S(1)}, bf16[768,128]{1,0:T(8,128)(2,1)S(1)}, u32[]{:S(2)}, u32[]{:S(2)}) collective-permute-start(bf16[768,128]{1,0:T(8,128)(2,1)S(1)} %get-tuple-element.53), channel_id=1, source_target_pairs={{4,0},{8,4},{12,8},{16,12},{20,16},{24,20},{28,24},{5,1},{9,5},{13... | collective-permute-start | bytes 589832 | tf_op jit(solution)/shard_map/ppermute | solution.py:591
  37.0 16.5 %collective-permute-start.13 = (bf16[128,2048]{1,0:T(8,128)(2,1)S(1)}, bf16[128,2048]{1,0:T(8,128)(2,1)S(1)}, u32[]{:S(2)}, u32[]{:S(2)}) collective-permute-start(bf16[128,2048]{1,0:T(8,128)(2,1)S(1)} %choose_sent.1), channel_id=1, source_target_pairs={{0,1},{3,2},{1,0},{2,3},{4,5},{7,6},{5,4},{6,7},{8,9},{11,10},{9,8... | collective-permute-start | bytes 1572872 | tf_op jit(solution)/shard_map/ppermute | solution.py:600
  40.8 15.4 %collective-permute-start.18 = (bf16[128,2048]{1,0:T(8,128)(2,1)S(1)}, bf16[128,2048]{1,0:T(8,128)(2,1)S(1)}, u32[]{:S(2)}, u32[]{:S(2)}) collective-permute-start(bf16[128,2048]{1,0:T(8,128)(2,1)S(1)} %inner_sum.1), channel_id=1, source_target_pairs={{1,2},{2,1},{5,6},{6,5},{9,10},{10,9},{13,14},{14,13},{17,18},{18,... | collective-permute-start | bytes 1572872 | tf_op jit(solution)/shard_map/ppermute | solution.py:601
  55.9 3.0 %collective-permute-start.14 = (bf16[16,128,128]{2,1,0:T(8,128)(2,1)S(1)}, bf16[16,128,128]{2,1,0:T(8,128)(2,1)S(1)}, u32[]{:S(2)}, u32[]{:S(2)}) collective-permute-start(bf16[16,128,128]{2,1,0:T(8,128)(2,1)S(1)} %get-tuple-element.64), channel_id=1, source_target_pairs={{0,4},{4,0},{8,12},{12,8},{16,20},{20,16},{24,28},{28,24},{1,5},{5... | collective-permute-start | bytes 1572872 | tf_op jit(solution)/shard_map/ppermute | solution.py:413
  56.4 14.4 %collective-permute-start.19 = (bf16[128,2048]{1,0:T(8,128)(2,1)S(1)}, bf16[128,2048]{1,0:T(8,128)(2,1)S(1)}, u32[]{:S(2)}, u32[]{:S(2)}) collective-permute-start(bf16[128,2048]{1,0:T(8,128)(2,1)S(1)} %add_convert_fusion.1), channel_id=1, source_target_pairs={{0,1},{3,2},{1,0},{2,3},{4,5},{7,6},{5,4},{6,7},{8,9},{11,10},{9,8... | collective-permute-start | bytes 1572872 | tf_op jit(solution)/shard_map/ppermute | solution.py:611
  58.3 12.6 %collective-permute-start.20 = (bf16[128,2048]{1,0:T(8,128)(2,1)S(1)}, bf16[128,2048]{1,0:T(8,128)(2,1)S(1)}, u32[]{:S(2)}, u32[]{:S(2)}) collective-permute-start(bf16[128,2048]{1,0:T(8,128)(2,1)S(1)} %add_convert_fusion.2), channel_id=1, source_target_pairs={{1,2},{2,1},{5,6},{6,5},{9,10},{10,9},{13,14},{14,13},{17,18},{18,... | collective-permute-start | bytes 1572872 | tf_op jit(solution)/shard_map/ppermute | solution.py:610
  59.2 7.2 %collective-permute-start.15 = (bf16[4,128,128]{2,1,0:T(8,128)(2,1)S(1)}, bf16[4,128,128]{2,1,0:T(8,128)(2,1)S(1)}, u32[]{:S(2)}, u32[]{:S(2)}) collective-permute-start(bf16[4,128,128]{2,1,0:T(8,128)(2,1)S(1)} %get-tuple-element.81), channel_id=1, source_target_pairs={{0,8},{4,12},{8,0},{12,4},{16,24},{20,28},{24,16},{28,20},{1,9},{5... | collective-permute-start | bytes 393224 | tf_op jit(solution)/shard_map/ppermute | solution.py:420
  60.6 8.1 %collective-permute-start.16 = (bf16[4,128,128]{2,1,0:T(8,128)(2,1)S(1)}, bf16[4,128,128]{2,1,0:T(8,128)(2,1)S(1)}, u32[]{:S(2)}, u32[]{:S(2)}) collective-permute-start(bf16[4,128,128]{2,1,0:T(8,128)(2,1)S(1)} %get-tuple-element.80), channel_id=1, source_target_pairs={{0,16},{4,20},{8,24},{12,28},{16,0},{20,4},{24,8},{28,12},{1,17},{... | collective-permute-start | bytes 393224 | tf_op jit(solution)/shard_map/ppermute | solution.py:420
  60.6 8.1 %collective-permute-start.17 = (bf16[4,128,128]{2,1,0:T(8,128)(2,1)S(1)}, bf16[4,128,128]{2,1,0:T(8,128)(2,1)S(1)}, u32[]{:S(2)}, u32[]{:S(2)}) collective-permute-start(bf16[4,128,128]{2,1,0:T(8,128)(2,1)S(1)} %get-tuple-element.79), channel_id=1, source_target_pairs={{0,24},{4,28},{8,16},{12,20},{16,8},{20,12},{24,0},{28,4},{1,25},{... | collective-permute-start | bytes 393224 | tf_op jit(solution)/shard_map/ppermute | solution.py:420

commit v4 on v3

--- a/solution.py
+++ b/solution.py
@@ -165,11 +165,7 @@
     count = len(ids)
     packs, up_ref = refs[:count], refs[count]
     acc, meta_s, *held, sems = refs[-3 - slices :]
-    if slices == 4:
-        middle_ref, refs = refs[count + 1], refs[count + 2 : -3 - slices]
-        mix_ref = refs[slices + 1]
-    else:
-        refs = refs[count + 1 : -3 - slices]
+    refs = refs[count + 1 : -3 - slices]
     shares, meta_ref = refs[:slices], refs[slices]
     side = meta_ref.shape[1]
     pitch = side + TILE
@@ -201,17 +197,6 @@
         share = lanes(acc, quarter, width) * grad_scale
         held[k][...] = share.astype(held[k].dtype)
         copies[k].start()
-    if slices == 4:
-        outer = lax.rem(lax.axis_index("mp"), 3) == 0
-
-        @pl.when(outer)
-        def _():
-            mix_ref[...] = held[1][...]
-
-        @pl.when(jnp.logical_not(outer))
-        def _():
-            mix_ref[...] = middle_ref[...]
-
     for copy in copies:
         copy.wait()
 
@@ -223,19 +208,18 @@
     return tuple(lax.rem(me + k, slices) for k in range(slices))
 
 
-def backward(packs, ids, upstream, middle, kept, slices, features):
+def backward(packs, ids, upstream, kept, slices, features):
     tokens = upstream.shape[0]
     side = packs[0].shape[1]
     blocks = len(ids) * kept
     shares = [
         jax.ShapeDtypeStruct((tokens, features), f32 if k == 0 else bf16) for k in range(slices)
     ]
-    mixed = [jax.ShapeDtypeStruct((tokens, features), bf16) for _ in middle]
     outs = pl.pallas_call(
         functools.partial(backward_kernel, kept, ids, slices),
-        out_shape=(*shares, jax.ShapeDtypeStruct((blocks, side), jnp.int32), *mixed),
-        in_specs=[VMEM] * (len(ids) + 1 + len(middle)),
-        out_specs=(HBM,) * slices + (VMEM,) * (1 + len(mixed)),
+        out_shape=(*shares, jax.ShapeDtypeStruct((blocks, side), jnp.int32)),
+        in_specs=[VMEM] * (len(ids) + 1),
+        out_specs=(HBM,) * slices + (VMEM,),
         scratch_shapes=[
             pltpu.VMEM((tokens, slices * features), f32),
             pltpu.SMEM((blocks, side), jnp.int32),
@@ -245,8 +229,8 @@
         compiler_params=params(),
         cost_estimate=pl.CostEstimate(flops=0, bytes_accessed=0, transcendentals=0),
         name="input_gradient",
-    )(*packs, upstream, *middle)
-    return outs[:slices], outs[slices], outs[slices + 1 :]
+    )(*packs, upstream)
+    return outs[:slices], outs[slices]
 
 
 def line_reduce(shares, axis):
@@ -331,11 +315,10 @@
     me = lax.axis_index("mp")
     todo = [(None, own, me)]
     if slices == 4:
-        near, middle, near_on, mixed, mixed_on = came
+        near, middle, near_on, mixed = came
         outer = lax.rem(me, 3) == 0
         todo.append((None, near, jnp.bitwise_xor(me, 1)))
         todo.append((outer, mixed, jnp.where(me == 0, 2, 1)))
-        todo.append((outer, mixed_on, 3 - me))
         todo.append((jnp.logical_not(outer), middle, 3 - me))
         todo.append((jnp.logical_not(outer), near_on, jnp.where(me == 1, 3, 0)))
     else:
@@ -355,26 +338,52 @@
         pl.when(when)(action)
 
 
-def gradient_kernel(kept, dp, slices, meta_s, up_h, own_h, *refs):
-    came, (keep_ref, send_ref, x_ref, up_ref, store, sems) = refs[:-6], refs[-6:]
-    side = keep_ref.shape[1]
+def assemble_kernel(slices, own_h, *refs):
+    came, (x_ref, sems) = refs[:-2], refs[-2:]
+    copies = token_copies(slices, own_h, came, x_ref, sems)
+    for when, copy in copies:
+        run(when, copy.start)
+    for when, copy in copies:
+        run(when, copy.wait)
+
+
+def assemble(own, came, slices):
+    return pl.pallas_call(
+        functools.partial(assemble_kernel, slices),
+        out_shape=jax.ShapeDtypeStruct((slices, *own.shape), bf16),
+        in_specs=[ANY] * (1 + len(came)),
+        out_specs=VMEM,
+        scratch_shapes=[pltpu.SemaphoreType.DMA((len(came) + 1,))],
+        compiler_params=params(),
+        cost_estimate=pl.CostEstimate(flops=0, bytes_accessed=0, transcendentals=0),
+        name="assemble_tokens",
+    )(own, *came)
+
+
+def token_block(x_ref, last, row, side):
     per = x_ref.shape[2] // side
+    place = pl.ds(pl.multiple_of((row % per) * side, side), side)
+    block = x_ref[row // per, :, place]
+    if last:
+        me = lax.axis_index("mp")
+        far_end = (lax.rem(me, 3) == 0) & (row // per == 3 - me)
+        block = jnp.where(far_end, last[0][:, place], block)
+    return block
+
+
+def gradient_kernel(kept, dp, meta_s, up_ref, x_ref, *refs):
+    last, (keep_ref, send_ref, store) = refs[:-3], refs[-3:]
+    side = keep_ref.shape[2]
     blocks = dp * kept
     me = lax.axis_index("dp")
-    up_copy = pltpu.make_async_copy(up_h, up_ref, sems.at[len(came) + 1])
-    copies = token_copies(slices, own_h, came, x_ref, sems)
-    up_copy.start()
-    for when, copy in copies:
-        run(when, copy.start)
     store[0:blocks] = jnp.zeros((blocks, side, side), f32)
-    up_copy.wait()
-    for when, copy in copies:
-        run(when, copy.wait)
     for b in range(blocks):
         row, col, dest = meta_s[b, 0], meta_s[b, 1], meta_s[b, 2]
-        x = x_ref[row // per, :, pl.ds(pl.multiple_of((row % per) * side, side), side)]
         grad = lax.dot_general(
-            x, lanes(up_ref, col, side), (((0,), (0,)), ((), ())), preferred_element_type=f32
+            token_block(x_ref, last, row, side),
+            lanes(up_ref, col, side),
+            (((0,), (0,)), ((), ())),
+            preferred_element_type=f32,
         )
         gap = jnp.bitwise_xor(jnp.maximum(dest, 0) // kept, me)
         place = (gap & 1) * (dp // 2) + lax.shift_right_logical(gap, 1)
@@ -385,28 +394,23 @@
     send_ref[...] = store[half : 2 * half].astype(bf16)
 
 
-def gradient(meta, own, came, upstream, kept, dp, slices):
+def gradient(meta, x_all, last, upstream, kept, dp):
     side = meta.shape[1]
     blocks = dp * kept
     half = blocks // 2
     return pl.pallas_call(
-        functools.partial(gradient_kernel, kept, dp, slices),
+        functools.partial(gradient_kernel, kept, dp),
         out_shape=(
             jax.ShapeDtypeStruct((half, side, side), f32),
             jax.ShapeDtypeStruct((half, side, side), bf16),
         ),
-        in_specs=[SMEM] + [ANY] * (2 + len(came)),
+        in_specs=[SMEM] + [VMEM] * (2 + len(last)),
         out_specs=(VMEM, VMEM),
-        scratch_shapes=[
-            pltpu.VMEM((slices, *own.shape), bf16),
-            pltpu.VMEM(upstream.shape, bf16),
-            pltpu.VMEM((blocks + 1, side, side), f32),
-            pltpu.SemaphoreType.DMA((len(came) + 2,)),
-        ],
+        scratch_shapes=[pltpu.VMEM((blocks + 1, side, side), f32)],
         compiler_params=params(),
         cost_estimate=pl.CostEstimate(flops=0, bytes_accessed=0, transcendentals=0),
         name="weight_gradient",
-    )(meta, upstream, own, *came)
+    )(meta, upstream, x_all, *last)
 
 
 def slot_reduce(keep, send, kept, dp):
@@ -421,49 +425,55 @@
     return parts, totals
 
 
-def forward_kernel(kept, ids, slices, meta_s, *refs):
+def forward_kernel(kept, ids, meta_s, *refs):
     count = len(ids)
-    packs, own_h, came = refs[:count], refs[count], refs[count + 1 : -4]
-    out_ref, x_ref, acc, sems = refs[-4:]
+    packs, x_ref, last, (out_ref, acc) = refs[:count], refs[count], refs[count + 1 : -2], refs[-2:]
     side = packs[0].shape[1]
     pitch = side + TILE
-    per = x_ref.shape[2] // side
-    copies = token_copies(slices, own_h, came, x_ref, sems)
-    for when, copy in copies:
-        run(when, copy.start)
     acc[...] = jnp.zeros_like(acc)
-    for when, copy in copies:
-        run(when, copy.wait)
     for at, ident in enumerate(ids):
         for s in range(kept):
             row = meta_s[ident * kept + s, 0]
             col = meta_s[ident * kept + s, 1]
-            x = x_ref[row // per, :, pl.ds(pl.multiple_of((row % per) * side, side), side)]
             part = jnp.dot(
-                x, packs[at][s * pitch : s * pitch + side, :], preferred_element_type=f32
+                token_block(x_ref, last, row, side),
+                packs[at][s * pitch : s * pitch + side, :],
+                preferred_element_type=f32,
             )
             place = pl.ds(pl.multiple_of(col * side, side), side)
             acc[:, place] = acc[:, place] + part
     out_ref[...] = (acc[...] * grad_scale).astype(bf16)
 
 
-def forward(meta, packs, ids, own, came, kept, slices, hidden):
-    tokens = own.shape[0]
-    side = meta.shape[1]
-    return pl.pallas_call(
-        functools.partial(forward_kernel, kept, ids, slices),
+def forward(meta, packs, ids, x_all, last, kept, hidden):
+    tokens = x_all.shape[1]
+    return pl.pallas_call(
+        functools.partial(forward_kernel, kept, ids),
         out_shape=jax.ShapeDtypeStruct((tokens, hidden), bf16),
-        in_specs=[SMEM] + [VMEM] * len(ids) + [ANY] * (1 + len(came)),
+        in_specs=[SMEM] + [VMEM] * (len(ids) + 1 + len(last)),
         out_specs=VMEM,
-        scratch_shapes=[
-            pltpu.VMEM((slices, *own.shape), bf16),
-            pltpu.VMEM((tokens, hidden), f32),
-            pltpu.SemaphoreType.DMA((len(came) + 1,)),
-        ],
+        scratch_shapes=[pltpu.VMEM((tokens, hidden), f32)],
         compiler_params=params(),
         cost_estimate=pl.CostEstimate(flops=0, bytes_accessed=0, transcendentals=0),
         name="hidden_out",
-    )(meta, *packs, own, *came)
+    )(meta, *packs, x_all, *last)
+
+
+def finish_kernel(own_ref, first_ref, second_ref, out_ref):
+    total = own_ref[...] + first_ref[...].astype(f32) + second_ref[...].astype(f32)
+    out_ref[...] = total.astype(bf16)
+
+
+def finish(own, first, second):
+    return pl.pallas_call(
+        finish_kernel,
+        out_shape=jax.ShapeDtypeStruct(own.shape, bf16),
+        in_specs=[VMEM] * 3,
+        out_specs=VMEM,
+        compiler_params=params(),
+        cost_estimate=pl.CostEstimate(flops=0, bytes_accessed=0, transcendentals=0),
+        name="finish_input_grad",
+    )(own, first, second)
 
 
 def update_kernel(
@@ -554,42 +564,33 @@
 
     packs, ids = [pack(block_row, block_col, dest_slot, weight)], [0]
     if four:
-        own_tokens = after(tokens, packs[0])
-        near = lax.ppermute(own_tokens, "mp", pairs)
-        middle = lax.ppermute(own_tokens, "mp", inner)
+        near = lax.ppermute(tokens, "mp", pairs)
+        middle = lax.ppermute(tokens, "mp", inner)
     else:
         came = line_gather(tokens, "mp")
-    bit = dp // 2
-    while bit:
-        packs = packs + [
-            lax.ppermute(p, "dp", [(i, i ^ bit) for i in range(dp)]) for p in packs
-        ]
-        ids = ids + [i ^ bit for i in ids]
-        bit //= 2
-        if bit == 1:
-            held = hold(after(upstream, packs[1]), packs[0])
-            packs[-1] = after(packs[-1], *held)
-            packs[0], up_held = held[1], held[0]
-    ids = tuple(ids)
-    middles = ()
-    if four:
-        near, middle, packs[-1] = lax.optimization_barrier((near, middle, packs[-1]))
-        middles = (middle,)
-    shares, meta, mixed = backward(
-        packs, ids, up_held, middles, kept, slices, tokens.shape[1]
-    )
+    for gap in range(2, dp, 2):
+        packs.append(lax.ppermute(packs[0], "dp", [(i, i ^ gap) for i in range(dp)]))
+        ids.append(gap)
+    held = hold(after(upstream, packs[0]), packs[0])
+    packs[0], up_held = held[1], held[0]
+    packs[1:] = lax.optimization_barrier((*packs[1:], *held))[: len(packs) - 1]
+    packs += [lax.ppermute(p, "dp", [(i, i ^ 1) for i in range(dp)]) for p in packs]
+    ids = tuple(ids + [i ^ 1 for i in ids])
+    shares, meta = backward(packs, ids, up_held, kept, slices, tokens.shape[1])
 
     dest_leave = dest_slot
     if four:
         outer = lax.rem(lax.axis_index("mp"), 3) == 0
         own_share, far, second, first = shares
-        mixed = lax.ppermute(mixed[0], "mp", inward + outward)
-        near_on = lax.ppermute(after(near, meta), "mp", inner)
+        near, middle, far = lax.optimization_barrier((near, middle, far))
+        mixed = choose(far, middle)
+        near, mixed = lax.optimization_barrier((near, mixed))
+        mixed = lax.ppermute(mixed, "mp", inward + outward)
+        near_on = lax.ppermute(near, "mp", inner)
         dest_leave = after(dest_slot, meta)
     to_left, to_right = leave(dest_leave, weight, moment_one, moment_two)
     from_left = lax.ppermute(to_right, "dp", [(i, i + 1) for i in range(dp - 1)])
     from_right = lax.ppermute(to_left, "dp", [(i + 1, i) for i in range(dp - 1)])
-    meta_grad = meta
     if four:
         far, mixed, from_left, from_right = lax.optimization_barrier(
             (far, mixed, from_left, from_right)
@@ -599,8 +600,12 @@
         sum_far, mixed_on = lax.optimization_barrier((sum_far, mixed_on))
         mixed_on = lax.ppermute(mixed_on, "mp", inward + outward)
         passed_far = lax.ppermute(sum_far, "mp", inner)
-        came = (near, middle, near_on, mixed, mixed_on)
-    keep, send = gradient(meta_grad, tokens, came, upstream, kept, dp, slices)
+        came = (near, middle, near_on, mixed)
+        x_all = assemble(after(tokens, sum_far), came, slices)
+        last = (mixed_on,)
+    else:
+        x_all, last = assemble(tokens, came, slices), ()
+    keep, send = gradient(meta, x_all, last, upstream, kept, dp)
     parts, totals = slot_reduce(keep, send, kept, dp)
     meta_out = meta
     if four:
@@ -610,16 +615,14 @@
         passed_second = lax.ppermute(sum_second, "mp", inner)
         came_first = lax.ppermute(sum_first, "mp", inward + outward)
         meta_out = after(meta, sum_second, sum_first, *totals)
-    hidden_out = forward(
-        meta_out, packs, ids, tokens, came, kept, slices, upstream.shape[1]
-    )
+    hidden_out = forward(meta_out, packs, ids, x_all, last, kept, upstream.shape[1])
     new_weight, new_first, new_second = update(
         meta, parts, weight, moment_one, moment_two, from_left, from_right, dp
     )
     if four:
-        input_grad = (
-            after(own_share, hidden_out, new_weight) + came_first.astype(f32) + passed_second.astype(f32)
-        ).astype(bf16)
+        input_grad = finish(
+            after(own_share, hidden_out, new_weight), came_first, passed_second
+        )
     else:
         input_grad = line_reduce(shares, "mp")
     return (new_weight, new_first, new_second, hidden_out, input_grad)

time: 72.8 us -> 71.6 us (0.984)
  Pallas kernels: 13.4 us -> 14.4 us
  waiting for transfers between devices: 26.7 us -> 25.7 us
  other arithmetic: 1.42 us -> 0.44 us
    ppermute x11, waiting for transfers between devices: 8.53 us -> 10.2 us  [the longest x1 5.15 us: body(): mixed = lax.ppermute(mixed, 'mp', inward + outward)]
    ppermute x1, waiting for transfers between devices: 12 us -> 10.6 us  [body(): mixed_on = lax.ppermute(mixed_on, 'mp', inward + outward)]
    ppermute x1, waiting for transfers between devices: 3.75 us -> 2.54 us  [body(): lax.ppermute(to_left, 'dp', [(i + 1, i) for i in range(dp - 1)])]
    convert_element_type x1 -> x0, other arithmetic: 0.98 us -> none  [body(): input_grad = (after(own_share, hidden_out, new_weight) + came_first.astyp...]
    pallas_call x2 -> x4, Pallas kernels: 6.06 us -> 7.03 us  [the longest x1 3.67 us: forward(): pl.pallas_call(functools.partial(forward_kernel, kept, ids), out_shape=ja...]
  transfers between devices with their start and end apart: 21 -> 21, of which waited for: 9 -> 10; matrix products, arithmetic and copies ran while one was open for 1% -> 1% of each run, Pallas kernels for 13% -> 19%
where the time goes in v4:
time: 71.6 us; the launch traced here: 70.7 us
  starting transfers between devices  26.7 us (37%)
  waiting for transfers between devices  25.7 us (36%)
  Pallas kernels  14.4 us (20%)
  local copies, waits for them, and re-layouts  2.48 us (3%)
  between operations  0.94 us (1%)
    ppermute x1, waiting for transfers between devices, body(): mixed_on = lax.ppermute(mixed_on, 'mp', inward + outward)  10.6 us
    ppermute x1, waiting for transfers between devices, body(): mixed = lax.ppermute(mixed, 'mp', inward + outward)  5.15 us
    ppermute x1, starting transfers between devices, body(): mixed = lax.ppermute(mixed, 'mp', inward + outward)  4.44 us
    ppermute x3, waiting for transfers between devices, body(): lax.ppermute(packs[0], 'dp', [(i, i ^ gap) for i in range(dp)])  3.73 us
    pallas_call x1, Pallas kernels, forward(): pl.pallas_call(functools.partial(forward_kernel, kept, ids), out_shape=ja...  3.67 us
    ppermute x1, starting transfers between devices, body(): mixed_on = lax.ppermute(mixed_on, 'mp', inward + outward)  3.65 us
    ppermute x3, starting transfers between devices, body(): lax.ppermute(packs[0], 'dp', [(i, i ^ gap) for i in range(dp)])  3.55 us
    ppermute x3, starting transfers between devices, slot_reduce(): lax.ppermute(totals[gap], 'dp', [(i, i ^ 2 * gap) for i in range(dp)])  3.55 us
  transfers between devices with their start and end apart: 21, of which 10 were waited for; matrix products, arithmetic and copies ran while one was open for 1% of the time, Pallas kernels for 19%

profile of v4, /device:TPU:0, one launch (start us, length us, event | category | flops | bytes accessed | tf_op | source)
XLA Modules:
  0.0 70.7 jit_solution(5233682210903555310)
XLA Ops:
  0.6 3.1 %collective-permute-start.7 = (bf16[128,2048]{1,0:T(8,128)(2,1)}, bf16[128,2048]{1,0:T(8,128)(2,1)S(1)}, u32[]{:S(2)}, u32[]{:S(2)}) collective-permute-start(bf16[128,2048]{1,0:T(8,128)(2,1)} %own_h), channel_id=1, source_target_pairs={{0,1},{1,0},{2,3},{3,2},{4,5},{5,4},{6,7},{7,6},{8,9},{9,8},{10,11... | collective-permute-start | bytes 1572872 | tf_op jit(solution)/shard_map/ppermute | solution.py:567
  3.7 0.7 collective-permute-start.8
  4.4 1.6 %pack_blocks.1.refs_1_ = bf16[576,128]{1,0:T(8,128)(2,1)} custom-call(s32[4]{0:T(128)} %row_h.1, s32[4]{0:T(128)} %col_h.1, s32[4]{0:T(128)} %dest_h.2, bf16[4,128,128]{2,1,0:T(8,128)(2,1)} %w_ref.1), custom_call_target="tpu_custom_call" | custom-call | tf_op jit(solution)/shard_map/pack_blocks/pallas_call | solution.py:58
  6.0 1.6 %collective-permute-start = (bf16[576,128]{1,0:T(8,128)(2,1)}, bf16[576,128]{1,0:T(8,128)(2,1)S(1)}, u32[]{:S(2)}, u32[]{:S(2)}) collective-permute-start(bf16[576,128]{1,0:T(8,128)(2,1)} %pack_blocks.1.refs_1_), channel_id=1, source_target_pairs={{0,8},{4,12},{8,0},{12,4},{16,24},{20,28},{24,16},{28,20},{1,9},{5... | collective-permute-start | bytes 442376 | tf_op jit(solution)/shard_map/ppermute | solution.py:572
  7.6 1.5 %collective-permute-start.1 = (bf16[576,128]{1,0:T(8,128)(2,1)}, bf16[576,128]{1,0:T(8,128)(2,1)S(1)}, u32[]{:S(2)}, u32[]{:S(2)}) collective-permute-start(bf16[576,128]{1,0:T(8,128)(2,1)} %pack_blocks.1.refs_1_), channel_id=1, source_target_pairs={{0,16},{4,20},{8,24},{12,28},{16,0},{20,4},{24,8},{28,12},{1,17},{... | collective-permute-start | bytes 442376 | tf_op jit(solution)/shard_map/ppermute | solution.py:572
  9.1 0.5 collective-permute-start.2
  9.6 1.5 %copy-done = bf16[128,7168]{1,0:T(8,128)(2,1)S(1)} copy-done((bf16[128,7168]{1,0:T(8,128)(2,1)S(1)}, bf16[128,7168]{1,0:T(8,128)(2,1)}, u32[]{:S(2)}) %copy-start) | copy-done | bytes 1835032
  11.1 0.9 %copy-done.5 = bf16[576,128]{1,0:T(8,128)(2,1)S(1)} copy-done((bf16[576,128]{1,0:T(8,128)(2,1)S(1)}, bf16[576,128]{1,0:T(8,128)(2,1)}, u32[]{:S(2)}) %copy-start.5) | copy-done | bytes 147480
  12.0 0.3 hold_arrays.1
  12.3 0.1 collective-permute-done.refs_1_
  12.4 0.0 collective-permute-start.3
  12.4 3.7 %collective-permute-done.1.refs_2_ = bf16[576,128]{1,0:T(8,128)(2,1)S(1)} collective-permute-done((bf16[576,128]{1,0:T(8,128)(2,1)}, bf16[576,128]{1,0:T(8,128)(2,1)S(1)}, u32[]{:S(2)}, u32[]{:S(2)}) %collective-permute-start.1) | collective-permute-done | bytes 147488 | tf_op jit(solution)/shard_map/ppermute | solution.py:572
  16.1 0.0 collective-permute-done.2.refs_3_
  16.1 0.0 copy-start.7
  16.1 0.1 collective-permute-start.4
  16.2 0.5 collective-permute-start.5
  16.7 0.0 collective-permute-done.3.refs_4_
  16.7 0.1 collective-permute-start.6
  16.8 0.8 %collective-permute-done.4.refs_5_ = bf16[576,128]{1,0:T(8,128)(2,1)S(1)} collective-permute-done((bf16[576,128]{1,0:T(8,128)(2,1)S(1)}, bf16[576,128]{1,0:T(8,128)(2,1)S(1)}, u32[]{:S(2)}, u32[]{:S(2)}) %collective-permute-start.4) | collective-permute-done | bytes 147488 | tf_op jit(solution)/shard_map/ppermute | solution.py:577
  17.6 0.2 collective-permute-done.5.refs_6_
  17.8 0.3 collective-permute-done.6.refs_7_
  18.1 2.6 %input_gradient.1 = (f32[128,2048]{1,0:T(8,128)S(1)}, bf16[128,2048]{1,0:T(8,128)(2,1)S(1)}, bf16[128,2048]{1,0:T(8,128)(2,1)S(1)}, bf16[128,2048]{1,0:T(8,128)(2,1)S(1)}, s32[32,128]{1,0:T(8,128)S(1)}) custom-call(bf16[576,128]{1,0:T(8,128)(2,1)S(1)} %get-tuple-element.44.refs_0_, bf16[576,128]{1,0:T(8,128)(2,1)S(1)} %collective-permute-done.refs_1_, ...), custom_call_target="tpu_custom_call" | custom-call | tf_op jit(solution)/shard_map/input_gradient/pallas_call | solution.py:218
  20.6 0.0 collective-permute-done.7.refs_0_
  20.7 0.0 collective-permute-done.8.inner_h.refs_1_
  20.7 0.1 choose_sent.2
  20.7 4.4 %collective-permute-start.9 = (bf16[128,2048]{1,0:T(8,128)(2,1)S(1)}, bf16[128,2048]{1,0:T(8,128)(2,1)S(1)}, u32[]{:S(2)}, u32[]{:S(2)}) collective-permute-start(bf16[128,2048]{1,0:T(8,128)(2,1)S(1)} %choose_sent.2), channel_id=1, source_target_pairs={{0,1},{3,2},{1,0},{2,3},{4,5},{7,6},{5,4},{6,7},{8,9},{11,10},{9,8... | collective-permute-start | bytes 1572872 | tf_op jit(solution)/shard_map/ppermute | solution.py:588
  25.2 0.7 collective-permute-start.12
  25.9 0.0 copy-done.2
  25.9 0.0 copy-done.3
  25.9 0.0 copy-start.6
  25.9 0.7 leaving_blocks.1
  26.6 1.9 %collective-permute-start.10 = (bf16[768,128]{1,0:T(8,128)(2,1)S(1)}, bf16[768,128]{1,0:T(8,128)(2,1)S(1)}, u32[]{:S(2)}, u32[]{:S(2)}) collective-permute-start(bf16[768,128]{1,0:T(8,128)(2,1)S(1)} %get-tuple-element.56), channel_id=1, source_target_pairs={{0,4},{4,8},{8,12},{12,16},{16,20},{20,24},{24,28},{1,5},{5,9},{9,... | collective-permute-start | bytes 589832 | tf_op jit(solution)/shard_map/ppermute | solution.py:592
  28.5 1.3 %collective-permute-start.11 = (bf16[768,128]{1,0:T(8,128)(2,1)S(1)}, bf16[768,128]{1,0:T(8,128)(2,1)S(1)}, u32[]{:S(2)}, u32[]{:S(2)}) collective-permute-start(bf16[768,128]{1,0:T(8,128)(2,1)S(1)} %get-tuple-element.57), channel_id=1, source_target_pairs={{4,0},{8,4},{12,8},{16,12},{20,16},{24,20},{28,24},{5,1},{9,5},{13... | collective-permute-start | bytes 589832 | tf_op jit(solution)/shard_map/ppermute | solution.py:593
  29.8 0.0 collective-permute-done.10.left_ref
  29.8 2.5 %collective-permute-done.11.right_ref = bf16[768,128]{1,0:T(8,128)(2,1)S(1)} collective-permute-done((bf16[768,128]{1,0:T(8,128)(2,1)S(1)}, bf16[768,128]{1,0:T(8,128)(2,1)S(1)}, u32[]{:S(2)}, u32[]{:S(2)}) %collective-permute-start.11) | collective-permute-done | bytes 196640 | tf_op jit(solution)/shard_map/ppermute | solution.py:593
  32.3 5.2 %collective-permute-done.9.came_h.refs_3_ = bf16[128,2048]{1,0:T(8,128)(2,1)S(1)} collective-permute-done((bf16[128,2048]{1,0:T(8,128)(2,1)S(1)}, bf16[128,2048]{1,0:T(8,128)(2,1)S(1)}, u32[]{:S(2)}, u32[]{:S(2)}) %collective-permute-start.9) | collective-permute-done | bytes 524320 | tf_op jit(solution)/shard_map/ppermute | solution.py:588
  37.5 0.0 collective-permute-done.12.inner_h.refs_2_
  37.5 0.1 choose_sent.3
  37.6 0.0 copy-start.1
  37.6 3.7 %collective-permute-start.13 = (bf16[128,2048]{1,0:T(8,128)(2,1)S(1)}, bf16[128,2048]{1,0:T(8,128)(2,1)S(1)}, u32[]{:S(2)}, u32[]{:S(2)}) collective-permute-start(bf16[128,2048]{1,0:T(8,128)(2,1)S(1)} %choose_sent.3), channel_id=1, source_target_pairs={{0,1},{3,2},{1,0},{2,3},{4,5},{7,6},{5,4},{6,7},{8,9},{11,10},{9,8... | collective-permute-start | bytes 1572872 | tf_op jit(solution)/shard_map/ppermute | solution.py:601
  41.3 0.7 collective-permute-start.18
  42.0 0.2 assemble_tokens.1.x_ref.refs_8_
  42.1 10.6 %collective-permute-done.13.refs_0_.refs_9_ = bf16[128,2048]{1,0:T(8,128)(2,1)S(1)} collective-permute-done((bf16[128,2048]{1,0:T(8,128)(2,1)S(1)}, bf16[128,2048]{1,0:T(8,128)(2,1)S(1)}, u32[]{:S(2)}, u32[]{:S(2)}) %collective-permute-start.13) | collective-permute-done | bytes 524320 | tf_op jit(solution)/shard_map/ppermute | solution.py:601
  52.7 0.0 copy-done.1
  52.7 2.2 %weight_gradient.1 = (f32[16,128,128]{2,1,0:T(8,128)S(1)}, bf16[16,128,128]{2,1,0:T(8,128)(2,1)S(1)}) custom-call(s32[32,128]{1,0:T(8,128)S(1)} %get-tuple-element.78.meta_s, bf16[128,7168]{1,0:T(8,128)(2,1)S(1)} %copy-done.1, bf16[4,128,2048]{2,1,0:T(8,128)(2,1)S(1)} %assemble_tokens.1.x_ref.refs_8_, ...), custom_call_target="tpu_custom_call" | custom-call | tf_op jit(solution)/shard_map/weight_gradient/pallas_call | solution.py:401
  55.0 0.1 collective-permute-start.14
  55.0 0.1 add_convert_fusion.1
  55.2 0.0 collective-permute-done.18
  55.2 0.1 add_convert_fusion
  55.3 1.8 %collective-permute-start.19 = (bf16[128,2048]{1,0:T(8,128)(2,1)S(1)}, bf16[128,2048]{1,0:T(8,128)(2,1)S(1)}, u32[]{:S(2)}, u32[]{:S(2)}) collective-permute-start(bf16[128,2048]{1,0:T(8,128)(2,1)S(1)} %add_convert_fusion), channel_id=1, source_target_pairs={{0,1},{3,2},{1,0},{2,3},{4,5},{7,6},{5,4},{6,7},{8,9},{11,10},{9,8... | collective-permute-start | bytes 1572872 | tf_op jit(solution)/shard_map/ppermute | solution.py:616
  57.1 0.7 collective-permute-start.20
  57.8 0.0 collective-permute-done.14
  57.8 0.2 fusion
  58.1 0.9 %collective-permute-start.15 = (bf16[4,128,128]{2,1,0:T(8,128)(2,1)S(1)}, bf16[4,128,128]{2,1,0:T(8,128)(2,1)S(1)}, u32[]{:S(2)}, u32[]{:S(2)}) collective-permute-start(bf16[4,128,128]{2,1,0:T(8,128)(2,1)S(1)} %get-tuple-element.85), channel_id=1, source_target_pairs={{0,8},{4,12},{8,0},{12,4},{16,24},{20,28},{24,16},{28,20},{1,9},{5... | collective-permute-start | bytes 393224 | tf_op jit(solution)/shard_map/ppermute | solution.py:424
  59.0 0.8 %collective-permute-start.16 = (bf16[4,128,128]{2,1,0:T(8,128)(2,1)S(1)}, bf16[4,128,128]{2,1,0:T(8,128)(2,1)S(1)}, u32[]{:S(2)}, u32[]{:S(2)}) collective-permute-start(bf16[4,128,128]{2,1,0:T(8,128)(2,1)S(1)} %get-tuple-element.84), channel_id=1, source_target_pairs={{0,16},{4,20},{8,24},{12,28},{16,0},{20,4},{24,8},{28,12},{1,17},{... | collective-permute-start | bytes 393224 | tf_op jit(solution)/shard_map/ppermute | solution.py:424
  59.8 1.8 %collective-permute-start.17 = (bf16[4,128,128]{2,1,0:T(8,128)(2,1)S(1)}, bf16[4,128,128]{2,1,0:T(8,128)(2,1)S(1)}, u32[]{:S(2)}, u32[]{:S(2)}) collective-permute-start(bf16[4,128,128]{2,1,0:T(8,128)(2,1)S(1)} %get-tuple-element.83), channel_id=1, source_target_pairs={{0,24},{4,28},{8,16},{12,20},{16,8},{20,12},{24,0},{28,4},{1,25},{... | collective-permute-start | bytes 393224 | tf_op jit(solution)/shard_map/ppermute | solution.py:424
  61.6 3.7 %hidden_out.1 = bf16[128,7168]{1,0:T(8,128)(2,1)} custom-call(s32[32,128]{1,0:T(8,128)S(1)} %get-tuple-element.78.meta_s, bf16[576,128]{1,0:T(8,128)(2,1)S(1)} %get-tuple-element.44.refs_0_, bf16[576,128]{1,0:T(8,128)(2,1)S(1)} %collective-permute-done.refs_1_, bf16[576,128]{1,0:T(8,128)(2,1)S(1)} %collective-permute-done.1.refs_2_, ...), custom_call_target="tpu_custom_call" | custom-call | tf_op jit(solution)/shard_map/hidden_out/pallas_call | solution.py:450
  65.3 0.0 collective-permute-done.15.refs_1_
  65.3 0.0 collective-permute-done.16.refs_2_
  65.3 1.8 %collective-permute-done.17.refs_3_ = bf16[4,128,128]{2,1,0:T(8,128)(2,1)S(1)} collective-permute-done((bf16[4,128,128]{2,1,0:T(8,128)(2,1)S(1)}, bf16[4,128,128]{2,1,0:T(8,128)(2,1)S(1)}, u32[]{:S(2)}, u32[]{:S(2)}) %collective-permute-start.17) | collective-permute-done | bytes 131104 | tf_op jit(solution)/shard_map/ppermute | solution.py:424
  67.1 2.0 %adam_update.1 = (bf16[4,128,128]{2,1,0:T(8,128)(2,1)}, f32[4,128,128]{2,1,0:T(8,128)}, f32[4,128,128]{2,1,0:T(8,128)}) custom-call(s32[32,128]{1,0:T(8,128)S(1)} %get-tuple-element.78.meta_s, bf16[4,128,128]{2,1,0:T(8,128)(2,1)S(1)} %copy-done.2, f32[4,128,128]{2,1,0:T(8,128)S(1)} %copy-done.3, f32[4,128,128]{2,1,0:T(8,128)S(1)} %copy-done.4, ...), custom_call_target="tpu_custom_call" | custom-call | tf_op jit(solution)/shard_map/adam_update/pallas_call | solution.py:542
  69.2 0.6 collective-permute-done.19.first_ref
  69.7 0.0 collective-permute-done.20.second_ref
  69.7 0.9 %finish_input_grad.1 = bf16[128,2048]{1,0:T(8,128)(2,1)} custom-call(f32[128,2048]{1,0:T(8,128)S(1)} %get-tuple-element.80.own_ref, bf16[128,2048]{1,0:T(8,128)(2,1)S(1)} %collective-permute-done.19.first_ref, bf16[128,2048]{1,0:T(8,128)(2,1)S(1)} %collective-permute-done.20.second_ref), custom_call_target="tpu_custom_call" | custom-call | tf_op jit(solution)/shard_map/finish_input_grad/pallas_call | solution.py:468
  (11 shorter events, 0.1 us)
Async XLA Ops:
  0.6 20.0 %collective-permute-start.7 = (bf16[128,2048]{1,0:T(8,128)(2,1)}, bf16[128,2048]{1,0:T(8,128)(2,1)S(1)}, u32[]{:S(2)}, u32[]{:S(2)}) collective-permute-start(bf16[128,2048]{1,0:T(8,128)(2,1)} %own_h), channel_id=1, source_target_pairs={{0,1},{1,0},{2,3},{3,2},{4,5},{5,4},{6,7},{7,6},{8,9},{9,8},{10,11... | collective-permute-start | bytes 1572872 | tf_op jit(solution)/shard_map/ppermute | solution.py:567
  3.7 16.9 %collective-permute-start.8 = (bf16[128,2048]{1,0:T(8,128)(2,1)}, bf16[128,2048]{1,0:T(8,128)(2,1)S(1)}, u32[]{:S(2)}, u32[]{:S(2)}) collective-permute-start(bf16[128,2048]{1,0:T(8,128)(2,1)} %own_h), channel_id=1, source_target_pairs={{1,2},{2,1},{5,6},{6,5},{9,10},{10,9},{13,14},{14,13},{17,18},{18,... | collective-permute-start | bytes 1572872 | tf_op jit(solution)/shard_map/ppermute | solution.py:568
  6.0 6.4 %collective-permute-start = (bf16[576,128]{1,0:T(8,128)(2,1)}, bf16[576,128]{1,0:T(8,128)(2,1)S(1)}, u32[]{:S(2)}, u32[]{:S(2)}) collective-permute-start(bf16[576,128]{1,0:T(8,128)(2,1)} %pack_blocks.1.refs_1_), channel_id=1, source_target_pairs={{0,8},{4,12},{8,0},{12,4},{16,24},{20,28},{24,16},{28,20},{1,9},{5... | collective-permute-start | bytes 442376 | tf_op jit(solution)/shard_map/ppermute | solution.py:572
  7.6 8.5 %collective-permute-start.1 = (bf16[576,128]{1,0:T(8,128)(2,1)}, bf16[576,128]{1,0:T(8,128)(2,1)S(1)}, u32[]{:S(2)}, u32[]{:S(2)}) collective-permute-start(bf16[576,128]{1,0:T(8,128)(2,1)} %pack_blocks.1.refs_1_), channel_id=1, source_target_pairs={{0,16},{4,20},{8,24},{12,28},{16,0},{20,4},{24,8},{28,12},{1,17},{... | collective-permute-start | bytes 442376 | tf_op jit(solution)/shard_map/ppermute | solution.py:572
  9.1 7.0 %collective-permute-start.2 = (bf16[576,128]{1,0:T(8,128)(2,1)}, bf16[576,128]{1,0:T(8,128)(2,1)S(1)}, u32[]{:S(2)}, u32[]{:S(2)}) collective-permute-start(bf16[576,128]{1,0:T(8,128)(2,1)} %pack_blocks.1.refs_1_), channel_id=1, source_target_pairs={{0,24},{4,28},{8,16},{12,20},{16,8},{20,12},{24,0},{28,4},{1,25},{... | collective-permute-start | bytes 442376 | tf_op jit(solution)/shard_map/ppermute | solution.py:572
  9.6 1.5 %copy-start = (bf16[128,7168]{1,0:T(8,128)(2,1)S(1)}, bf16[128,7168]{1,0:T(8,128)(2,1)}, u32[]{:S(2)}) copy-start(bf16[128,7168]{1,0:T(8,128)(2,1)} %up_ref.1) | copy-start | bytes 5505028
  11.1 0.9 %copy-start.5 = (bf16[576,128]{1,0:T(8,128)(2,1)S(1)}, bf16[576,128]{1,0:T(8,128)(2,1)}, u32[]{:S(2)}) copy-start(bf16[576,128]{1,0:T(8,128)(2,1)} %pack_blocks.1.refs_1_) | copy-start | bytes 442372
  12.4 4.3 %collective-permute-start.3 = (bf16[576,128]{1,0:T(8,128)(2,1)S(1)}, bf16[576,128]{1,0:T(8,128)(2,1)S(1)}, u32[]{:S(2)}, u32[]{:S(2)}) collective-permute-start(bf16[576,128]{1,0:T(8,128)(2,1)S(1)} %get-tuple-element.44.refs_0_), channel_id=1, source_target_pairs={{0,4},{4,0},{8,12},{12,8},{16,20},{20,16},{24,28},{28,24},{1,5},{5... | collective-permute-start | bytes 442376 | tf_op jit(solution)/shard_map/ppermute | solution.py:577
  16.1 9.8 %copy-start.2 = (bf16[4,128,128]{2,1,0:T(8,128)(2,1)S(1)}, bf16[4,128,128]{2,1,0:T(8,128)(2,1)}, u32[]{:S(2)}) copy-start(bf16[4,128,128]{2,1,0:T(8,128)(2,1)} %w_ref.1) | copy-start | bytes 393220
  16.1 9.8 %copy-start.3 = (f32[4,128,128]{2,1,0:T(8,128)S(1)}, f32[4,128,128]{2,1,0:T(8,128)}, u32[]{:S(2)}) copy-start(f32[4,128,128]{2,1,0:T(8,128)} %one_ref.1) | copy-start | bytes 786436
  16.1 9.8 %copy-start.4 = (f32[4,128,128]{2,1,0:T(8,128)S(1)}, f32[4,128,128]{2,1,0:T(8,128)}, u32[]{:S(2)}) copy-start(f32[4,128,128]{2,1,0:T(8,128)} %two_ref.1) | copy-start | bytes 786436
  16.1 9.8 %copy-start.7 = (s32[4]{0:T(128)S(1)}, s32[4]{0:T(128)}, u32[]{:S(2)}) copy-start(s32[4]{0:T(128)} %dest_h.2) | copy-start | bytes 52
  16.1 1.4 %collective-permute-start.4 = (bf16[576,128]{1,0:T(8,128)(2,1)S(1)}, bf16[576,128]{1,0:T(8,128)(2,1)S(1)}, u32[]{:S(2)}, u32[]{:S(2)}) collective-permute-start(bf16[576,128]{1,0:T(8,128)(2,1)S(1)} %collective-permute-done.refs_1_), channel_id=1, source_target_pairs={{0,4},{4,0},{8,12},{12,8},{16,20},{20,16},{24,28},{28,24},{1,5},{5... | collective-permute-start | bytes 442376 | tf_op jit(solution)/shard_map/ppermute | solution.py:577
  16.2 1.6 %collective-permute-start.5 = (bf16[576,128]{1,0:T(8,128)(2,1)S(1)}, bf16[576,128]{1,0:T(8,128)(2,1)S(1)}, u32[]{:S(2)}, u32[]{:S(2)}) collective-permute-start(bf16[576,128]{1,0:T(8,128)(2,1)S(1)} %collective-permute-done.1.refs_2_), channel_id=1, source_target_pairs={{0,4},{4,0},{8,12},{12,8},{16,20},{20,16},{24,28},{28,24},{1,5},{5... | collective-permute-start | bytes 442376 | tf_op jit(solution)/shard_map/ppermute | solution.py:577
  16.7 1.4 %collective-permute-start.6 = (bf16[576,128]{1,0:T(8,128)(2,1)S(1)}, bf16[576,128]{1,0:T(8,128)(2,1)S(1)}, u32[]{:S(2)}, u32[]{:S(2)}) collective-permute-start(bf16[576,128]{1,0:T(8,128)(2,1)S(1)} %collective-permute-done.2.refs_3_), channel_id=1, source_target_pairs={{0,4},{4,0},{8,12},{12,8},{16,20},{20,16},{24,28},{28,24},{1,5},{5... | collective-permute-start | bytes 442376 | tf_op jit(solution)/shard_map/ppermute | solution.py:577
  20.7 16.7 %collective-permute-start.9 = (bf16[128,2048]{1,0:T(8,128)(2,1)S(1)}, bf16[128,2048]{1,0:T(8,128)(2,1)S(1)}, u32[]{:S(2)}, u32[]{:S(2)}) collective-permute-start(bf16[128,2048]{1,0:T(8,128)(2,1)S(1)} %choose_sent.2), channel_id=1, source_target_pairs={{0,1},{3,2},{1,0},{2,3},{4,5},{7,6},{5,4},{6,7},{8,9},{11,10},{9,8... | collective-permute-start | bytes 1572872 | tf_op jit(solution)/shard_map/ppermute | solution.py:588
  25.2 12.3 %collective-permute-start.12 = (bf16[128,2048]{1,0:T(8,128)(2,1)S(1)}, bf16[128,2048]{1,0:T(8,128)(2,1)S(1)}, u32[]{:S(2)}, u32[]{:S(2)}) collective-permute-start(bf16[128,2048]{1,0:T(8,128)(2,1)S(1)} %collective-permute-done.7.refs_0_), channel_id=1, source_target_pairs={{1,2},{2,1},{5,6},{6,5},{9,10},{10,9},{13,14},{14,13},{17,18},{18,... | collective-permute-start | bytes 1572872 | tf_op jit(solution)/shard_map/ppermute | solution.py:589
  25.9 16.0 %copy-start.6 = (bf16[128,2048]{1,0:T(8,128)(2,1)S(1)}, bf16[128,2048]{1,0:T(8,128)(2,1)}, u32[]{:S(2)}) copy-start(bf16[128,2048]{1,0:T(8,128)(2,1)} %own_h) | copy-start | bytes 1572868
  26.6 3.2 %collective-permute-start.10 = (bf16[768,128]{1,0:T(8,128)(2,1)S(1)}, bf16[768,128]{1,0:T(8,128)(2,1)S(1)}, u32[]{:S(2)}, u32[]{:S(2)}) collective-permute-start(bf16[768,128]{1,0:T(8,128)(2,1)S(1)} %get-tuple-element.56), channel_id=1, source_target_pairs={{0,4},{4,8},{8,12},{12,16},{16,20},{20,24},{24,28},{1,5},{5,9},{9,... | collective-permute-start | bytes 589832 | tf_op jit(solution)/shard_map/ppermute | solution.py:592
  28.5 3.9 %collective-permute-start.11 = (bf16[768,128]{1,0:T(8,128)(2,1)S(1)}, bf16[768,128]{1,0:T(8,128)(2,1)S(1)}, u32[]{:S(2)}, u32[]{:S(2)}) collective-permute-start(bf16[768,128]{1,0:T(8,128)(2,1)S(1)} %get-tuple-element.57), channel_id=1, source_target_pairs={{4,0},{8,4},{12,8},{16,12},{20,16},{24,20},{28,24},{5,1},{9,5},{13... | collective-permute-start | bytes 589832 | tf_op jit(solution)/shard_map/ppermute | solution.py:593
  37.6 15.1 %copy-start.1 = (bf16[128,7168]{1,0:T(8,128)(2,1)S(1)}, bf16[128,7168]{1,0:T(8,128)(2,1)}, u32[]{:S(2)}) copy-start(bf16[128,7168]{1,0:T(8,128)(2,1)} %up_ref.1) | copy-start | bytes 5505028
  37.6 15.1 %collective-permute-start.13 = (bf16[128,2048]{1,0:T(8,128)(2,1)S(1)}, bf16[128,2048]{1,0:T(8,128)(2,1)S(1)}, u32[]{:S(2)}, u32[]{:S(2)}) collective-permute-start(bf16[128,2048]{1,0:T(8,128)(2,1)S(1)} %choose_sent.3), channel_id=1, source_target_pairs={{0,1},{3,2},{1,0},{2,3},{4,5},{7,6},{5,4},{6,7},{8,9},{11,10},{9,8... | collective-permute-start | bytes 1572872 | tf_op jit(solution)/shard_map/ppermute | solution.py:601
  41.3 13.9 %collective-permute-start.18 = (bf16[128,2048]{1,0:T(8,128)(2,1)S(1)}, bf16[128,2048]{1,0:T(8,128)(2,1)S(1)}, u32[]{:S(2)}, u32[]{:S(2)}) collective-permute-start(bf16[128,2048]{1,0:T(8,128)(2,1)S(1)} %inner_sum.1), channel_id=1, source_target_pairs={{1,2},{2,1},{5,6},{6,5},{9,10},{10,9},{13,14},{14,13},{17,18},{18,... | collective-permute-start | bytes 1572872 | tf_op jit(solution)/shard_map/ppermute | solution.py:602
  55.0 2.9 %collective-permute-start.14 = (bf16[16,128,128]{2,1,0:T(8,128)(2,1)S(1)}, bf16[16,128,128]{2,1,0:T(8,128)(2,1)S(1)}, u32[]{:S(2)}, u32[]{:S(2)}) collective-permute-start(bf16[16,128,128]{2,1,0:T(8,128)(2,1)S(1)} %get-tuple-element.69), channel_id=1, source_target_pairs={{0,4},{4,0},{8,12},{12,8},{16,20},{20,16},{24,28},{28,24},{1,5},{5... | collective-permute-start | bytes 1572872 | tf_op jit(solution)/shard_map/ppermute | solution.py:417
  55.3 14.4 %collective-permute-start.19 = (bf16[128,2048]{1,0:T(8,128)(2,1)S(1)}, bf16[128,2048]{1,0:T(8,128)(2,1)S(1)}, u32[]{:S(2)}, u32[]{:S(2)}) collective-permute-start(bf16[128,2048]{1,0:T(8,128)(2,1)S(1)} %add_convert_fusion), channel_id=1, source_target_pairs={{0,1},{3,2},{1,0},{2,3},{4,5},{7,6},{5,4},{6,7},{8,9},{11,10},{9,8... | collective-permute-start | bytes 1572872 | tf_op jit(solution)/shard_map/ppermute | solution.py:616
  57.1 12.6 %collective-permute-start.20 = (bf16[128,2048]{1,0:T(8,128)(2,1)S(1)}, bf16[128,2048]{1,0:T(8,128)(2,1)S(1)}, u32[]{:S(2)}, u32[]{:S(2)}) collective-permute-start(bf16[128,2048]{1,0:T(8,128)(2,1)S(1)} %add_convert_fusion.1), channel_id=1, source_target_pairs={{1,2},{2,1},{5,6},{6,5},{9,10},{10,9},{13,14},{14,13},{17,18},{18,... | collective-permute-start | bytes 1572872 | tf_op jit(solution)/shard_map/ppermute | solution.py:615
  58.1 7.2 %collective-permute-start.15 = (bf16[4,128,128]{2,1,0:T(8,128)(2,1)S(1)}, bf16[4,128,128]{2,1,0:T(8,128)(2,1)S(1)}, u32[]{:S(2)}, u32[]{:S(2)}) collective-permute-start(bf16[4,128,128]{2,1,0:T(8,128)(2,1)S(1)} %get-tuple-element.85), channel_id=1, source_target_pairs={{0,8},{4,12},{8,0},{12,4},{16,24},{20,28},{24,16},{28,20},{1,9},{5... | collective-permute-start | bytes 393224 | tf_op jit(solution)/shard_map/ppermute | solution.py:424
  59.0 6.3 %collective-permute-start.16 = (bf16[4,128,128]{2,1,0:T(8,128)(2,1)S(1)}, bf16[4,128,128]{2,1,0:T(8,128)(2,1)S(1)}, u32[]{:S(2)}, u32[]{:S(2)}) collective-permute-start(bf16[4,128,128]{2,1,0:T(8,128)(2,1)S(1)} %get-tuple-element.84), channel_id=1, source_target_pairs={{0,16},{4,20},{8,24},{12,28},{16,0},{20,4},{24,8},{28,12},{1,17},{... | collective-permute-start | bytes 393224 | tf_op jit(solution)/shard_map/ppermute | solution.py:424
  59.8 7.3 %collective-permute-start.17 = (bf16[4,128,128]{2,1,0:T(8,128)(2,1)S(1)}, bf16[4,128,128]{2,1,0:T(8,128)(2,1)S(1)}, u32[]{:S(2)}, u32[]{:S(2)}) collective-permute-start(bf16[4,128,128]{2,1,0:T(8,128)(2,1)S(1)} %get-tuple-element.83), channel_id=1, source_target_pairs={{0,24},{4,28},{8,16},{12,20},{16,8},{20,12},{24,0},{28,4},{1,25},{... | collective-permute-start | bytes 393224 | tf_op jit(solution)/shard_map/ppermute | solution.py:424

commit v5 on v4

--- a/solution.py
+++ b/solution.py
@@ -22,7 +22,6 @@
 VMEM = pl.BlockSpec(memory_space=pltpu.VMEM)
 ANY = pl.BlockSpec(memory_space=pl.ANY)
 SMEM = pl.BlockSpec(memory_space=pltpu.SMEM)
-HBM = pl.BlockSpec(memory_space=pltpu.HBM)
 
 
 def params(mib=24):
@@ -164,18 +163,17 @@
 def backward_kernel(kept, ids, slices, *refs):
     count = len(ids)
     packs, up_ref = refs[:count], refs[count]
-    acc, meta_s, *held, sems = refs[-3 - slices :]
-    refs = refs[count + 1 : -3 - slices]
-    shares, meta_ref = refs[:slices], refs[slices]
-    side = meta_ref.shape[1]
+    acc, meta_ref, *far_ref = refs[count + 1 : -2]
+    meta_s, sem = refs[-2:]
+    side = packs[0].shape[1]
     pitch = side + TILE
-    width = shares[0].shape[1]
+    width = acc.shape[1] // slices
     for at, ident in enumerate(ids):
         for s in range(kept):
             tile = packs[at][s * pitch + side : (s + 1) * pitch, :].astype(f32)
             row = ident * kept + s
             meta_ref[row : row + 1, :] = tile[0:1, :].astype(jnp.int32)
-    copy = pltpu.make_async_copy(meta_ref, meta_s, sems.at[slices])
+    copy = pltpu.make_async_copy(meta_ref, meta_s, sem)
     copy.start()
     acc[...] = jnp.zeros_like(acc)
     copy.wait()
@@ -191,14 +189,29 @@
             )
             place = pl.ds(pl.multiple_of(row * side, side), side)
             acc[:, place] = acc[:, place] + part
+    for ref in far_ref:
+        far = share_order(lax.axis_index("mp"), slices)[1]
+        ref[...] = (lanes(acc, far, width) * grad_scale).astype(bf16)
+
+
+def split_kernel(slices, chosen, acc, *shares):
+    width = acc.shape[1] // slices
     order = share_order(lax.axis_index("mp"), slices)
-    copies = [pltpu.make_async_copy(held[k], shares[k], sems.at[k]) for k in range(slices)]
-    for k, quarter in enumerate(order):
-        share = lanes(acc, quarter, width) * grad_scale
-        held[k][...] = share.astype(held[k].dtype)
-        copies[k].start()
-    for copy in copies:
-        copy.wait()
+    for ref, k in zip(shares, chosen):
+        ref[...] = (lanes(acc, order[k], width) * grad_scale).astype(ref.dtype)
+
+
+def split(acc, slices, chosen):
+    shape = (acc.shape[0], acc.shape[1] // slices)
+    return pl.pallas_call(
+        functools.partial(split_kernel, slices, chosen),
+        out_shape=tuple(jax.ShapeDtypeStruct(shape, bf16 if k else f32) for k in chosen),
+        in_specs=[VMEM],
+        out_specs=(VMEM,) * len(chosen),
+        compiler_params=params(),
+        cost_estimate=pl.CostEstimate(flops=0, bytes_accessed=0, transcendentals=0),
+        name="split_shares",
+    )(acc)
 
 
 def share_order(me, slices):
@@ -212,25 +225,21 @@
     tokens = upstream.shape[0]
     side = packs[0].shape[1]
     blocks = len(ids) * kept
-    shares = [
-        jax.ShapeDtypeStruct((tokens, features), f32 if k == 0 else bf16) for k in range(slices)
-    ]
-    outs = pl.pallas_call(
+    far = [jax.ShapeDtypeStruct((tokens, features), bf16)] * (slices == 4)
+    return pl.pallas_call(
         functools.partial(backward_kernel, kept, ids, slices),
-        out_shape=(*shares, jax.ShapeDtypeStruct((blocks, side), jnp.int32)),
+        out_shape=(
+            jax.ShapeDtypeStruct((tokens, slices * features), f32),
+            jax.ShapeDtypeStruct((blocks, side), jnp.int32),
+            *far,
+        ),
         in_specs=[VMEM] * (len(ids) + 1),
-        out_specs=(HBM,) * slices + (VMEM,),
-        scratch_shapes=[
-            pltpu.VMEM((tokens, slices * features), f32),
-            pltpu.SMEM((blocks, side), jnp.int32),
-            *(pltpu.VMEM(share.shape, share.dtype) for share in shares),
-            pltpu.SemaphoreType.DMA((slices + 1,)),
-        ],
+        out_specs=(VMEM,) * (2 + len(far)),
+        scratch_shapes=[pltpu.SMEM((blocks, side), jnp.int32), pltpu.SemaphoreType.DMA],
         compiler_params=params(),
         cost_estimate=pl.CostEstimate(flops=0, bytes_accessed=0, transcendentals=0),
         name="input_gradient",
     )(*packs, upstream)
-    return outs[:slices], outs[slices]
 
 
 def line_reduce(shares, axis):
@@ -371,51 +380,64 @@
     return block
 
 
-def gradient_kernel(kept, dp, meta_s, up_ref, x_ref, *refs):
-    last, (keep_ref, send_ref, store) = refs[:-3], refs[-3:]
-    side = keep_ref.shape[2]
+def turn_kernel(meta_s, up_ref, turned_ref):
+    side = turned_ref.shape[1]
+    for b in range(turned_ref.shape[0]):
+        turned_ref[b] = jnp.transpose(lanes(up_ref, meta_s[b, 1], side))
+
+
+def turn(meta, upstream):
+    blocks, side = meta.shape
+    return pl.pallas_call(
+        turn_kernel,
+        out_shape=jax.ShapeDtypeStruct((blocks, side, upstream.shape[0]), bf16),
+        in_specs=[SMEM, VMEM],
+        out_specs=VMEM,
+        compiler_params=params(),
+        cost_estimate=pl.CostEstimate(flops=0, bytes_accessed=0, transcendentals=0),
+        name="turn_upstream",
+    )(meta, upstream)
+
+
+def gradient_kernel(kept, dp, meta_s, turned_ref, x_ref, *refs):
+    last, (store, send_ref) = refs[:-2], refs[-2:]
+    side = store.shape[2]
     blocks = dp * kept
+    half = blocks // 2
     me = lax.axis_index("dp")
-    store[0:blocks] = jnp.zeros((blocks, side, side), f32)
     for b in range(blocks):
-        row, col, dest = meta_s[b, 0], meta_s[b, 1], meta_s[b, 2]
-        grad = lax.dot_general(
-            token_block(x_ref, last, row, side),
-            lanes(up_ref, col, side),
-            (((0,), (0,)), ((), ())),
-            preferred_element_type=f32,
+        row, dest = meta_s[b, 0], meta_s[b, 2]
+        grad = jnp.dot(
+            turned_ref[b], token_block(x_ref, last, row, side), preferred_element_type=f32
         )
         gap = jnp.bitwise_xor(jnp.maximum(dest, 0) // kept, me)
         place = (gap & 1) * (dp // 2) + lax.shift_right_logical(gap, 1)
         slot = jnp.where(dest >= 0, place * kept + jnp.maximum(dest, 0) % kept, blocks)
         store[slot] = grad * grad_scale
-    half = keep_ref.shape[0]
-    keep_ref[...] = store[0:half]
     send_ref[...] = store[half : 2 * half].astype(bf16)
 
 
-def gradient(meta, x_all, last, upstream, kept, dp):
+def gradient(meta, x_all, last, turned, kept, dp):
     side = meta.shape[1]
     blocks = dp * kept
     half = blocks // 2
     return pl.pallas_call(
         functools.partial(gradient_kernel, kept, dp),
         out_shape=(
-            jax.ShapeDtypeStruct((half, side, side), f32),
+            jax.ShapeDtypeStruct((blocks + 1, side, side), f32),
             jax.ShapeDtypeStruct((half, side, side), bf16),
         ),
         in_specs=[SMEM] + [VMEM] * (2 + len(last)),
         out_specs=(VMEM, VMEM),
-        scratch_shapes=[pltpu.VMEM((blocks + 1, side, side), f32)],
         compiler_params=params(),
         cost_estimate=pl.CostEstimate(flops=0, bytes_accessed=0, transcendentals=0),
         name="weight_gradient",
-    )(meta, upstream, x_all, *last)
+    )(meta, turned, x_all, *last)
 
 
 def slot_reduce(keep, send, kept, dp):
     came = lax.ppermute(send, "dp", [(i, i ^ 1) for i in range(dp)])
-    total = keep + came.astype(f32)
+    total = keep[: send.shape[0]] + came.astype(f32)
     totals = [total[:kept]]
     for gap in range(1, dp // 2):
         totals.append(total[gap * kept : (gap + 1) * kept].astype(bf16))
@@ -506,6 +528,7 @@
             grad = parts[0][q]
             for part in parts[1:]:
                 grad = grad + part[q].astype(f32)
+            grad = jnp.transpose(grad)
             first = beta_first * one + (1.0 - beta_first) * grad
             second = beta_second * two + (1.0 - beta_second) * grad * grad
             stepped = weight - learn_rate * first / (jnp.sqrt(second) + epsilon)
@@ -576,18 +599,18 @@
     packs[1:] = lax.optimization_barrier((*packs[1:], *held))[: len(packs) - 1]
     packs += [lax.ppermute(p, "dp", [(i, i ^ 1) for i in range(dp)]) for p in packs]
     ids = tuple(ids + [i ^ 1 for i in ids])
-    shares, meta = backward(packs, ids, up_held, kept, slices, tokens.shape[1])
+    sums, meta, *far = backward(packs, ids, up_held, kept, slices, tokens.shape[1])
 
     dest_leave = dest_slot
     if four:
         outer = lax.rem(lax.axis_index("mp"), 3) == 0
-        own_share, far, second, first = shares
-        near, middle, far = lax.optimization_barrier((near, middle, far))
-        mixed = choose(far, middle)
-        near, mixed = lax.optimization_barrier((near, mixed))
+        near, middle, far = lax.optimization_barrier((near, middle, far[0]))
+        mixed_sent = choose(far, middle)
+        near, mixed = lax.optimization_barrier((near, mixed_sent))
         mixed = lax.ppermute(mixed, "mp", inward + outward)
         near_on = lax.ppermute(near, "mp", inner)
-        dest_leave = after(dest_slot, meta)
+        own_share, second, first = split(after(sums, mixed_sent), slices, (0, 2, 3))
+        dest_leave = after(dest_slot, own_share)
     to_left, to_right = leave(dest_leave, weight, moment_one, moment_two)
     from_left = lax.ppermute(to_right, "dp", [(i, i + 1) for i in range(dp - 1)])
     from_right = lax.ppermute(to_left, "dp", [(i + 1, i) for i in range(dp - 1)])
@@ -602,10 +625,12 @@
         passed_far = lax.ppermute(sum_far, "mp", inner)
         came = (near, middle, near_on, mixed)
         x_all = assemble(after(tokens, sum_far), came, slices)
+        turned = turn(after(meta, x_all), upstream)
         last = (mixed_on,)
     else:
         x_all, last = assemble(tokens, came, slices), ()
-    keep, send = gradient(meta, x_all, last, upstream, kept, dp)
+        turned = turn(meta, upstream)
+    keep, send = gradient(meta, x_all, last, turned, kept, dp)
     parts, totals = slot_reduce(keep, send, kept, dp)
     meta_out = meta
     if four:
@@ -624,7 +649,7 @@
             after(own_share, hidden_out, new_weight), came_first, passed_second
         )
     else:
-        input_grad = line_reduce(shares, "mp")
+        input_grad = line_reduce(split(sums, slices, tuple(range(slices))), "mp")
     return (new_weight, new_first, new_second, hidden_out, input_grad)
 
 

time: 71.6 us -> 70.5 us (0.985)
  waiting for transfers between devices: 25.7 us -> 23.5 us
  local copies, waits for them, and re-layouts: 2.48 us -> 3.26 us
    pallas_call x0 -> x2, Pallas kernels: none -> 1.39 us  [the longest x1 1.13 us: turn(): pl.pallas_call(turn_kernel, out_shape=jax.ShapeDtypeStruct((blocks, side,...]
    ppermute x1, waiting for transfers between devices: 10.6 us -> 9.44 us  [body(): mixed_on = lax.ppermute(mixed_on, 'mp', inward + outward)]
    ppermute x1, waiting for transfers between devices: 5.15 us -> 4.09 us  [body(): mixed = lax.ppermute(mixed, 'mp', inward + outward)]
    unnamed x16, local copies, waits for them, and re-layouts: 2.44 us -> 3.22 us
  transfers between devices with their start and end apart: 21 -> 21, of which waited for: 10 -> 9; matrix products, arithmetic and copies ran while one was open for 1% -> 1% of each run, Pallas kernels for 19% -> 20%
where the time goes in v5:
time: 70.5 us; the launch traced here: 69.8 us
  starting transfers between devices  26.7 us (38%)
  waiting for transfers between devices  23.5 us (33%)
  Pallas kernels  15 us (21%)
  local copies, waits for them, and re-layouts  3.26 us (5%)
  between operations  0.94 us (1%)
    ppermute x1, waiting for transfers between devices, body(): mixed_on = lax.ppermute(mixed_on, 'mp', inward + outward)  9.44 us
    ppermute x1, starting transfers between devices, body(): mixed = lax.ppermute(mixed, 'mp', inward + outward)  4.44 us
    ppermute x1, waiting for transfers between devices, body(): mixed = lax.ppermute(mixed, 'mp', inward + outward)  4.09 us
    ppermute x3, waiting for transfers between devices, body(): lax.ppermute(packs[0], 'dp', [(i, i ^ gap) for i in range(dp)])  3.73 us
    pallas_call x1, Pallas kernels, forward(): pl.pallas_call(functools.partial(forward_kernel, kept, ids), out_shape=ja...  3.67 us
    ppermute x1, starting transfers between devices, body(): mixed_on = lax.ppermute(mixed_on, 'mp', inward + outward)  3.65 us
    ppermute x3, starting transfers between devices, body(): lax.ppermute(packs[0], 'dp', [(i, i ^ gap) for i in range(dp)])  3.55 us
    ppermute x3, starting transfers between devices, slot_reduce(): lax.ppermute(totals[gap], 'dp', [(i, i ^ 2 * gap) for i in range(dp)])  3.55 us
  transfers between devices with their start and end apart: 21, of which 9 were waited for; matrix products, arithmetic and copies ran while one was open for 1% of the time, Pallas kernels for 20%

profile of v5, /device:TPU:0, one launch (start us, length us, event | category | flops | bytes accessed | tf_op | source)
XLA Modules:
  0.0 69.8 jit_solution(12455933843997037904)
XLA Ops:
  0.6 3.1 %collective-permute-start.7 = (bf16[128,2048]{1,0:T(8,128)(2,1)}, bf16[128,2048]{1,0:T(8,128)(2,1)S(1)}, u32[]{:S(2)}, u32[]{:S(2)}) collective-permute-start(bf16[128,2048]{1,0:T(8,128)(2,1)} %own_h), channel_id=1, source_target_pairs={{0,1},{1,0},{2,3},{3,2},{4,5},{5,4},{6,7},{7,6},{8,9},{9,8},{10,11... | collective-permute-start | bytes 1572872 | tf_op jit(solution)/shard_map/ppermute | solution.py:590
  3.7 0.7 collective-permute-start.8
  4.4 1.6 %pack_blocks.1.refs_1_ = bf16[576,128]{1,0:T(8,128)(2,1)} custom-call(s32[4]{0:T(128)} %row_h.1, s32[4]{0:T(128)} %col_h.1, s32[4]{0:T(128)} %dest_h.2, bf16[4,128,128]{2,1,0:T(8,128)(2,1)} %w_ref.1), custom_call_target="tpu_custom_call" | custom-call | tf_op jit(solution)/shard_map/pack_blocks/pallas_call | solution.py:57
  6.0 1.6 %collective-permute-start = (bf16[576,128]{1,0:T(8,128)(2,1)}, bf16[576,128]{1,0:T(8,128)(2,1)S(1)}, u32[]{:S(2)}, u32[]{:S(2)}) collective-permute-start(bf16[576,128]{1,0:T(8,128)(2,1)} %pack_blocks.1.refs_1_), channel_id=1, source_target_pairs={{0,8},{4,12},{8,0},{12,4},{16,24},{20,28},{24,16},{28,20},{1,9},{5... | collective-permute-start | bytes 442376 | tf_op jit(solution)/shard_map/ppermute | solution.py:595
  7.6 1.5 %collective-permute-start.1 = (bf16[576,128]{1,0:T(8,128)(2,1)}, bf16[576,128]{1,0:T(8,128)(2,1)S(1)}, u32[]{:S(2)}, u32[]{:S(2)}) collective-permute-start(bf16[576,128]{1,0:T(8,128)(2,1)} %pack_blocks.1.refs_1_), channel_id=1, source_target_pairs={{0,16},{4,20},{8,24},{12,28},{16,0},{20,4},{24,8},{28,12},{1,17},{... | collective-permute-start | bytes 442376 | tf_op jit(solution)/shard_map/ppermute | solution.py:595
  9.1 0.5 collective-permute-start.2
  9.6 1.5 %copy-done = bf16[128,7168]{1,0:T(8,128)(2,1)S(1)} copy-done((bf16[128,7168]{1,0:T(8,128)(2,1)S(1)}, bf16[128,7168]{1,0:T(8,128)(2,1)}, u32[]{:S(2)}) %copy-start) | copy-done | bytes 1835032
  11.1 0.9 %copy-done.5 = bf16[576,128]{1,0:T(8,128)(2,1)S(1)} copy-done((bf16[576,128]{1,0:T(8,128)(2,1)S(1)}, bf16[576,128]{1,0:T(8,128)(2,1)}, u32[]{:S(2)}) %copy-start.5) | copy-done | bytes 147480
  12.0 0.3 hold_arrays.1
  12.3 0.1 collective-permute-done.refs_1_
  12.4 0.0 collective-permute-start.3
  12.4 3.7 %collective-permute-done.1.refs_2_ = bf16[576,128]{1,0:T(8,128)(2,1)S(1)} collective-permute-done((bf16[576,128]{1,0:T(8,128)(2,1)}, bf16[576,128]{1,0:T(8,128)(2,1)S(1)}, u32[]{:S(2)}, u32[]{:S(2)}) %collective-permute-start.1) | collective-permute-done | bytes 147488 | tf_op jit(solution)/shard_map/ppermute | solution.py:595
  16.1 0.0 collective-permute-done.2.refs_3_
  16.1 0.5 collective-permute-start.5
  16.6 0.0 collective-permute-done.3.refs_4_
  16.6 0.0 collective-permute-start.6
  16.6 0.9 %collective-permute-done.4.refs_5_ = bf16[576,128]{1,0:T(8,128)(2,1)S(1)} collective-permute-done((bf16[576,128]{1,0:T(8,128)(2,1)S(1)}, bf16[576,128]{1,0:T(8,128)(2,1)S(1)}, u32[]{:S(2)}, u32[]{:S(2)}) %collective-permute-start.4) | collective-permute-done | bytes 147488 | tf_op jit(solution)/shard_map/ppermute | solution.py:600
  17.5 0.2 collective-permute-done.5.refs_6_
  17.7 0.3 collective-permute-done.6.refs_7_
  18.0 2.1 %input_gradient.1 = (f32[128,8192]{1,0:T(8,128)S(1)}, s32[32,128]{1,0:T(8,128)S(1)}, bf16[128,2048]{1,0:T(8,128)(2,1)S(1)}) custom-call(bf16[576,128]{1,0:T(8,128)(2,1)S(1)} %get-tuple-element.47.refs_0_, bf16[576,128]{1,0:T(8,128)(2,1)S(1)} %collective-permute-done.refs_1_, bf16[576,128]{1,0:T(8,128)(2,1)S(1)} %collective-permute-done.1.refs_2_, ...), custom_call_target="tpu_custom_call" | custom-call | tf_op jit(solution)/shard_map/input_gradient/pallas_call | solution.py:229
  20.1 0.0 collective-permute-done.7.refs_0_
  20.1 0.0 collective-permute-done.8.inner_h.refs_1_
  20.1 0.1 choose_sent.2
  20.2 4.4 %collective-permute-start.9 = (bf16[128,2048]{1,0:T(8,128)(2,1)S(1)}, bf16[128,2048]{1,0:T(8,128)(2,1)S(1)}, u32[]{:S(2)}, u32[]{:S(2)}) collective-permute-start(bf16[128,2048]{1,0:T(8,128)(2,1)S(1)} %choose_sent.2), channel_id=1, source_target_pairs={{0,1},{3,2},{1,0},{2,3},{4,5},{7,6},{5,4},{6,7},{8,9},{11,10},{9,8... | collective-permute-start | bytes 1572872 | tf_op jit(solution)/shard_map/ppermute | solution.py:610
  24.6 0.7 collective-permute-start.12
  25.3 0.0 copy-start.2
  25.3 0.0 copy-start.3
  25.3 0.0 copy-start.4
  25.3 0.0 copy-start.7
  25.3 0.3 split_shares.1
  25.6 0.0 copy-start.6
  25.6 0.6 copy-done.2
  26.2 0.1 copy-done.3
  26.3 0.1 copy-done.4
  26.4 0.7 leaving_blocks.1
  27.1 1.9 %collective-permute-start.10 = (bf16[768,128]{1,0:T(8,128)(2,1)S(1)}, bf16[768,128]{1,0:T(8,128)(2,1)S(1)}, u32[]{:S(2)}, u32[]{:S(2)}) collective-permute-start(bf16[768,128]{1,0:T(8,128)(2,1)S(1)} %get-tuple-element.62), channel_id=1, source_target_pairs={{0,4},{4,8},{8,12},{12,16},{16,20},{20,24},{24,28},{1,5},{5,9},{9,... | collective-permute-start | bytes 589832 | tf_op jit(solution)/shard_map/ppermute | solution.py:615
  29.0 1.3 %collective-permute-start.11 = (bf16[768,128]{1,0:T(8,128)(2,1)S(1)}, bf16[768,128]{1,0:T(8,128)(2,1)S(1)}, u32[]{:S(2)}, u32[]{:S(2)}) collective-permute-start(bf16[768,128]{1,0:T(8,128)(2,1)S(1)} %get-tuple-element.63), channel_id=1, source_target_pairs={{4,0},{8,4},{12,8},{16,12},{20,16},{24,20},{28,24},{5,1},{9,5},{13... | collective-permute-start | bytes 589832 | tf_op jit(solution)/shard_map/ppermute | solution.py:616
  30.3 0.0 collective-permute-done.10.left_ref
  30.3 2.5 %collective-permute-done.11.right_ref = bf16[768,128]{1,0:T(8,128)(2,1)S(1)} collective-permute-done((bf16[768,128]{1,0:T(8,128)(2,1)S(1)}, bf16[768,128]{1,0:T(8,128)(2,1)S(1)}, u32[]{:S(2)}, u32[]{:S(2)}) %collective-permute-start.11) | collective-permute-done | bytes 196640 | tf_op jit(solution)/shard_map/ppermute | solution.py:616
  32.8 4.1 %collective-permute-done.9.came_h.refs_3_ = bf16[128,2048]{1,0:T(8,128)(2,1)S(1)} collective-permute-done((bf16[128,2048]{1,0:T(8,128)(2,1)S(1)}, bf16[128,2048]{1,0:T(8,128)(2,1)S(1)}, u32[]{:S(2)}, u32[]{:S(2)}) %collective-permute-start.9) | collective-permute-done | bytes 524320 | tf_op jit(solution)/shard_map/ppermute | solution.py:610
  36.9 0.0 collective-permute-done.12.inner_h.refs_2_
  36.9 0.1 choose_sent.3
  37.0 0.0 copy-start.1
  37.0 3.7 %collective-permute-start.13 = (bf16[128,2048]{1,0:T(8,128)(2,1)S(1)}, bf16[128,2048]{1,0:T(8,128)(2,1)S(1)}, u32[]{:S(2)}, u32[]{:S(2)}) collective-permute-start(bf16[128,2048]{1,0:T(8,128)(2,1)S(1)} %choose_sent.3), channel_id=1, source_target_pairs={{0,1},{3,2},{1,0},{2,3},{4,5},{7,6},{5,4},{6,7},{8,9},{11,10},{9,8... | collective-permute-start | bytes 1572872 | tf_op jit(solution)/shard_map/ppermute | solution.py:624
  40.7 0.7 collective-permute-start.18
  41.4 0.2 assemble_tokens.1.x_ref.refs_8_
  41.6 1.1 %turn_upstream.1.turned_ref = bf16[32,128,128]{2,1,0:T(8,128)(2,1)S(1)} custom-call(s32[32,128]{1,0:T(8,128)S(1)} %get-tuple-element.85.meta_s, bf16[128,7168]{1,0:T(8,128)(2,1)S(1)} %copy-done.1), custom_call_target="tpu_custom_call" | custom-call | tf_op jit(solution)/shard_map/turn_upstream/pallas_call | solution.py:391
  42.7 9.4 %collective-permute-done.13.refs_0_.refs_9_ = bf16[128,2048]{1,0:T(8,128)(2,1)S(1)} collective-permute-done((bf16[128,2048]{1,0:T(8,128)(2,1)S(1)}, bf16[128,2048]{1,0:T(8,128)(2,1)S(1)}, u32[]{:S(2)}, u32[]{:S(2)}) %collective-permute-start.13) | collective-permute-done | bytes 524320 | tf_op jit(solution)/shard_map/ppermute | solution.py:624
  52.2 1.7 %weight_gradient.1 = (f32[33,128,128]{2,1,0:T(8,128)S(1)}, bf16[16,128,128]{2,1,0:T(8,128)(2,1)S(1)}) custom-call(s32[32,128]{1,0:T(8,128)S(1)} %get-tuple-element.85.meta_s, bf16[32,128,128]{2,1,0:T(8,128)(2,1)S(1)} %turn_upstream.1.turned_ref, bf16[4,128,2048]{2,1,0:T(8,128)(2,1)S(1)} %assemble_tokens.1.x_ref.refs_8_, ...), custom_call_target="tpu_custom_call" | custom-call | tf_op jit(solution)/shard_map/weight_gradient/pallas_call | solution.py:424
  53.9 0.1 collective-permute-start.14
  54.0 0.1 add_convert_fusion.1
  54.1 0.0 collective-permute-done.18
  54.1 0.1 add_convert_fusion
  54.2 1.9 %collective-permute-start.19 = (bf16[128,2048]{1,0:T(8,128)(2,1)S(1)}, bf16[128,2048]{1,0:T(8,128)(2,1)S(1)}, u32[]{:S(2)}, u32[]{:S(2)}) collective-permute-start(bf16[128,2048]{1,0:T(8,128)(2,1)S(1)} %add_convert_fusion), channel_id=1, source_target_pairs={{0,1},{3,2},{1,0},{2,3},{4,5},{7,6},{5,4},{6,7},{8,9},{11,10},{9,8... | collective-permute-start | bytes 1572872 | tf_op jit(solution)/shard_map/ppermute | solution.py:641
  56.1 0.7 collective-permute-start.20
  56.8 0.0 collective-permute-done.14
  56.8 0.2 fusion
  57.1 1.5 %collective-permute-start.15 = (bf16[4,128,128]{2,1,0:T(8,128)(2,1)S(1)}, bf16[4,128,128]{2,1,0:T(8,128)(2,1)S(1)}, u32[]{:S(2)}, u32[]{:S(2)}) collective-permute-start(bf16[4,128,128]{2,1,0:T(8,128)(2,1)S(1)} %get-tuple-element.91), channel_id=1, source_target_pairs={{0,8},{4,12},{8,0},{12,4},{16,24},{20,28},{24,16},{28,20},{1,9},{5... | collective-permute-start | bytes 393224 | tf_op jit(solution)/shard_map/ppermute | solution.py:446
  58.6 0.2 collective-permute-start.16
  58.8 1.8 %collective-permute-start.17 = (bf16[4,128,128]{2,1,0:T(8,128)(2,1)S(1)}, bf16[4,128,128]{2,1,0:T(8,128)(2,1)S(1)}, u32[]{:S(2)}, u32[]{:S(2)}) collective-permute-start(bf16[4,128,128]{2,1,0:T(8,128)(2,1)S(1)} %get-tuple-element.89), channel_id=1, source_target_pairs={{0,24},{4,28},{8,16},{12,20},{16,8},{20,12},{24,0},{28,4},{1,25},{... | collective-permute-start | bytes 393224 | tf_op jit(solution)/shard_map/ppermute | solution.py:446
  60.6 3.7 %hidden_out.1 = bf16[128,7168]{1,0:T(8,128)(2,1)} custom-call(s32[32,128]{1,0:T(8,128)S(1)} %get-tuple-element.85.meta_s, bf16[576,128]{1,0:T(8,128)(2,1)S(1)} %get-tuple-element.47.refs_0_, bf16[576,128]{1,0:T(8,128)(2,1)S(1)} %collective-permute-done.refs_1_, bf16[576,128]{1,0:T(8,128)(2,1)S(1)} %collective-permute-done.1.refs_2_, ...), custom_call_target="tpu_custom_call" | custom-call | tf_op jit(solution)/shard_map/hidden_out/pallas_call | solution.py:472
  64.3 2.3 %collective-permute-done.16.refs_2_ = bf16[4,128,128]{2,1,0:T(8,128)(2,1)S(1)} collective-permute-done((bf16[4,128,128]{2,1,0:T(8,128)(2,1)S(1)}, bf16[4,128,128]{2,1,0:T(8,128)(2,1)S(1)}, u32[]{:S(2)}, u32[]{:S(2)}) %collective-permute-start.16) | collective-permute-done | bytes 131104 | tf_op jit(solution)/shard_map/ppermute | solution.py:446
  66.6 2.2 %adam_update.1 = (bf16[4,128,128]{2,1,0:T(8,128)(2,1)}, f32[4,128,128]{2,1,0:T(8,128)}, f32[4,128,128]{2,1,0:T(8,128)}) custom-call(s32[32,128]{1,0:T(8,128)S(1)} %get-tuple-element.85.meta_s, bf16[4,128,128]{2,1,0:T(8,128)(2,1)S(1)} %copy-done.2, f32[4,128,128]{2,1,0:T(8,128)S(1)} %copy-done.3, f32[4,128,128]{2,1,0:T(8,128)S(1)} %copy-done.4, ...), custom_call_target="tpu_custom_call" | custom-call | tf_op jit(solution)/shard_map/adam_update/pallas_call | solution.py:565
  68.8 0.9 %finish_input_grad.1 = bf16[128,2048]{1,0:T(8,128)(2,1)} custom-call(f32[128,2048]{1,0:T(8,128)S(1)} %get-tuple-element.86.own_ref, bf16[128,2048]{1,0:T(8,128)(2,1)S(1)} %collective-permute-done.19.first_ref, bf16[128,2048]{1,0:T(8,128)(2,1)S(1)} %collective-permute-done.20.second_ref), custom_call_target="tpu_custom_call" | custom-call | tf_op jit(solution)/shard_map/finish_input_grad/pallas_call | solution.py:490
  (13 shorter events, 0.1 us)
Async XLA Ops:
  0.6 19.4 %collective-permute-start.7 = (bf16[128,2048]{1,0:T(8,128)(2,1)}, bf16[128,2048]{1,0:T(8,128)(2,1)S(1)}, u32[]{:S(2)}, u32[]{:S(2)}) collective-permute-start(bf16[128,2048]{1,0:T(8,128)(2,1)} %own_h), channel_id=1, source_target_pairs={{0,1},{1,0},{2,3},{3,2},{4,5},{5,4},{6,7},{7,6},{8,9},{9,8},{10,11... | collective-permute-start | bytes 1572872 | tf_op jit(solution)/shard_map/ppermute | solution.py:590
  3.7 16.4 %collective-permute-start.8 = (bf16[128,2048]{1,0:T(8,128)(2,1)}, bf16[128,2048]{1,0:T(8,128)(2,1)S(1)}, u32[]{:S(2)}, u32[]{:S(2)}) collective-permute-start(bf16[128,2048]{1,0:T(8,128)(2,1)} %own_h), channel_id=1, source_target_pairs={{1,2},{2,1},{5,6},{6,5},{9,10},{10,9},{13,14},{14,13},{17,18},{18,... | collective-permute-start | bytes 1572872 | tf_op jit(solution)/shard_map/ppermute | solution.py:591
  6.0 6.4 %collective-permute-start = (bf16[576,128]{1,0:T(8,128)(2,1)}, bf16[576,128]{1,0:T(8,128)(2,1)S(1)}, u32[]{:S(2)}, u32[]{:S(2)}) collective-permute-start(bf16[576,128]{1,0:T(8,128)(2,1)} %pack_blocks.1.refs_1_), channel_id=1, source_target_pairs={{0,8},{4,12},{8,0},{12,4},{16,24},{20,28},{24,16},{28,20},{1,9},{5... | collective-permute-start | bytes 442376 | tf_op jit(solution)/shard_map/ppermute | solution.py:595
  7.6 8.5 %collective-permute-start.1 = (bf16[576,128]{1,0:T(8,128)(2,1)}, bf16[576,128]{1,0:T(8,128)(2,1)S(1)}, u32[]{:S(2)}, u32[]{:S(2)}) collective-permute-start(bf16[576,128]{1,0:T(8,128)(2,1)} %pack_blocks.1.refs_1_), channel_id=1, source_target_pairs={{0,16},{4,20},{8,24},{12,28},{16,0},{20,4},{24,8},{28,12},{1,17},{... | collective-permute-start | bytes 442376 | tf_op jit(solution)/shard_map/ppermute | solution.py:595
  9.1 7.0 %collective-permute-start.2 = (bf16[576,128]{1,0:T(8,128)(2,1)}, bf16[576,128]{1,0:T(8,128)(2,1)S(1)}, u32[]{:S(2)}, u32[]{:S(2)}) collective-permute-start(bf16[576,128]{1,0:T(8,128)(2,1)} %pack_blocks.1.refs_1_), channel_id=1, source_target_pairs={{0,24},{4,28},{8,16},{12,20},{16,8},{20,12},{24,0},{28,4},{1,25},{... | collective-permute-start | bytes 442376 | tf_op jit(solution)/shard_map/ppermute | solution.py:595
  9.6 1.5 %copy-start = (bf16[128,7168]{1,0:T(8,128)(2,1)S(1)}, bf16[128,7168]{1,0:T(8,128)(2,1)}, u32[]{:S(2)}) copy-start(bf16[128,7168]{1,0:T(8,128)(2,1)} %up_ref.1) | copy-start | bytes 5505028
  11.1 0.9 %copy-start.5 = (bf16[576,128]{1,0:T(8,128)(2,1)S(1)}, bf16[576,128]{1,0:T(8,128)(2,1)}, u32[]{:S(2)}) copy-start(bf16[576,128]{1,0:T(8,128)(2,1)} %pack_blocks.1.refs_1_) | copy-start | bytes 442372
  12.4 4.2 %collective-permute-start.3 = (bf16[576,128]{1,0:T(8,128)(2,1)S(1)}, bf16[576,128]{1,0:T(8,128)(2,1)S(1)}, u32[]{:S(2)}, u32[]{:S(2)}) collective-permute-start(bf16[576,128]{1,0:T(8,128)(2,1)S(1)} %get-tuple-element.47.refs_0_), channel_id=1, source_target_pairs={{0,4},{4,0},{8,12},{12,8},{16,20},{20,16},{24,28},{28,24},{1,5},{5... | collective-permute-start | bytes 442376 | tf_op jit(solution)/shard_map/ppermute | solution.py:600
  16.1 1.4 %collective-permute-start.4 = (bf16[576,128]{1,0:T(8,128)(2,1)S(1)}, bf16[576,128]{1,0:T(8,128)(2,1)S(1)}, u32[]{:S(2)}, u32[]{:S(2)}) collective-permute-start(bf16[576,128]{1,0:T(8,128)(2,1)S(1)} %collective-permute-done.refs_1_), channel_id=1, source_target_pairs={{0,4},{4,0},{8,12},{12,8},{16,20},{20,16},{24,28},{28,24},{1,5},{5... | collective-permute-start | bytes 442376 | tf_op jit(solution)/shard_map/ppermute | solution.py:600
  16.1 1.6 %collective-permute-start.5 = (bf16[576,128]{1,0:T(8,128)(2,1)S(1)}, bf16[576,128]{1,0:T(8,128)(2,1)S(1)}, u32[]{:S(2)}, u32[]{:S(2)}) collective-permute-start(bf16[576,128]{1,0:T(8,128)(2,1)S(1)} %collective-permute-done.1.refs_2_), channel_id=1, source_target_pairs={{0,4},{4,0},{8,12},{12,8},{16,20},{20,16},{24,28},{28,24},{1,5},{5... | collective-permute-start | bytes 442376 | tf_op jit(solution)/shard_map/ppermute | solution.py:600
  16.6 1.4 %collective-permute-start.6 = (bf16[576,128]{1,0:T(8,128)(2,1)S(1)}, bf16[576,128]{1,0:T(8,128)(2,1)S(1)}, u32[]{:S(2)}, u32[]{:S(2)}) collective-permute-start(bf16[576,128]{1,0:T(8,128)(2,1)S(1)} %collective-permute-done.2.refs_3_), channel_id=1, source_target_pairs={{0,4},{4,0},{8,12},{12,8},{16,20},{20,16},{24,28},{28,24},{1,5},{5... | collective-permute-start | bytes 442376 | tf_op jit(solution)/shard_map/ppermute | solution.py:600
  20.2 16.7 %collective-permute-start.9 = (bf16[128,2048]{1,0:T(8,128)(2,1)S(1)}, bf16[128,2048]{1,0:T(8,128)(2,1)S(1)}, u32[]{:S(2)}, u32[]{:S(2)}) collective-permute-start(bf16[128,2048]{1,0:T(8,128)(2,1)S(1)} %choose_sent.2), channel_id=1, source_target_pairs={{0,1},{3,2},{1,0},{2,3},{4,5},{7,6},{5,4},{6,7},{8,9},{11,10},{9,8... | collective-permute-start | bytes 1572872 | tf_op jit(solution)/shard_map/ppermute | solution.py:610
  24.6 12.3 %collective-permute-start.12 = (bf16[128,2048]{1,0:T(8,128)(2,1)S(1)}, bf16[128,2048]{1,0:T(8,128)(2,1)S(1)}, u32[]{:S(2)}, u32[]{:S(2)}) collective-permute-start(bf16[128,2048]{1,0:T(8,128)(2,1)S(1)} %collective-permute-done.7.refs_0_), channel_id=1, source_target_pairs={{1,2},{2,1},{5,6},{6,5},{9,10},{10,9},{13,14},{14,13},{17,18},{18,... | collective-permute-start | bytes 1572872 | tf_op jit(solution)/shard_map/ppermute | solution.py:611
  25.3 0.9 %copy-start.2 = (bf16[4,128,128]{2,1,0:T(8,128)(2,1)S(1)}, bf16[4,128,128]{2,1,0:T(8,128)(2,1)}, u32[]{:S(2)}) copy-start(bf16[4,128,128]{2,1,0:T(8,128)(2,1)} %w_ref.1) | copy-start | bytes 393220
  25.3 1.0 %copy-start.3 = (f32[4,128,128]{2,1,0:T(8,128)S(1)}, f32[4,128,128]{2,1,0:T(8,128)}, u32[]{:S(2)}) copy-start(f32[4,128,128]{2,1,0:T(8,128)} %one_ref.1) | copy-start | bytes 786436
  25.3 1.1 %copy-start.4 = (f32[4,128,128]{2,1,0:T(8,128)S(1)}, f32[4,128,128]{2,1,0:T(8,128)}, u32[]{:S(2)}) copy-start(f32[4,128,128]{2,1,0:T(8,128)} %two_ref.1) | copy-start | bytes 786436
  25.3 1.1 %copy-start.7 = (s32[4]{0:T(128)S(1)}, s32[4]{0:T(128)}, u32[]{:S(2)}) copy-start(s32[4]{0:T(128)} %dest_h.2) | copy-start | bytes 52
  25.6 15.8 %copy-start.6 = (bf16[128,2048]{1,0:T(8,128)(2,1)S(1)}, bf16[128,2048]{1,0:T(8,128)(2,1)}, u32[]{:S(2)}) copy-start(bf16[128,2048]{1,0:T(8,128)(2,1)} %own_h) | copy-start | bytes 1572868
  27.1 3.2 %collective-permute-start.10 = (bf16[768,128]{1,0:T(8,128)(2,1)S(1)}, bf16[768,128]{1,0:T(8,128)(2,1)S(1)}, u32[]{:S(2)}, u32[]{:S(2)}) collective-permute-start(bf16[768,128]{1,0:T(8,128)(2,1)S(1)} %get-tuple-element.62), channel_id=1, source_target_pairs={{0,4},{4,8},{8,12},{12,16},{16,20},{20,24},{24,28},{1,5},{5,9},{9,... | collective-permute-start | bytes 589832 | tf_op jit(solution)/shard_map/ppermute | solution.py:615
  29.0 3.8 %collective-permute-start.11 = (bf16[768,128]{1,0:T(8,128)(2,1)S(1)}, bf16[768,128]{1,0:T(8,128)(2,1)S(1)}, u32[]{:S(2)}, u32[]{:S(2)}) collective-permute-start(bf16[768,128]{1,0:T(8,128)(2,1)S(1)} %get-tuple-element.63), channel_id=1, source_target_pairs={{4,0},{8,4},{12,8},{16,12},{20,16},{24,20},{28,24},{5,1},{9,5},{13... | collective-permute-start | bytes 589832 | tf_op jit(solution)/shard_map/ppermute | solution.py:616
  37.0 4.6 %copy-start.1 = (bf16[128,7168]{1,0:T(8,128)(2,1)S(1)}, bf16[128,7168]{1,0:T(8,128)(2,1)}, u32[]{:S(2)}) copy-start(bf16[128,7168]{1,0:T(8,128)(2,1)} %up_ref.1) | copy-start | bytes 5505028
  37.0 15.1 %collective-permute-start.13 = (bf16[128,2048]{1,0:T(8,128)(2,1)S(1)}, bf16[128,2048]{1,0:T(8,128)(2,1)S(1)}, u32[]{:S(2)}, u32[]{:S(2)}) collective-permute-start(bf16[128,2048]{1,0:T(8,128)(2,1)S(1)} %choose_sent.3), channel_id=1, source_target_pairs={{0,1},{3,2},{1,0},{2,3},{4,5},{7,6},{5,4},{6,7},{8,9},{11,10},{9,8... | collective-permute-start | bytes 1572872 | tf_op jit(solution)/shard_map/ppermute | solution.py:624
  40.7 13.4 %collective-permute-start.18 = (bf16[128,2048]{1,0:T(8,128)(2,1)S(1)}, bf16[128,2048]{1,0:T(8,128)(2,1)S(1)}, u32[]{:S(2)}, u32[]{:S(2)}) collective-permute-start(bf16[128,2048]{1,0:T(8,128)(2,1)S(1)} %inner_sum.1), channel_id=1, source_target_pairs={{1,2},{2,1},{5,6},{6,5},{9,10},{10,9},{13,14},{14,13},{17,18},{18,... | collective-permute-start | bytes 1572872 | tf_op jit(solution)/shard_map/ppermute | solution.py:625
  53.9 2.9 %collective-permute-start.14 = (bf16[16,128,128]{2,1,0:T(8,128)(2,1)S(1)}, bf16[16,128,128]{2,1,0:T(8,128)(2,1)S(1)}, u32[]{:S(2)}, u32[]{:S(2)}) collective-permute-start(bf16[16,128,128]{2,1,0:T(8,128)(2,1)S(1)} %get-tuple-element.76), channel_id=1, source_target_pairs={{0,4},{4,0},{8,12},{12,8},{16,20},{20,16},{24,28},{28,24},{1,5},{5... | collective-permute-start | bytes 1572872 | tf_op jit(solution)/shard_map/ppermute | solution.py:439
  54.2 14.6 %collective-permute-start.19 = (bf16[128,2048]{1,0:T(8,128)(2,1)S(1)}, bf16[128,2048]{1,0:T(8,128)(2,1)S(1)}, u32[]{:S(2)}, u32[]{:S(2)}) collective-permute-start(bf16[128,2048]{1,0:T(8,128)(2,1)S(1)} %add_convert_fusion), channel_id=1, source_target_pairs={{0,1},{3,2},{1,0},{2,3},{4,5},{7,6},{5,4},{6,7},{8,9},{11,10},{9,8... | collective-permute-start | bytes 1572872 | tf_op jit(solution)/shard_map/ppermute | solution.py:641
  56.1 12.7 %collective-permute-start.20 = (bf16[128,2048]{1,0:T(8,128)(2,1)S(1)}, bf16[128,2048]{1,0:T(8,128)(2,1)S(1)}, u32[]{:S(2)}, u32[]{:S(2)}) collective-permute-start(bf16[128,2048]{1,0:T(8,128)(2,1)S(1)} %add_convert_fusion.1), channel_id=1, source_target_pairs={{1,2},{2,1},{5,6},{6,5},{9,10},{10,9},{13,14},{14,13},{17,18},{18,... | collective-permute-start | bytes 1572872 | tf_op jit(solution)/shard_map/ppermute | solution.py:640
  57.1 7.2 %collective-permute-start.15 = (bf16[4,128,128]{2,1,0:T(8,128)(2,1)S(1)}, bf16[4,128,128]{2,1,0:T(8,128)(2,1)S(1)}, u32[]{:S(2)}, u32[]{:S(2)}) collective-permute-start(bf16[4,128,128]{2,1,0:T(8,128)(2,1)S(1)} %get-tuple-element.91), channel_id=1, source_target_pairs={{0,8},{4,12},{8,0},{12,4},{16,24},{20,28},{24,16},{28,20},{1,9},{5... | collective-permute-start | bytes 393224 | tf_op jit(solution)/shard_map/ppermute | solution.py:446
  58.6 8.0 %collective-permute-start.16 = (bf16[4,128,128]{2,1,0:T(8,128)(2,1)S(1)}, bf16[4,128,128]{2,1,0:T(8,128)(2,1)S(1)}, u32[]{:S(2)}, u32[]{:S(2)}) collective-permute-start(bf16[4,128,128]{2,1,0:T(8,128)(2,1)S(1)} %get-tuple-element.90), channel_id=1, source_target_pairs={{0,16},{4,20},{8,24},{12,28},{16,0},{20,4},{24,8},{28,12},{1,17},{... | collective-permute-start | bytes 393224 | tf_op jit(solution)/shard_map/ppermute | solution.py:446
  58.8 7.8 %collective-permute-start.17 = (bf16[4,128,128]{2,1,0:T(8,128)(2,1)S(1)}, bf16[4,128,128]{2,1,0:T(8,128)(2,1)S(1)}, u32[]{:S(2)}, u32[]{:S(2)}) collective-permute-start(bf16[4,128,128]{2,1,0:T(8,128)(2,1)S(1)} %get-tuple-element.89), channel_id=1, source_target_pairs={{0,24},{4,28},{8,16},{12,20},{16,8},{20,12},{24,0},{28,4},{1,25},{... | collective-permute-start | bytes 393224 | tf_op jit(solution)/shard_map/ppermute | solution.py:446

commit v6 on v5

--- a/solution.py
+++ b/solution.py
@@ -610,15 +610,9 @@
         mixed = lax.ppermute(mixed, "mp", inward + outward)
         near_on = lax.ppermute(near, "mp", inner)
         own_share, second, first = split(after(sums, mixed_sent), slices, (0, 2, 3))
-        dest_leave = after(dest_slot, own_share)
-    to_left, to_right = leave(dest_leave, weight, moment_one, moment_two)
-    from_left = lax.ppermute(to_right, "dp", [(i, i + 1) for i in range(dp - 1)])
-    from_right = lax.ppermute(to_left, "dp", [(i + 1, i) for i in range(dp - 1)])
+        sum_base = after(far, own_share)
     if four:
-        far, mixed, from_left, from_right = lax.optimization_barrier(
-            (far, mixed, from_left, from_right)
-        )
-        sum_far = inner_sum(far, mixed)
+        sum_far = inner_sum(sum_base, mixed)
         mixed_on = choose(after(second, sum_far), near_on)
         sum_far, mixed_on = lax.optimization_barrier((sum_far, mixed_on))
         mixed_on = lax.ppermute(mixed_on, "mp", inward + outward)
@@ -626,10 +620,14 @@
         came = (near, middle, near_on, mixed)
         x_all = assemble(after(tokens, sum_far), came, slices)
         turned = turn(after(meta, x_all), upstream)
+        dest_leave = after(dest_slot, turned)
         last = (mixed_on,)
     else:
         x_all, last = assemble(tokens, came, slices), ()
         turned = turn(meta, upstream)
+    to_left, to_right = leave(dest_leave, weight, moment_one, moment_two)
+    from_left = lax.ppermute(to_right, "dp", [(i, i + 1) for i in range(dp - 1)])
+    from_right = lax.ppermute(to_left, "dp", [(i + 1, i) for i in range(dp - 1)])
     keep, send = gradient(meta, x_all, last, turned, kept, dp)
     parts, totals = slot_reduce(keep, send, kept, dp)
     meta_out = meta

time: 70.5 us -> 70.5 us (level)
  waiting for transfers between devices: 23.5 us -> 24.6 us
  local copies, waits for them, and re-layouts: 3.26 us -> 2.49 us
    ppermute x1, waiting for transfers between devices: 4.09 us -> 11.3 us  [body(): mixed = lax.ppermute(mixed, 'mp', inward + outward)]
    ppermute x1, waiting for transfers between devices: 9.44 us -> 6.04 us  [body(): mixed_on = lax.ppermute(mixed_on, 'mp', inward + outward)]
    ppermute x1, waiting for transfers between devices: 2.54 us -> 0.01 us  [body(): lax.ppermute(to_left, 'dp', [(i + 1, i) for i in range(dp - 1)])]
    unnamed x16, local copies, waits for them, and re-layouts: 3.22 us -> 2.45 us
where the time goes in v6:
time: 70.5 us; the launch traced here: 69.6 us
  starting transfers between devices  26.1 us (37%)
  waiting for transfers between devices  24.6 us (35%)
  Pallas kernels  14.9 us (21%)
  local copies, waits for them, and re-layouts  2.49 us (4%)
  between operations  0.96 us (1%)
    ppermute x1, waiting for transfers between devices, body(): mixed = lax.ppermute(mixed, 'mp', inward + outward)  11.3 us
    ppermute x1, waiting for transfers between devices, body(): mixed_on = lax.ppermute(mixed_on, 'mp', inward + outward)  6.04 us
    ppermute x1, starting transfers between devices, body(): mixed = lax.ppermute(mixed, 'mp', inward + outward)  4.43 us
    ppermute x3, waiting for transfers between devices, body(): lax.ppermute(packs[0], 'dp', [(i, i ^ gap) for i in range(dp)])  3.73 us
    pallas_call x1, Pallas kernels, forward(): pl.pallas_call(functools.partial(forward_kernel, kept, ids), out_shape=ja...  3.66 us
    ppermute x1, starting transfers between devices, body(): mixed_on = lax.ppermute(mixed_on, 'mp', inward + outward)  3.65 us
    ppermute x3, starting transfers between devices, slot_reduce(): lax.ppermute(totals[gap], 'dp', [(i, i ^ 2 * gap) for i in range(dp)])  3.55 us
    ppermute x3, starting transfers between devices, body(): lax.ppermute(packs[0], 'dp', [(i, i ^ gap) for i in range(dp)])  3.55 us
  transfers between devices with their start and end apart: 21, of which 9 were waited for; matrix products, arithmetic and copies ran while one was open for 1% of the time, Pallas kernels for 20%

profile of v6, /device:TPU:0, one launch (start us, length us, event | category | flops | bytes accessed | tf_op | source)
XLA Modules:
  0.0 69.6 jit_solution(9796111517322250879)
XLA Ops:
  0.6 3.1 %collective-permute-start.7 = (bf16[128,2048]{1,0:T(8,128)(2,1)}, bf16[128,2048]{1,0:T(8,128)(2,1)S(1)}, u32[]{:S(2)}, u32[]{:S(2)}) collective-permute-start(bf16[128,2048]{1,0:T(8,128)(2,1)} %own_h), channel_id=1, source_target_pairs={{0,1},{1,0},{2,3},{3,2},{4,5},{5,4},{6,7},{7,6},{8,9},{9,8},{10,11... | collective-permute-start | bytes 1572872 | tf_op jit(solution)/shard_map/ppermute | solution.py:590
  3.7 0.7 collective-permute-start.8
  4.4 1.6 %pack_blocks.1.refs_1_ = bf16[576,128]{1,0:T(8,128)(2,1)} custom-call(s32[4]{0:T(128)} %row_h.1, s32[4]{0:T(128)} %col_h.1, s32[4]{0:T(128)} %dest_h.2, bf16[4,128,128]{2,1,0:T(8,128)(2,1)} %w_ref.1), custom_call_target="tpu_custom_call" | custom-call | tf_op jit(solution)/shard_map/pack_blocks/pallas_call | solution.py:57
  6.0 1.6 %collective-permute-start = (bf16[576,128]{1,0:T(8,128)(2,1)}, bf16[576,128]{1,0:T(8,128)(2,1)S(1)}, u32[]{:S(2)}, u32[]{:S(2)}) collective-permute-start(bf16[576,128]{1,0:T(8,128)(2,1)} %pack_blocks.1.refs_1_), channel_id=1, source_target_pairs={{0,8},{4,12},{8,0},{12,4},{16,24},{20,28},{24,16},{28,20},{1,9},{5... | collective-permute-start | bytes 442376 | tf_op jit(solution)/shard_map/ppermute | solution.py:595
  7.6 1.5 %collective-permute-start.1 = (bf16[576,128]{1,0:T(8,128)(2,1)}, bf16[576,128]{1,0:T(8,128)(2,1)S(1)}, u32[]{:S(2)}, u32[]{:S(2)}) collective-permute-start(bf16[576,128]{1,0:T(8,128)(2,1)} %pack_blocks.1.refs_1_), channel_id=1, source_target_pairs={{0,16},{4,20},{8,24},{12,28},{16,0},{20,4},{24,8},{28,12},{1,17},{... | collective-permute-start | bytes 442376 | tf_op jit(solution)/shard_map/ppermute | solution.py:595
  9.1 0.5 collective-permute-start.2
  9.6 1.5 %copy-done = bf16[128,7168]{1,0:T(8,128)(2,1)S(1)} copy-done((bf16[128,7168]{1,0:T(8,128)(2,1)S(1)}, bf16[128,7168]{1,0:T(8,128)(2,1)}, u32[]{:S(2)}) %copy-start) | copy-done | bytes 1835032
  11.1 0.9 %copy-done.5 = bf16[576,128]{1,0:T(8,128)(2,1)S(1)} copy-done((bf16[576,128]{1,0:T(8,128)(2,1)S(1)}, bf16[576,128]{1,0:T(8,128)(2,1)}, u32[]{:S(2)}) %copy-start.5) | copy-done | bytes 147480
  12.0 0.3 hold_arrays.1
  12.3 0.1 collective-permute-done.refs_1_
  12.4 0.0 collective-permute-start.3
  12.4 3.7 %collective-permute-done.1.refs_2_ = bf16[576,128]{1,0:T(8,128)(2,1)S(1)} collective-permute-done((bf16[576,128]{1,0:T(8,128)(2,1)}, bf16[576,128]{1,0:T(8,128)(2,1)S(1)}, u32[]{:S(2)}, u32[]{:S(2)}) %collective-permute-start.1) | collective-permute-done | bytes 147488 | tf_op jit(solution)/shard_map/ppermute | solution.py:595
  16.1 0.0 collective-permute-done.2.refs_3_
  16.1 0.0 collective-permute-start.4
  16.1 0.5 collective-permute-start.5
  16.6 0.0 collective-permute-done.3.refs_4_
  16.6 0.0 collective-permute-start.6
  16.6 0.9 %collective-permute-done.4.refs_5_ = bf16[576,128]{1,0:T(8,128)(2,1)S(1)} collective-permute-done((bf16[576,128]{1,0:T(8,128)(2,1)S(1)}, bf16[576,128]{1,0:T(8,128)(2,1)S(1)}, u32[]{:S(2)}, u32[]{:S(2)}) %collective-permute-start.4) | collective-permute-done | bytes 147488 | tf_op jit(solution)/shard_map/ppermute | solution.py:600
  17.5 0.2 collective-permute-done.5.refs_6_
  17.7 0.3 collective-permute-done.6.refs_7_
  18.0 2.1 %input_gradient.1 = (f32[128,8192]{1,0:T(8,128)S(1)}, s32[32,128]{1,0:T(8,128)S(1)}, bf16[128,2048]{1,0:T(8,128)(2,1)S(1)}) custom-call(bf16[576,128]{1,0:T(8,128)(2,1)S(1)} %get-tuple-element.44.refs_0_, bf16[576,128]{1,0:T(8,128)(2,1)S(1)} %collective-permute-done.refs_1_, bf16[576,128]{1,0:T(8,128)(2,1)S(1)} %collective-permute-done.1.refs_2_, ...), custom_call_target="tpu_custom_call" | custom-call | tf_op jit(solution)/shard_map/input_gradient/pallas_call | solution.py:229
  20.1 0.0 collective-permute-done.7.refs_0_
  20.1 0.0 collective-permute-done.8.inner_h.refs_1_
  20.1 0.1 choose_sent.2
  20.2 4.4 %collective-permute-start.9 = (bf16[128,2048]{1,0:T(8,128)(2,1)S(1)}, bf16[128,2048]{1,0:T(8,128)(2,1)S(1)}, u32[]{:S(2)}, u32[]{:S(2)}) collective-permute-start(bf16[128,2048]{1,0:T(8,128)(2,1)S(1)} %choose_sent.2), channel_id=1, source_target_pairs={{0,1},{3,2},{1,0},{2,3},{4,5},{7,6},{5,4},{6,7},{8,9},{11,10},{9,8... | collective-permute-start | bytes 1572872 | tf_op jit(solution)/shard_map/ppermute | solution.py:610
  24.6 0.7 collective-permute-start.10
  25.3 0.3 split_shares.1
  25.6 0.0 copy-start.6
  25.6 11.3 %collective-permute-done.9.came_h.refs_3_ = bf16[128,2048]{1,0:T(8,128)(2,1)S(1)} collective-permute-done((bf16[128,2048]{1,0:T(8,128)(2,1)S(1)}, bf16[128,2048]{1,0:T(8,128)(2,1)S(1)}, u32[]{:S(2)}, u32[]{:S(2)}) %collective-permute-start.9) | collective-permute-done | bytes 524320 | tf_op jit(solution)/shard_map/ppermute | solution.py:610
  36.9 0.0 collective-permute-done.10.inner_h.refs_2_
  36.9 0.1 choose_sent.3
  37.0 0.0 copy-start.1
  37.0 3.7 %collective-permute-start.13 = (bf16[128,2048]{1,0:T(8,128)(2,1)S(1)}, bf16[128,2048]{1,0:T(8,128)(2,1)S(1)}, u32[]{:S(2)}, u32[]{:S(2)}) collective-permute-start(bf16[128,2048]{1,0:T(8,128)(2,1)S(1)} %choose_sent.3), channel_id=1, source_target_pairs={{0,1},{3,2},{1,0},{2,3},{4,5},{7,6},{5,4},{6,7},{8,9},{11,10},{9,8... | collective-permute-start | bytes 1572872 | tf_op jit(solution)/shard_map/ppermute | solution.py:618
  40.7 0.7 collective-permute-start.18
  41.4 0.2 assemble_tokens.1.x_ref.refs_8_
  41.6 0.0 copy-start.2
  41.6 0.0 copy-start.3
  41.6 0.0 copy-start.4
  41.6 0.0 copy-start.7
  41.6 1.1 %turn_upstream.1.turned_ref = bf16[32,128,128]{2,1,0:T(8,128)(2,1)S(1)} custom-call(s32[32,128]{1,0:T(8,128)S(1)} %get-tuple-element.79.meta_s, bf16[128,7168]{1,0:T(8,128)(2,1)S(1)} %copy-done.1), custom_call_target="tpu_custom_call" | custom-call | tf_op jit(solution)/shard_map/turn_upstream/pallas_call | solution.py:391
  42.8 0.7 leaving_blocks.1
  43.5 1.3 %collective-permute-start.11 = (bf16[768,128]{1,0:T(8,128)(2,1)S(1)}, bf16[768,128]{1,0:T(8,128)(2,1)S(1)}, u32[]{:S(2)}, u32[]{:S(2)}) collective-permute-start(bf16[768,128]{1,0:T(8,128)(2,1)S(1)} %get-tuple-element.66), channel_id=1, source_target_pairs={{0,4},{4,8},{8,12},{12,16},{16,20},{20,24},{24,28},{1,5},{5,9},{9,... | collective-permute-start | bytes 589832 | tf_op jit(solution)/shard_map/ppermute | solution.py:629
  44.8 1.3 %collective-permute-start.12 = (bf16[768,128]{1,0:T(8,128)(2,1)S(1)}, bf16[768,128]{1,0:T(8,128)(2,1)S(1)}, u32[]{:S(2)}, u32[]{:S(2)}) collective-permute-start(bf16[768,128]{1,0:T(8,128)(2,1)S(1)} %get-tuple-element.67), channel_id=1, source_target_pairs={{4,0},{8,4},{12,8},{16,12},{20,16},{24,20},{28,24},{5,1},{9,5},{13... | collective-permute-start | bytes 589832 | tf_op jit(solution)/shard_map/ppermute | solution.py:630
  46.1 6.0 %collective-permute-done.13.refs_0_.refs_9_ = bf16[128,2048]{1,0:T(8,128)(2,1)S(1)} collective-permute-done((bf16[128,2048]{1,0:T(8,128)(2,1)S(1)}, bf16[128,2048]{1,0:T(8,128)(2,1)S(1)}, u32[]{:S(2)}, u32[]{:S(2)}) %collective-permute-start.13) | collective-permute-done | bytes 524320 | tf_op jit(solution)/shard_map/ppermute | solution.py:618
  52.1 1.7 %weight_gradient.1 = (f32[33,128,128]{2,1,0:T(8,128)S(1)}, bf16[16,128,128]{2,1,0:T(8,128)(2,1)S(1)}) custom-call(s32[32,128]{1,0:T(8,128)S(1)} %get-tuple-element.79.meta_s, bf16[32,128,128]{2,1,0:T(8,128)(2,1)S(1)} %turn_upstream.1.turned_ref, bf16[4,128,2048]{2,1,0:T(8,128)(2,1)S(1)} %assemble_tokens.1.x_ref.refs_8_, ...), custom_call_target="tpu_custom_call" | custom-call | tf_op jit(solution)/shard_map/weight_gradient/pallas_call | solution.py:424
  53.9 0.1 collective-permute-start.14
  53.9 0.1 add_convert_fusion.1
  54.1 0.0 collective-permute-done.18
  54.1 0.1 add_convert_fusion
  54.2 1.9 %collective-permute-start.19 = (bf16[128,2048]{1,0:T(8,128)(2,1)S(1)}, bf16[128,2048]{1,0:T(8,128)(2,1)S(1)}, u32[]{:S(2)}, u32[]{:S(2)}) collective-permute-start(bf16[128,2048]{1,0:T(8,128)(2,1)S(1)} %add_convert_fusion), channel_id=1, source_target_pairs={{0,1},{3,2},{1,0},{2,3},{4,5},{7,6},{5,4},{6,7},{8,9},{11,10},{9,8... | collective-permute-start | bytes 1572872 | tf_op jit(solution)/shard_map/ppermute | solution.py:639
  56.1 0.7 collective-permute-start.20
  56.8 0.0 collective-permute-done.14
  56.8 0.2 fusion
  57.0 0.9 %collective-permute-start.15 = (bf16[4,128,128]{2,1,0:T(8,128)(2,1)S(1)}, bf16[4,128,128]{2,1,0:T(8,128)(2,1)S(1)}, u32[]{:S(2)}, u32[]{:S(2)}) collective-permute-start(bf16[4,128,128]{2,1,0:T(8,128)(2,1)S(1)} %get-tuple-element.85), channel_id=1, source_target_pairs={{0,8},{4,12},{8,0},{12,4},{16,24},{20,28},{24,16},{28,20},{1,9},{5... | collective-permute-start | bytes 393224 | tf_op jit(solution)/shard_map/ppermute | solution.py:446
  57.9 0.0 collective-permute-done.11.left_ref
  58.0 0.8 %collective-permute-start.16 = (bf16[4,128,128]{2,1,0:T(8,128)(2,1)S(1)}, bf16[4,128,128]{2,1,0:T(8,128)(2,1)S(1)}, u32[]{:S(2)}, u32[]{:S(2)}) collective-permute-start(bf16[4,128,128]{2,1,0:T(8,128)(2,1)S(1)} %get-tuple-element.84), channel_id=1, source_target_pairs={{0,16},{4,20},{8,24},{12,28},{16,0},{20,4},{24,8},{28,12},{1,17},{... | collective-permute-start | bytes 393224 | tf_op jit(solution)/shard_map/ppermute | solution.py:446
  58.8 1.8 %collective-permute-start.17 = (bf16[4,128,128]{2,1,0:T(8,128)(2,1)S(1)}, bf16[4,128,128]{2,1,0:T(8,128)(2,1)S(1)}, u32[]{:S(2)}, u32[]{:S(2)}) collective-permute-start(bf16[4,128,128]{2,1,0:T(8,128)(2,1)S(1)} %get-tuple-element.83), channel_id=1, source_target_pairs={{0,24},{4,28},{8,16},{12,20},{16,8},{20,12},{24,0},{28,4},{1,25},{... | collective-permute-start | bytes 393224 | tf_op jit(solution)/shard_map/ppermute | solution.py:446
  60.6 3.7 %hidden_out.1 = bf16[128,7168]{1,0:T(8,128)(2,1)} custom-call(s32[32,128]{1,0:T(8,128)S(1)} %get-tuple-element.79.meta_s, bf16[576,128]{1,0:T(8,128)(2,1)S(1)} %get-tuple-element.44.refs_0_, bf16[576,128]{1,0:T(8,128)(2,1)S(1)} %collective-permute-done.refs_1_, bf16[576,128]{1,0:T(8,128)(2,1)S(1)} %collective-permute-done.1.refs_2_, ...), custom_call_target="tpu_custom_call" | custom-call | tf_op jit(solution)/shard_map/hidden_out/pallas_call | solution.py:472
  64.3 0.0 collective-permute-done.15.refs_1_
  64.3 0.0 collective-permute-done.16.refs_2_
  64.3 1.8 %collective-permute-done.17.refs_3_ = bf16[4,128,128]{2,1,0:T(8,128)(2,1)S(1)} collective-permute-done((bf16[4,128,128]{2,1,0:T(8,128)(2,1)S(1)}, bf16[4,128,128]{2,1,0:T(8,128)(2,1)S(1)}, u32[]{:S(2)}, u32[]{:S(2)}) %collective-permute-start.17) | collective-permute-done | bytes 131104 | tf_op jit(solution)/shard_map/ppermute | solution.py:446
  66.0 2.2 %adam_update.1 = (bf16[4,128,128]{2,1,0:T(8,128)(2,1)}, f32[4,128,128]{2,1,0:T(8,128)}, f32[4,128,128]{2,1,0:T(8,128)}) custom-call(s32[32,128]{1,0:T(8,128)S(1)} %get-tuple-element.79.meta_s, bf16[4,128,128]{2,1,0:T(8,128)(2,1)S(1)} %copy-done.2, f32[4,128,128]{2,1,0:T(8,128)S(1)} %copy-done.3, f32[4,128,128]{2,1,0:T(8,128)S(1)} %copy-done.4, ...), custom_call_target="tpu_custom_call" | custom-call | tf_op jit(solution)/shard_map/adam_update/pallas_call | solution.py:565
  68.2 0.4 collective-permute-done.19.first_ref
  68.6 0.9 %finish_input_grad.1 = bf16[128,2048]{1,0:T(8,128)(2,1)} custom-call(f32[128,2048]{1,0:T(8,128)S(1)} %get-tuple-element.80.own_ref, bf16[128,2048]{1,0:T(8,128)(2,1)S(1)} %collective-permute-done.19.first_ref, bf16[128,2048]{1,0:T(8,128)(2,1)S(1)} %collective-permute-done.20.second_ref), custom_call_target="tpu_custom_call" | custom-call | tf_op jit(solution)/shard_map/finish_input_grad/pallas_call | solution.py:490
  (13 shorter events, 0.1 us)
Async XLA Ops:
  0.6 19.4 %collective-permute-start.7 = (bf16[128,2048]{1,0:T(8,128)(2,1)}, bf16[128,2048]{1,0:T(8,128)(2,1)S(1)}, u32[]{:S(2)}, u32[]{:S(2)}) collective-permute-start(bf16[128,2048]{1,0:T(8,128)(2,1)} %own_h), channel_id=1, source_target_pairs={{0,1},{1,0},{2,3},{3,2},{4,5},{5,4},{6,7},{7,6},{8,9},{9,8},{10,11... | collective-permute-start | bytes 1572872 | tf_op jit(solution)/shard_map/ppermute | solution.py:590
  3.7 16.4 %collective-permute-start.8 = (bf16[128,2048]{1,0:T(8,128)(2,1)}, bf16[128,2048]{1,0:T(8,128)(2,1)S(1)}, u32[]{:S(2)}, u32[]{:S(2)}) collective-permute-start(bf16[128,2048]{1,0:T(8,128)(2,1)} %own_h), channel_id=1, source_target_pairs={{1,2},{2,1},{5,6},{6,5},{9,10},{10,9},{13,14},{14,13},{17,18},{18,... | collective-permute-start | bytes 1572872 | tf_op jit(solution)/shard_map/ppermute | solution.py:591
  6.0 6.4 %collective-permute-start = (bf16[576,128]{1,0:T(8,128)(2,1)}, bf16[576,128]{1,0:T(8,128)(2,1)S(1)}, u32[]{:S(2)}, u32[]{:S(2)}) collective-permute-start(bf16[576,128]{1,0:T(8,128)(2,1)} %pack_blocks.1.refs_1_), channel_id=1, source_target_pairs={{0,8},{4,12},{8,0},{12,4},{16,24},{20,28},{24,16},{28,20},{1,9},{5... | collective-permute-start | bytes 442376 | tf_op jit(solution)/shard_map/ppermute | solution.py:595
  7.6 8.5 %collective-permute-start.1 = (bf16[576,128]{1,0:T(8,128)(2,1)}, bf16[576,128]{1,0:T(8,128)(2,1)S(1)}, u32[]{:S(2)}, u32[]{:S(2)}) collective-permute-start(bf16[576,128]{1,0:T(8,128)(2,1)} %pack_blocks.1.refs_1_), channel_id=1, source_target_pairs={{0,16},{4,20},{8,24},{12,28},{16,0},{20,4},{24,8},{28,12},{1,17},{... | collective-permute-start | bytes 442376 | tf_op jit(solution)/shard_map/ppermute | solution.py:595
  9.1 7.0 %collective-permute-start.2 = (bf16[576,128]{1,0:T(8,128)(2,1)}, bf16[576,128]{1,0:T(8,128)(2,1)S(1)}, u32[]{:S(2)}, u32[]{:S(2)}) collective-permute-start(bf16[576,128]{1,0:T(8,128)(2,1)} %pack_blocks.1.refs_1_), channel_id=1, source_target_pairs={{0,24},{4,28},{8,16},{12,20},{16,8},{20,12},{24,0},{28,4},{1,25},{... | collective-permute-start | bytes 442376 | tf_op jit(solution)/shard_map/ppermute | solution.py:595
  9.6 1.5 %copy-start = (bf16[128,7168]{1,0:T(8,128)(2,1)S(1)}, bf16[128,7168]{1,0:T(8,128)(2,1)}, u32[]{:S(2)}) copy-start(bf16[128,7168]{1,0:T(8,128)(2,1)} %up_ref.1) | copy-start | bytes 5505028
  11.1 0.9 %copy-start.5 = (bf16[576,128]{1,0:T(8,128)(2,1)S(1)}, bf16[576,128]{1,0:T(8,128)(2,1)}, u32[]{:S(2)}) copy-start(bf16[576,128]{1,0:T(8,128)(2,1)} %pack_blocks.1.refs_1_) | copy-start | bytes 442372
  12.4 4.2 %collective-permute-start.3 = (bf16[576,128]{1,0:T(8,128)(2,1)S(1)}, bf16[576,128]{1,0:T(8,128)(2,1)S(1)}, u32[]{:S(2)}, u32[]{:S(2)}) collective-permute-start(bf16[576,128]{1,0:T(8,128)(2,1)S(1)} %get-tuple-element.44.refs_0_), channel_id=1, source_target_pairs={{0,4},{4,0},{8,12},{12,8},{16,20},{20,16},{24,28},{28,24},{1,5},{5... | collective-permute-start | bytes 442376 | tf_op jit(solution)/shard_map/ppermute | solution.py:600
  16.1 1.4 %collective-permute-start.4 = (bf16[576,128]{1,0:T(8,128)(2,1)S(1)}, bf16[576,128]{1,0:T(8,128)(2,1)S(1)}, u32[]{:S(2)}, u32[]{:S(2)}) collective-permute-start(bf16[576,128]{1,0:T(8,128)(2,1)S(1)} %collective-permute-done.refs_1_), channel_id=1, source_target_pairs={{0,4},{4,0},{8,12},{12,8},{16,20},{20,16},{24,28},{28,24},{1,5},{5... | collective-permute-start | bytes 442376 | tf_op jit(solution)/shard_map/ppermute | solution.py:600
  16.1 1.6 %collective-permute-start.5 = (bf16[576,128]{1,0:T(8,128)(2,1)S(1)}, bf16[576,128]{1,0:T(8,128)(2,1)S(1)}, u32[]{:S(2)}, u32[]{:S(2)}) collective-permute-start(bf16[576,128]{1,0:T(8,128)(2,1)S(1)} %collective-permute-done.1.refs_2_), channel_id=1, source_target_pairs={{0,4},{4,0},{8,12},{12,8},{16,20},{20,16},{24,28},{28,24},{1,5},{5... | collective-permute-start | bytes 442376 | tf_op jit(solution)/shard_map/ppermute | solution.py:600
  16.6 1.4 %collective-permute-start.6 = (bf16[576,128]{1,0:T(8,128)(2,1)S(1)}, bf16[576,128]{1,0:T(8,128)(2,1)S(1)}, u32[]{:S(2)}, u32[]{:S(2)}) collective-permute-start(bf16[576,128]{1,0:T(8,128)(2,1)S(1)} %collective-permute-done.2.refs_3_), channel_id=1, source_target_pairs={{0,4},{4,0},{8,12},{12,8},{16,20},{20,16},{24,28},{28,24},{1,5},{5... | collective-permute-start | bytes 442376 | tf_op jit(solution)/shard_map/ppermute | solution.py:600
  20.2 16.7 %collective-permute-start.9 = (bf16[128,2048]{1,0:T(8,128)(2,1)S(1)}, bf16[128,2048]{1,0:T(8,128)(2,1)S(1)}, u32[]{:S(2)}, u32[]{:S(2)}) collective-permute-start(bf16[128,2048]{1,0:T(8,128)(2,1)S(1)} %choose_sent.2), channel_id=1, source_target_pairs={{0,1},{3,2},{1,0},{2,3},{4,5},{7,6},{5,4},{6,7},{8,9},{11,10},{9,8... | collective-permute-start | bytes 1572872 | tf_op jit(solution)/shard_map/ppermute | solution.py:610
  24.6 12.3 %collective-permute-start.10 = (bf16[128,2048]{1,0:T(8,128)(2,1)S(1)}, bf16[128,2048]{1,0:T(8,128)(2,1)S(1)}, u32[]{:S(2)}, u32[]{:S(2)}) collective-permute-start(bf16[128,2048]{1,0:T(8,128)(2,1)S(1)} %collective-permute-done.7.refs_0_), channel_id=1, source_target_pairs={{1,2},{2,1},{5,6},{6,5},{9,10},{10,9},{13,14},{14,13},{17,18},{18,... | collective-permute-start | bytes 1572872 | tf_op jit(solution)/shard_map/ppermute | solution.py:611
  25.6 15.8 %copy-start.6 = (bf16[128,2048]{1,0:T(8,128)(2,1)S(1)}, bf16[128,2048]{1,0:T(8,128)(2,1)}, u32[]{:S(2)}) copy-start(bf16[128,2048]{1,0:T(8,128)(2,1)} %own_h) | copy-start | bytes 1572868
  37.0 4.6 %copy-start.1 = (bf16[128,7168]{1,0:T(8,128)(2,1)S(1)}, bf16[128,7168]{1,0:T(8,128)(2,1)}, u32[]{:S(2)}) copy-start(bf16[128,7168]{1,0:T(8,128)(2,1)} %up_ref.1) | copy-start | bytes 5505028
  37.0 15.1 %collective-permute-start.13 = (bf16[128,2048]{1,0:T(8,128)(2,1)S(1)}, bf16[128,2048]{1,0:T(8,128)(2,1)S(1)}, u32[]{:S(2)}, u32[]{:S(2)}) collective-permute-start(bf16[128,2048]{1,0:T(8,128)(2,1)S(1)} %choose_sent.3), channel_id=1, source_target_pairs={{0,1},{3,2},{1,0},{2,3},{4,5},{7,6},{5,4},{6,7},{8,9},{11,10},{9,8... | collective-permute-start | bytes 1572872 | tf_op jit(solution)/shard_map/ppermute | solution.py:618
  40.7 13.4 %collective-permute-start.18 = (bf16[128,2048]{1,0:T(8,128)(2,1)S(1)}, bf16[128,2048]{1,0:T(8,128)(2,1)S(1)}, u32[]{:S(2)}, u32[]{:S(2)}) collective-permute-start(bf16[128,2048]{1,0:T(8,128)(2,1)S(1)} %inner_sum.1), channel_id=1, source_target_pairs={{1,2},{2,1},{5,6},{6,5},{9,10},{10,9},{13,14},{14,13},{17,18},{18,... | collective-permute-start | bytes 1572872 | tf_op jit(solution)/shard_map/ppermute | solution.py:619
  41.6 1.2 %copy-start.2 = (bf16[4,128,128]{2,1,0:T(8,128)(2,1)S(1)}, bf16[4,128,128]{2,1,0:T(8,128)(2,1)}, u32[]{:S(2)}) copy-start(bf16[4,128,128]{2,1,0:T(8,128)(2,1)} %w_ref.1) | copy-start | bytes 393220
  41.6 1.2 %copy-start.3 = (f32[4,128,128]{2,1,0:T(8,128)S(1)}, f32[4,128,128]{2,1,0:T(8,128)}, u32[]{:S(2)}) copy-start(f32[4,128,128]{2,1,0:T(8,128)} %one_ref.1) | copy-start | bytes 786436
  41.6 1.2 %copy-start.4 = (f32[4,128,128]{2,1,0:T(8,128)S(1)}, f32[4,128,128]{2,1,0:T(8,128)}, u32[]{:S(2)}) copy-start(f32[4,128,128]{2,1,0:T(8,128)} %two_ref.1) | copy-start | bytes 786436
  41.6 1.2 %copy-start.7 = (s32[4]{0:T(128)S(1)}, s32[4]{0:T(128)}, u32[]{:S(2)}) copy-start(s32[4]{0:T(128)} %dest_h.2) | copy-start | bytes 52
  43.5 14.5 %collective-permute-start.11 = (bf16[768,128]{1,0:T(8,128)(2,1)S(1)}, bf16[768,128]{1,0:T(8,128)(2,1)S(1)}, u32[]{:S(2)}, u32[]{:S(2)}) collective-permute-start(bf16[768,128]{1,0:T(8,128)(2,1)S(1)} %get-tuple-element.66), channel_id=1, source_target_pairs={{0,4},{4,8},{8,12},{12,16},{16,20},{20,24},{24,28},{1,5},{5,9},{9,... | collective-permute-start | bytes 589832 | tf_op jit(solution)/shard_map/ppermute | solution.py:629
  44.8 14.0 %collective-permute-start.12 = (bf16[768,128]{1,0:T(8,128)(2,1)S(1)}, bf16[768,128]{1,0:T(8,128)(2,1)S(1)}, u32[]{:S(2)}, u32[]{:S(2)}) collective-permute-start(bf16[768,128]{1,0:T(8,128)(2,1)S(1)} %get-tuple-element.67), channel_id=1, source_target_pairs={{4,0},{8,4},{12,8},{16,12},{20,16},{24,20},{28,24},{5,1},{9,5},{13... | collective-permute-start | bytes 589832 | tf_op jit(solution)/shard_map/ppermute | solution.py:630
  53.9 2.9 %collective-permute-start.14 = (bf16[16,128,128]{2,1,0:T(8,128)(2,1)S(1)}, bf16[16,128,128]{2,1,0:T(8,128)(2,1)S(1)}, u32[]{:S(2)}, u32[]{:S(2)}) collective-permute-start(bf16[16,128,128]{2,1,0:T(8,128)(2,1)S(1)} %get-tuple-element.70), channel_id=1, source_target_pairs={{0,4},{4,0},{8,12},{12,8},{16,20},{20,16},{24,28},{28,24},{1,5},{5... | collective-permute-start | bytes 1572872 | tf_op jit(solution)/shard_map/ppermute | solution.py:439
  54.2 14.4 %collective-permute-start.19 = (bf16[128,2048]{1,0:T(8,128)(2,1)S(1)}, bf16[128,2048]{1,0:T(8,128)(2,1)S(1)}, u32[]{:S(2)}, u32[]{:S(2)}) collective-permute-start(bf16[128,2048]{1,0:T(8,128)(2,1)S(1)} %add_convert_fusion), channel_id=1, source_target_pairs={{0,1},{3,2},{1,0},{2,3},{4,5},{7,6},{5,4},{6,7},{8,9},{11,10},{9,8... | collective-permute-start | bytes 1572872 | tf_op jit(solution)/shard_map/ppermute | solution.py:639
  56.1 12.5 %collective-permute-start.20 = (bf16[128,2048]{1,0:T(8,128)(2,1)S(1)}, bf16[128,2048]{1,0:T(8,128)(2,1)S(1)}, u32[]{:S(2)}, u32[]{:S(2)}) collective-permute-start(bf16[128,2048]{1,0:T(8,128)(2,1)S(1)} %add_convert_fusion.1), channel_id=1, source_target_pairs={{1,2},{2,1},{5,6},{6,5},{9,10},{10,9},{13,14},{14,13},{17,18},{18,... | collective-permute-start | bytes 1572872 | tf_op jit(solution)/shard_map/ppermute | solution.py:638
  57.0 7.2 %collective-permute-start.15 = (bf16[4,128,128]{2,1,0:T(8,128)(2,1)S(1)}, bf16[4,128,128]{2,1,0:T(8,128)(2,1)S(1)}, u32[]{:S(2)}, u32[]{:S(2)}) collective-permute-start(bf16[4,128,128]{2,1,0:T(8,128)(2,1)S(1)} %get-tuple-element.85), channel_id=1, source_target_pairs={{0,8},{4,12},{8,0},{12,4},{16,24},{20,28},{24,16},{28,20},{1,9},{5... | collective-permute-start | bytes 393224 | tf_op jit(solution)/shard_map/ppermute | solution.py:446
  58.0 6.3 %collective-permute-start.16 = (bf16[4,128,128]{2,1,0:T(8,128)(2,1)S(1)}, bf16[4,128,128]{2,1,0:T(8,128)(2,1)S(1)}, u32[]{:S(2)}, u32[]{:S(2)}) collective-permute-start(bf16[4,128,128]{2,1,0:T(8,128)(2,1)S(1)} %get-tuple-element.84), channel_id=1, source_target_pairs={{0,16},{4,20},{8,24},{12,28},{16,0},{20,4},{24,8},{28,12},{1,17},{... | collective-permute-start | bytes 393224 | tf_op jit(solution)/shard_map/ppermute | solution.py:446
  58.8 7.3 %collective-permute-start.17 = (bf16[4,128,128]{2,1,0:T(8,128)(2,1)S(1)}, bf16[4,128,128]{2,1,0:T(8,128)(2,1)S(1)}, u32[]{:S(2)}, u32[]{:S(2)}) collective-permute-start(bf16[4,128,128]{2,1,0:T(8,128)(2,1)S(1)} %get-tuple-element.83), channel_id=1, source_target_pairs={{0,24},{4,28},{8,16},{12,20},{16,8},{20,12},{24,0},{28,4},{1,25},{... | collective-permute-start | bytes 393224 | tf_op jit(solution)/shard_map/ppermute | solution.py:446

commit v7 on v6

--- a/solution.py
+++ b/solution.py
@@ -32,24 +32,27 @@
     return ref[:, pl.ds(pl.multiple_of(index * width, width), width)]
 
 
-def pack_kernel(row_h, col_h, dest_h, w_h, pack_ref, row_s, col_s, dest_s, w_ref, sems):
-    kept, side = w_ref.shape[0], w_ref.shape[1]
+def pack_kernel(row_h, col_h, dest_h, w_h, pack_ref, row_s, col_s, dest_s, sems):
+    kept, side = w_h.shape[0], w_h.shape[1]
     pitch = side + TILE
-    copies = [
+    names = [
         pltpu.make_async_copy(source, target, sems.at[i])
-        for i, (source, target) in enumerate(
-            ((row_h, row_s), (col_h, col_s), (dest_h, dest_s), (w_h, w_ref))
-        )
+        for i, (source, target) in enumerate(((row_h, row_s), (col_h, col_s), (dest_h, dest_s)))
     ]
-    for copy in copies:
+    blocks = [
+        pltpu.make_async_copy(w_h.at[s], pack_ref.at[pl.ds(s * pitch, side)], sems.at[3 + s])
+        for s in range(kept)
+    ]
+    for copy in names + blocks:
         copy.start()
-    for copy in copies:
+    for copy in names:
         copy.wait()
     lane = lax.broadcasted_iota(jnp.int32, (TILE, side), 1)
     for s in range(kept):
         tile = jnp.where(lane == 0, row_s[s], jnp.where(lane == 1, col_s[s], dest_s[s]))
-        pack_ref[s * pitch : s * pitch + side, :] = w_ref[s]
         pack_ref[s * pitch + side : (s + 1) * pitch, :] = tile.astype(f32).astype(bf16)
+    for copy in blocks:
+        copy.wait()
 
 
 def pack(rows, cols, dests, weight):
@@ -60,7 +63,7 @@
         in_specs=[ANY] * 4,
         out_specs=VMEM,
         scratch_shapes=[pltpu.SMEM((kept,), jnp.int32)] * 3
-        + [pltpu.VMEM(weight.shape, bf16), pltpu.SemaphoreType.DMA((4,))],
+        + [pltpu.SemaphoreType.DMA((3 + kept,))],
         compiler_params=params(60),
         cost_estimate=pl.CostEstimate(flops=0, bytes_accessed=0, transcendentals=0),
         name="pack_blocks",

time: 70.5 us -> 70.5 us (level)
  no operation moved by 1% of the time
where the time goes in v7:
time: 70.5 us; the launch traced here: 69.5 us
  starting transfers between devices  26.1 us (37%)
  waiting for transfers between devices  24.7 us (35%)
  Pallas kernels  14.8 us (21%)
  local copies, waits for them, and re-layouts  2.49 us (4%)
  between operations  0.96 us (1%)
    ppermute x1, waiting for transfers between devices, body(): mixed = lax.ppermute(mixed, 'mp', inward + outward)  11.3 us
    ppermute x1, waiting for transfers between devices, body(): mixed_on = lax.ppermute(mixed_on, 'mp', inward + outward)  6.04 us
    ppermute x1, starting transfers between devices, body(): mixed = lax.ppermute(mixed, 'mp', inward + outward)  4.43 us
    ppermute x3, waiting for transfers between devices, body(): lax.ppermute(packs[0], 'dp', [(i, i ^ gap) for i in range(dp)])  3.73 us
    pallas_call x1, Pallas kernels, forward(): pl.pallas_call(functools.partial(forward_kernel, kept, ids), out_shape=ja...  3.67 us
    ppermute x1, starting transfers between devices, body(): mixed_on = lax.ppermute(mixed_on, 'mp', inward + outward)  3.65 us
    ppermute x3, starting transfers between devices, slot_reduce(): lax.ppermute(totals[gap], 'dp', [(i, i ^ 2 * gap) for i in range(dp)])  3.55 us
    ppermute x3, starting transfers between devices, body(): lax.ppermute(packs[0], 'dp', [(i, i ^ gap) for i in range(dp)])  3.55 us
  transfers between devices with their start and end apart: 21, of which 9 were waited for; matrix products, arithmetic and copies ran while one was open for 1% of the time, Pallas kernels for 20%

profile of v7, /device:TPU:0, one launch (start us, length us, event | category | flops | bytes accessed | tf_op | source)
XLA Modules:
  0.0 69.5 jit_solution(7610656114809148160)
XLA Ops:
  0.6 3.1 %collective-permute-start.7 = (bf16[128,2048]{1,0:T(8,128)(2,1)}, bf16[128,2048]{1,0:T(8,128)(2,1)S(1)}, u32[]{:S(2)}, u32[]{:S(2)}) collective-permute-start(bf16[128,2048]{1,0:T(8,128)(2,1)} %own_h), channel_id=1, source_target_pairs={{0,1},{1,0},{2,3},{3,2},{4,5},{5,4},{6,7},{7,6},{8,9},{9,8},{10,11... | collective-permute-start | bytes 1572872 | tf_op jit(solution)/shard_map/ppermute | solution.py:593
  3.7 0.7 collective-permute-start.8
  4.4 1.5 %pack_blocks.1.refs_1_ = bf16[576,128]{1,0:T(8,128)(2,1)} custom-call(s32[4]{0:T(128)} %row_h.1, s32[4]{0:T(128)} %col_h.1, s32[4]{0:T(128)} %dest_h.2, bf16[4,128,128]{2,1,0:T(8,128)(2,1)} %w_ref.1), custom_call_target="tpu_custom_call" | custom-call | tf_op jit(solution)/shard_map/pack_blocks/pallas_call | solution.py:60
  6.0 1.6 %collective-permute-start = (bf16[576,128]{1,0:T(8,128)(2,1)}, bf16[576,128]{1,0:T(8,128)(2,1)S(1)}, u32[]{:S(2)}, u32[]{:S(2)}) collective-permute-start(bf16[576,128]{1,0:T(8,128)(2,1)} %pack_blocks.1.refs_1_), channel_id=1, source_target_pairs={{0,8},{4,12},{8,0},{12,4},{16,24},{20,28},{24,16},{28,20},{1,9},{5... | collective-permute-start | bytes 442376 | tf_op jit(solution)/shard_map/ppermute | solution.py:598
  7.5 1.5 %collective-permute-start.1 = (bf16[576,128]{1,0:T(8,128)(2,1)}, bf16[576,128]{1,0:T(8,128)(2,1)S(1)}, u32[]{:S(2)}, u32[]{:S(2)}) collective-permute-start(bf16[576,128]{1,0:T(8,128)(2,1)} %pack_blocks.1.refs_1_), channel_id=1, source_target_pairs={{0,16},{4,20},{8,24},{12,28},{16,0},{20,4},{24,8},{28,12},{1,17},{... | collective-permute-start | bytes 442376 | tf_op jit(solution)/shard_map/ppermute | solution.py:598
  9.0 0.5 collective-permute-start.2
  9.5 1.5 %copy-done = bf16[128,7168]{1,0:T(8,128)(2,1)S(1)} copy-done((bf16[128,7168]{1,0:T(8,128)(2,1)S(1)}, bf16[128,7168]{1,0:T(8,128)(2,1)}, u32[]{:S(2)}) %copy-start) | copy-done | bytes 1835032
  11.0 0.9 %copy-done.5 = bf16[576,128]{1,0:T(8,128)(2,1)S(1)} copy-done((bf16[576,128]{1,0:T(8,128)(2,1)S(1)}, bf16[576,128]{1,0:T(8,128)(2,1)}, u32[]{:S(2)}) %copy-start.5) | copy-done | bytes 147480
  11.9 0.3 hold_arrays.1
  12.3 0.1 collective-permute-done.refs_1_
  12.3 0.0 collective-permute-start.3
  12.3 3.7 %collective-permute-done.1.refs_2_ = bf16[576,128]{1,0:T(8,128)(2,1)S(1)} collective-permute-done((bf16[576,128]{1,0:T(8,128)(2,1)}, bf16[576,128]{1,0:T(8,128)(2,1)S(1)}, u32[]{:S(2)}, u32[]{:S(2)}) %collective-permute-start.1) | collective-permute-done | bytes 147488 | tf_op jit(solution)/shard_map/ppermute | solution.py:598
  16.0 0.0 collective-permute-done.2.refs_3_
  16.0 0.0 collective-permute-start.4
  16.0 0.5 collective-permute-start.5
  16.5 0.0 collective-permute-done.3.refs_4_
  16.5 0.0 collective-permute-start.6
  16.5 0.9 %collective-permute-done.4.refs_5_ = bf16[576,128]{1,0:T(8,128)(2,1)S(1)} collective-permute-done((bf16[576,128]{1,0:T(8,128)(2,1)S(1)}, bf16[576,128]{1,0:T(8,128)(2,1)S(1)}, u32[]{:S(2)}, u32[]{:S(2)}) %collective-permute-start.4) | collective-permute-done | bytes 147488 | tf_op jit(solution)/shard_map/ppermute | solution.py:603
  17.4 0.2 collective-permute-done.5.refs_6_
  17.6 0.3 collective-permute-done.6.refs_7_
  17.9 2.1 %input_gradient.1 = (f32[128,8192]{1,0:T(8,128)S(1)}, s32[32,128]{1,0:T(8,128)S(1)}, bf16[128,2048]{1,0:T(8,128)(2,1)S(1)}) custom-call(bf16[576,128]{1,0:T(8,128)(2,1)S(1)} %get-tuple-element.44.refs_0_, bf16[576,128]{1,0:T(8,128)(2,1)S(1)} %collective-permute-done.refs_1_, bf16[576,128]{1,0:T(8,128)(2,1)S(1)} %collective-permute-done.1.refs_2_, ...), custom_call_target="tpu_custom_call" | custom-call | tf_op jit(solution)/shard_map/input_gradient/pallas_call | solution.py:232
  20.0 0.0 collective-permute-done.7.refs_0_
  20.0 0.0 collective-permute-done.8.inner_h.refs_1_
  20.0 0.1 choose_sent.2
  20.1 4.4 %collective-permute-start.9 = (bf16[128,2048]{1,0:T(8,128)(2,1)S(1)}, bf16[128,2048]{1,0:T(8,128)(2,1)S(1)}, u32[]{:S(2)}, u32[]{:S(2)}) collective-permute-start(bf16[128,2048]{1,0:T(8,128)(2,1)S(1)} %choose_sent.2), channel_id=1, source_target_pairs={{0,1},{3,2},{1,0},{2,3},{4,5},{7,6},{5,4},{6,7},{8,9},{11,10},{9,8... | collective-permute-start | bytes 1572872 | tf_op jit(solution)/shard_map/ppermute | solution.py:613
  24.5 0.7 collective-permute-start.10
  25.2 0.3 split_shares.1
  25.5 0.0 copy-start.6
  25.5 11.3 %collective-permute-done.9.came_h.refs_3_ = bf16[128,2048]{1,0:T(8,128)(2,1)S(1)} collective-permute-done((bf16[128,2048]{1,0:T(8,128)(2,1)S(1)}, bf16[128,2048]{1,0:T(8,128)(2,1)S(1)}, u32[]{:S(2)}, u32[]{:S(2)}) %collective-permute-start.9) | collective-permute-done | bytes 524320 | tf_op jit(solution)/shard_map/ppermute | solution.py:613
  36.8 0.0 collective-permute-done.10.inner_h.refs_2_
  36.8 0.1 choose_sent.3
  36.9 0.0 copy-start.1
  36.9 3.7 %collective-permute-start.13 = (bf16[128,2048]{1,0:T(8,128)(2,1)S(1)}, bf16[128,2048]{1,0:T(8,128)(2,1)S(1)}, u32[]{:S(2)}, u32[]{:S(2)}) collective-permute-start(bf16[128,2048]{1,0:T(8,128)(2,1)S(1)} %choose_sent.3), channel_id=1, source_target_pairs={{0,1},{3,2},{1,0},{2,3},{4,5},{7,6},{5,4},{6,7},{8,9},{11,10},{9,8... | collective-permute-start | bytes 1572872 | tf_op jit(solution)/shard_map/ppermute | solution.py:621
  40.6 0.7 collective-permute-start.18
  41.3 0.2 assemble_tokens.1.x_ref.refs_8_
  41.5 0.0 copy-start.2
  41.5 0.0 copy-start.3
  41.5 0.0 copy-start.4
  41.5 0.0 copy-start.7
  41.5 1.1 %turn_upstream.1.turned_ref = bf16[32,128,128]{2,1,0:T(8,128)(2,1)S(1)} custom-call(s32[32,128]{1,0:T(8,128)S(1)} %get-tuple-element.79.meta_s, bf16[128,7168]{1,0:T(8,128)(2,1)S(1)} %copy-done.1), custom_call_target="tpu_custom_call" | custom-call | tf_op jit(solution)/shard_map/turn_upstream/pallas_call | solution.py:394
  42.7 0.7 leaving_blocks.1
  43.4 1.3 %collective-permute-start.11 = (bf16[768,128]{1,0:T(8,128)(2,1)S(1)}, bf16[768,128]{1,0:T(8,128)(2,1)S(1)}, u32[]{:S(2)}, u32[]{:S(2)}) collective-permute-start(bf16[768,128]{1,0:T(8,128)(2,1)S(1)} %get-tuple-element.66), channel_id=1, source_target_pairs={{0,4},{4,8},{8,12},{12,16},{16,20},{20,24},{24,28},{1,5},{5,9},{9,... | collective-permute-start | bytes 589832 | tf_op jit(solution)/shard_map/ppermute | solution.py:632
  44.7 1.3 %collective-permute-start.12 = (bf16[768,128]{1,0:T(8,128)(2,1)S(1)}, bf16[768,128]{1,0:T(8,128)(2,1)S(1)}, u32[]{:S(2)}, u32[]{:S(2)}) collective-permute-start(bf16[768,128]{1,0:T(8,128)(2,1)S(1)} %get-tuple-element.67), channel_id=1, source_target_pairs={{4,0},{8,4},{12,8},{16,12},{20,16},{24,20},{28,24},{5,1},{9,5},{13... | collective-permute-start | bytes 589832 | tf_op jit(solution)/shard_map/ppermute | solution.py:633
  46.0 6.0 %collective-permute-done.13.refs_0_.refs_9_ = bf16[128,2048]{1,0:T(8,128)(2,1)S(1)} collective-permute-done((bf16[128,2048]{1,0:T(8,128)(2,1)S(1)}, bf16[128,2048]{1,0:T(8,128)(2,1)S(1)}, u32[]{:S(2)}, u32[]{:S(2)}) %collective-permute-start.13) | collective-permute-done | bytes 524320 | tf_op jit(solution)/shard_map/ppermute | solution.py:621
  52.1 1.7 %weight_gradient.1 = (f32[33,128,128]{2,1,0:T(8,128)S(1)}, bf16[16,128,128]{2,1,0:T(8,128)(2,1)S(1)}) custom-call(s32[32,128]{1,0:T(8,128)S(1)} %get-tuple-element.79.meta_s, bf16[32,128,128]{2,1,0:T(8,128)(2,1)S(1)} %turn_upstream.1.turned_ref, bf16[4,128,2048]{2,1,0:T(8,128)(2,1)S(1)} %assemble_tokens.1.x_ref.refs_8_, ...), custom_call_target="tpu_custom_call" | custom-call | tf_op jit(solution)/shard_map/weight_gradient/pallas_call | solution.py:427
  53.8 0.1 collective-permute-start.14
  53.9 0.1 add_convert_fusion.1
  54.0 0.0 collective-permute-done.18
  54.0 0.1 add_convert_fusion
  54.1 1.9 %collective-permute-start.19 = (bf16[128,2048]{1,0:T(8,128)(2,1)S(1)}, bf16[128,2048]{1,0:T(8,128)(2,1)S(1)}, u32[]{:S(2)}, u32[]{:S(2)}) collective-permute-start(bf16[128,2048]{1,0:T(8,128)(2,1)S(1)} %add_convert_fusion), channel_id=1, source_target_pairs={{0,1},{3,2},{1,0},{2,3},{4,5},{7,6},{5,4},{6,7},{8,9},{11,10},{9,8... | collective-permute-start | bytes 1572872 | tf_op jit(solution)/shard_map/ppermute | solution.py:642
  56.0 0.7 collective-permute-start.20
  56.7 0.0 collective-permute-done.14
  56.7 0.2 fusion
  57.0 0.9 %collective-permute-start.15 = (bf16[4,128,128]{2,1,0:T(8,128)(2,1)S(1)}, bf16[4,128,128]{2,1,0:T(8,128)(2,1)S(1)}, u32[]{:S(2)}, u32[]{:S(2)}) collective-permute-start(bf16[4,128,128]{2,1,0:T(8,128)(2,1)S(1)} %get-tuple-element.85), channel_id=1, source_target_pairs={{0,8},{4,12},{8,0},{12,4},{16,24},{20,28},{24,16},{28,20},{1,9},{5... | collective-permute-start | bytes 393224 | tf_op jit(solution)/shard_map/ppermute | solution.py:449
  57.9 0.0 collective-permute-done.11.left_ref
  57.9 0.8 %collective-permute-start.16 = (bf16[4,128,128]{2,1,0:T(8,128)(2,1)S(1)}, bf16[4,128,128]{2,1,0:T(8,128)(2,1)S(1)}, u32[]{:S(2)}, u32[]{:S(2)}) collective-permute-start(bf16[4,128,128]{2,1,0:T(8,128)(2,1)S(1)} %get-tuple-element.84), channel_id=1, source_target_pairs={{0,16},{4,20},{8,24},{12,28},{16,0},{20,4},{24,8},{28,12},{1,17},{... | collective-permute-start | bytes 393224 | tf_op jit(solution)/shard_map/ppermute | solution.py:449
  58.7 1.8 %collective-permute-start.17 = (bf16[4,128,128]{2,1,0:T(8,128)(2,1)S(1)}, bf16[4,128,128]{2,1,0:T(8,128)(2,1)S(1)}, u32[]{:S(2)}, u32[]{:S(2)}) collective-permute-start(bf16[4,128,128]{2,1,0:T(8,128)(2,1)S(1)} %get-tuple-element.83), channel_id=1, source_target_pairs={{0,24},{4,28},{8,16},{12,20},{16,8},{20,12},{24,0},{28,4},{1,25},{... | collective-permute-start | bytes 393224 | tf_op jit(solution)/shard_map/ppermute | solution.py:449
  60.5 3.7 %hidden_out.1 = bf16[128,7168]{1,0:T(8,128)(2,1)} custom-call(s32[32,128]{1,0:T(8,128)S(1)} %get-tuple-element.79.meta_s, bf16[576,128]{1,0:T(8,128)(2,1)S(1)} %get-tuple-element.44.refs_0_, bf16[576,128]{1,0:T(8,128)(2,1)S(1)} %collective-permute-done.refs_1_, bf16[576,128]{1,0:T(8,128)(2,1)S(1)} %collective-permute-done.1.refs_2_, ...), custom_call_target="tpu_custom_call" | custom-call | tf_op jit(solution)/shard_map/hidden_out/pallas_call | solution.py:475
  64.2 0.0 collective-permute-done.15.refs_1_
  64.2 0.0 collective-permute-done.16.refs_2_
  64.2 1.8 %collective-permute-done.17.refs_3_ = bf16[4,128,128]{2,1,0:T(8,128)(2,1)S(1)} collective-permute-done((bf16[4,128,128]{2,1,0:T(8,128)(2,1)S(1)}, bf16[4,128,128]{2,1,0:T(8,128)(2,1)S(1)}, u32[]{:S(2)}, u32[]{:S(2)}) %collective-permute-start.17) | collective-permute-done | bytes 131104 | tf_op jit(solution)/shard_map/ppermute | solution.py:449
  66.0 2.1 %adam_update.1 = (bf16[4,128,128]{2,1,0:T(8,128)(2,1)}, f32[4,128,128]{2,1,0:T(8,128)}, f32[4,128,128]{2,1,0:T(8,128)}) custom-call(s32[32,128]{1,0:T(8,128)S(1)} %get-tuple-element.79.meta_s, bf16[4,128,128]{2,1,0:T(8,128)(2,1)S(1)} %copy-done.2, f32[4,128,128]{2,1,0:T(8,128)S(1)} %copy-done.3, f32[4,128,128]{2,1,0:T(8,128)S(1)} %copy-done.4, ...), custom_call_target="tpu_custom_call" | custom-call | tf_op jit(solution)/shard_map/adam_update/pallas_call | solution.py:568
  68.1 0.5 collective-permute-done.19.first_ref
  68.5 0.9 %finish_input_grad.1 = bf16[128,2048]{1,0:T(8,128)(2,1)} custom-call(f32[128,2048]{1,0:T(8,128)S(1)} %get-tuple-element.80.own_ref, bf16[128,2048]{1,0:T(8,128)(2,1)S(1)} %collective-permute-done.19.first_ref, bf16[128,2048]{1,0:T(8,128)(2,1)S(1)} %collective-permute-done.20.second_ref), custom_call_target="tpu_custom_call" | custom-call | tf_op jit(solution)/shard_map/finish_input_grad/pallas_call | solution.py:493
  (13 shorter events, 0.1 us)
Async XLA Ops:
  0.6 19.4 %collective-permute-start.7 = (bf16[128,2048]{1,0:T(8,128)(2,1)}, bf16[128,2048]{1,0:T(8,128)(2,1)S(1)}, u32[]{:S(2)}, u32[]{:S(2)}) collective-permute-start(bf16[128,2048]{1,0:T(8,128)(2,1)} %own_h), channel_id=1, source_target_pairs={{0,1},{1,0},{2,3},{3,2},{4,5},{5,4},{6,7},{7,6},{8,9},{9,8},{10,11... | collective-permute-start | bytes 1572872 | tf_op jit(solution)/shard_map/ppermute | solution.py:593
  3.7 16.3 %collective-permute-start.8 = (bf16[128,2048]{1,0:T(8,128)(2,1)}, bf16[128,2048]{1,0:T(8,128)(2,1)S(1)}, u32[]{:S(2)}, u32[]{:S(2)}) collective-permute-start(bf16[128,2048]{1,0:T(8,128)(2,1)} %own_h), channel_id=1, source_target_pairs={{1,2},{2,1},{5,6},{6,5},{9,10},{10,9},{13,14},{14,13},{17,18},{18,... | collective-permute-start | bytes 1572872 | tf_op jit(solution)/shard_map/ppermute | solution.py:594
  6.0 6.4 %collective-permute-start = (bf16[576,128]{1,0:T(8,128)(2,1)}, bf16[576,128]{1,0:T(8,128)(2,1)S(1)}, u32[]{:S(2)}, u32[]{:S(2)}) collective-permute-start(bf16[576,128]{1,0:T(8,128)(2,1)} %pack_blocks.1.refs_1_), channel_id=1, source_target_pairs={{0,8},{4,12},{8,0},{12,4},{16,24},{20,28},{24,16},{28,20},{1,9},{5... | collective-permute-start | bytes 442376 | tf_op jit(solution)/shard_map/ppermute | solution.py:598
  7.5 8.5 %collective-permute-start.1 = (bf16[576,128]{1,0:T(8,128)(2,1)}, bf16[576,128]{1,0:T(8,128)(2,1)S(1)}, u32[]{:S(2)}, u32[]{:S(2)}) collective-permute-start(bf16[576,128]{1,0:T(8,128)(2,1)} %pack_blocks.1.refs_1_), channel_id=1, source_target_pairs={{0,16},{4,20},{8,24},{12,28},{16,0},{20,4},{24,8},{28,12},{1,17},{... | collective-permute-start | bytes 442376 | tf_op jit(solution)/shard_map/ppermute | solution.py:598
  9.0 7.0 %collective-permute-start.2 = (bf16[576,128]{1,0:T(8,128)(2,1)}, bf16[576,128]{1,0:T(8,128)(2,1)S(1)}, u32[]{:S(2)}, u32[]{:S(2)}) collective-permute-start(bf16[576,128]{1,0:T(8,128)(2,1)} %pack_blocks.1.refs_1_), channel_id=1, source_target_pairs={{0,24},{4,28},{8,16},{12,20},{16,8},{20,12},{24,0},{28,4},{1,25},{... | collective-permute-start | bytes 442376 | tf_op jit(solution)/shard_map/ppermute | solution.py:598
  9.5 1.5 %copy-start = (bf16[128,7168]{1,0:T(8,128)(2,1)S(1)}, bf16[128,7168]{1,0:T(8,128)(2,1)}, u32[]{:S(2)}) copy-start(bf16[128,7168]{1,0:T(8,128)(2,1)} %up_ref.1) | copy-start | bytes 5505028
  11.0 0.9 %copy-start.5 = (bf16[576,128]{1,0:T(8,128)(2,1)S(1)}, bf16[576,128]{1,0:T(8,128)(2,1)}, u32[]{:S(2)}) copy-start(bf16[576,128]{1,0:T(8,128)(2,1)} %pack_blocks.1.refs_1_) | copy-start | bytes 442372
  12.3 4.2 %collective-permute-start.3 = (bf16[576,128]{1,0:T(8,128)(2,1)S(1)}, bf16[576,128]{1,0:T(8,128)(2,1)S(1)}, u32[]{:S(2)}, u32[]{:S(2)}) collective-permute-start(bf16[576,128]{1,0:T(8,128)(2,1)S(1)} %get-tuple-element.44.refs_0_), channel_id=1, source_target_pairs={{0,4},{4,0},{8,12},{12,8},{16,20},{20,16},{24,28},{28,24},{1,5},{5... | collective-permute-start | bytes 442376 | tf_op jit(solution)/shard_map/ppermute | solution.py:603
  16.0 1.4 %collective-permute-start.4 = (bf16[576,128]{1,0:T(8,128)(2,1)S(1)}, bf16[576,128]{1,0:T(8,128)(2,1)S(1)}, u32[]{:S(2)}, u32[]{:S(2)}) collective-permute-start(bf16[576,128]{1,0:T(8,128)(2,1)S(1)} %collective-permute-done.refs_1_), channel_id=1, source_target_pairs={{0,4},{4,0},{8,12},{12,8},{16,20},{20,16},{24,28},{28,24},{1,5},{5... | collective-permute-start | bytes 442376 | tf_op jit(solution)/shard_map/ppermute | solution.py:603
  16.0 1.6 %collective-permute-start.5 = (bf16[576,128]{1,0:T(8,128)(2,1)S(1)}, bf16[576,128]{1,0:T(8,128)(2,1)S(1)}, u32[]{:S(2)}, u32[]{:S(2)}) collective-permute-start(bf16[576,128]{1,0:T(8,128)(2,1)S(1)} %collective-permute-done.1.refs_2_), channel_id=1, source_target_pairs={{0,4},{4,0},{8,12},{12,8},{16,20},{20,16},{24,28},{28,24},{1,5},{5... | collective-permute-start | bytes 442376 | tf_op jit(solution)/shard_map/ppermute | solution.py:603
  16.5 1.4 %collective-permute-start.6 = (bf16[576,128]{1,0:T(8,128)(2,1)S(1)}, bf16[576,128]{1,0:T(8,128)(2,1)S(1)}, u32[]{:S(2)}, u32[]{:S(2)}) collective-permute-start(bf16[576,128]{1,0:T(8,128)(2,1)S(1)} %collective-permute-done.2.refs_3_), channel_id=1, source_target_pairs={{0,4},{4,0},{8,12},{12,8},{16,20},{20,16},{24,28},{28,24},{1,5},{5... | collective-permute-start | bytes 442376 | tf_op jit(solution)/shard_map/ppermute | solution.py:603
  20.1 16.7 %collective-permute-start.9 = (bf16[128,2048]{1,0:T(8,128)(2,1)S(1)}, bf16[128,2048]{1,0:T(8,128)(2,1)S(1)}, u32[]{:S(2)}, u32[]{:S(2)}) collective-permute-start(bf16[128,2048]{1,0:T(8,128)(2,1)S(1)} %choose_sent.2), channel_id=1, source_target_pairs={{0,1},{3,2},{1,0},{2,3},{4,5},{7,6},{5,4},{6,7},{8,9},{11,10},{9,8... | collective-permute-start | bytes 1572872 | tf_op jit(solution)/shard_map/ppermute | solution.py:613
  24.5 12.3 %collective-permute-start.10 = (bf16[128,2048]{1,0:T(8,128)(2,1)S(1)}, bf16[128,2048]{1,0:T(8,128)(2,1)S(1)}, u32[]{:S(2)}, u32[]{:S(2)}) collective-permute-start(bf16[128,2048]{1,0:T(8,128)(2,1)S(1)} %collective-permute-done.7.refs_0_), channel_id=1, source_target_pairs={{1,2},{2,1},{5,6},{6,5},{9,10},{10,9},{13,14},{14,13},{17,18},{18,... | collective-permute-start | bytes 1572872 | tf_op jit(solution)/shard_map/ppermute | solution.py:614
  25.5 15.8 %copy-start.6 = (bf16[128,2048]{1,0:T(8,128)(2,1)S(1)}, bf16[128,2048]{1,0:T(8,128)(2,1)}, u32[]{:S(2)}) copy-start(bf16[128,2048]{1,0:T(8,128)(2,1)} %own_h) | copy-start | bytes 1572868
  36.9 4.6 %copy-start.1 = (bf16[128,7168]{1,0:T(8,128)(2,1)S(1)}, bf16[128,7168]{1,0:T(8,128)(2,1)}, u32[]{:S(2)}) copy-start(bf16[128,7168]{1,0:T(8,128)(2,1)} %up_ref.1) | copy-start | bytes 5505028
  36.9 15.1 %collective-permute-start.13 = (bf16[128,2048]{1,0:T(8,128)(2,1)S(1)}, bf16[128,2048]{1,0:T(8,128)(2,1)S(1)}, u32[]{:S(2)}, u32[]{:S(2)}) collective-permute-start(bf16[128,2048]{1,0:T(8,128)(2,1)S(1)} %choose_sent.3), channel_id=1, source_target_pairs={{0,1},{3,2},{1,0},{2,3},{4,5},{7,6},{5,4},{6,7},{8,9},{11,10},{9,8... | collective-permute-start | bytes 1572872 | tf_op jit(solution)/shard_map/ppermute | solution.py:621
  40.6 13.4 %collective-permute-start.18 = (bf16[128,2048]{1,0:T(8,128)(2,1)S(1)}, bf16[128,2048]{1,0:T(8,128)(2,1)S(1)}, u32[]{:S(2)}, u32[]{:S(2)}) collective-permute-start(bf16[128,2048]{1,0:T(8,128)(2,1)S(1)} %inner_sum.1), channel_id=1, source_target_pairs={{1,2},{2,1},{5,6},{6,5},{9,10},{10,9},{13,14},{14,13},{17,18},{18,... | collective-permute-start | bytes 1572872 | tf_op jit(solution)/shard_map/ppermute | solution.py:622
  41.5 1.2 %copy-start.2 = (bf16[4,128,128]{2,1,0:T(8,128)(2,1)S(1)}, bf16[4,128,128]{2,1,0:T(8,128)(2,1)}, u32[]{:S(2)}) copy-start(bf16[4,128,128]{2,1,0:T(8,128)(2,1)} %w_ref.1) | copy-start | bytes 393220
  41.5 1.2 %copy-start.3 = (f32[4,128,128]{2,1,0:T(8,128)S(1)}, f32[4,128,128]{2,1,0:T(8,128)}, u32[]{:S(2)}) copy-start(f32[4,128,128]{2,1,0:T(8,128)} %one_ref.1) | copy-start | bytes 786436
  41.5 1.2 %copy-start.4 = (f32[4,128,128]{2,1,0:T(8,128)S(1)}, f32[4,128,128]{2,1,0:T(8,128)}, u32[]{:S(2)}) copy-start(f32[4,128,128]{2,1,0:T(8,128)} %two_ref.1) | copy-start | bytes 786436
  41.5 1.2 %copy-start.7 = (s32[4]{0:T(128)S(1)}, s32[4]{0:T(128)}, u32[]{:S(2)}) copy-start(s32[4]{0:T(128)} %dest_h.2) | copy-start | bytes 52
  43.4 14.5 %collective-permute-start.11 = (bf16[768,128]{1,0:T(8,128)(2,1)S(1)}, bf16[768,128]{1,0:T(8,128)(2,1)S(1)}, u32[]{:S(2)}, u32[]{:S(2)}) collective-permute-start(bf16[768,128]{1,0:T(8,128)(2,1)S(1)} %get-tuple-element.66), channel_id=1, source_target_pairs={{0,4},{4,8},{8,12},{12,16},{16,20},{20,24},{24,28},{1,5},{5,9},{9,... | collective-permute-start | bytes 589832 | tf_op jit(solution)/shard_map/ppermute | solution.py:632
  44.7 14.0 %collective-permute-start.12 = (bf16[768,128]{1,0:T(8,128)(2,1)S(1)}, bf16[768,128]{1,0:T(8,128)(2,1)S(1)}, u32[]{:S(2)}, u32[]{:S(2)}) collective-permute-start(bf16[768,128]{1,0:T(8,128)(2,1)S(1)} %get-tuple-element.67), channel_id=1, source_target_pairs={{4,0},{8,4},{12,8},{16,12},{20,16},{24,20},{28,24},{5,1},{9,5},{13... | collective-permute-start | bytes 589832 | tf_op jit(solution)/shard_map/ppermute | solution.py:633
  53.8 2.9 %collective-permute-start.14 = (bf16[16,128,128]{2,1,0:T(8,128)(2,1)S(1)}, bf16[16,128,128]{2,1,0:T(8,128)(2,1)S(1)}, u32[]{:S(2)}, u32[]{:S(2)}) collective-permute-start(bf16[16,128,128]{2,1,0:T(8,128)(2,1)S(1)} %get-tuple-element.70), channel_id=1, source_target_pairs={{0,4},{4,0},{8,12},{12,8},{16,20},{20,16},{24,28},{28,24},{1,5},{5... | collective-permute-start | bytes 1572872 | tf_op jit(solution)/shard_map/ppermute | solution.py:442
  54.1 14.4 %collective-permute-start.19 = (bf16[128,2048]{1,0:T(8,128)(2,1)S(1)}, bf16[128,2048]{1,0:T(8,128)(2,1)S(1)}, u32[]{:S(2)}, u32[]{:S(2)}) collective-permute-start(bf16[128,2048]{1,0:T(8,128)(2,1)S(1)} %add_convert_fusion), channel_id=1, source_target_pairs={{0,1},{3,2},{1,0},{2,3},{4,5},{7,6},{5,4},{6,7},{8,9},{11,10},{9,8... | collective-permute-start | bytes 1572872 | tf_op jit(solution)/shard_map/ppermute | solution.py:642
  56.0 12.5 %collective-permute-start.20 = (bf16[128,2048]{1,0:T(8,128)(2,1)S(1)}, bf16[128,2048]{1,0:T(8,128)(2,1)S(1)}, u32[]{:S(2)}, u32[]{:S(2)}) collective-permute-start(bf16[128,2048]{1,0:T(8,128)(2,1)S(1)} %add_convert_fusion.1), channel_id=1, source_target_pairs={{1,2},{2,1},{5,6},{6,5},{9,10},{10,9},{13,14},{14,13},{17,18},{18,... | collective-permute-start | bytes 1572872 | tf_op jit(solution)/shard_map/ppermute | solution.py:641
  57.0 7.3 %collective-permute-start.15 = (bf16[4,128,128]{2,1,0:T(8,128)(2,1)S(1)}, bf16[4,128,128]{2,1,0:T(8,128)(2,1)S(1)}, u32[]{:S(2)}, u32[]{:S(2)}) collective-permute-start(bf16[4,128,128]{2,1,0:T(8,128)(2,1)S(1)} %get-tuple-element.85), channel_id=1, source_target_pairs={{0,8},{4,12},{8,0},{12,4},{16,24},{20,28},{24,16},{28,20},{1,9},{5... | collective-permute-start | bytes 393224 | tf_op jit(solution)/shard_map/ppermute | solution.py:449
  57.9 6.3 %collective-permute-start.16 = (bf16[4,128,128]{2,1,0:T(8,128)(2,1)S(1)}, bf16[4,128,128]{2,1,0:T(8,128)(2,1)S(1)}, u32[]{:S(2)}, u32[]{:S(2)}) collective-permute-start(bf16[4,128,128]{2,1,0:T(8,128)(2,1)S(1)} %get-tuple-element.84), channel_id=1, source_target_pairs={{0,16},{4,20},{8,24},{12,28},{16,0},{20,4},{24,8},{28,12},{1,17},{... | collective-permute-start | bytes 393224 | tf_op jit(solution)/shard_map/ppermute | solution.py:449
  58.7 7.2 %collective-permute-start.17 = (bf16[4,128,128]{2,1,0:T(8,128)(2,1)S(1)}, bf16[4,128,128]{2,1,0:T(8,128)(2,1)S(1)}, u32[]{:S(2)}, u32[]{:S(2)}) collective-permute-start(bf16[4,128,128]{2,1,0:T(8,128)(2,1)S(1)} %get-tuple-element.83), channel_id=1, source_target_pairs={{0,24},{4,28},{8,16},{12,20},{16,8},{20,12},{24,0},{28,4},{1,25},{... | collective-permute-start | bytes 393224 | tf_op jit(solution)/shard_map/ppermute | solution.py:449
